TPU v7x, 256 devices: a whole 4x4x8 slice. The times are simulated.
256 devices in a mesh: theta: 32 (over x_hi, z, core), xr: 8 (over x_lo, y).
Axes of the slice: x: 4 (x_hi: 2, x_lo: 2; x = x_hi * 2 + x_lo), y: 4, z: 8, core: 2. Of those that a mesh axis runs over, the one named last changes fastest.
Arguments:
- state: float32 [3, 2, 5, 256, 64, 128], P(None, None, None, 'theta', 'xr'), may hold values from -6 to 6
- source: float32 [3, 2, 5, 256, 64, 128], P(None, None, None, 'theta', 'xr'), may hold values from -6 to 6
- sigma: float32 [256, 64, 128], P('theta', 'xr'), may hold values from 0.25 to 4
- stagger: int32 [64], P('theta'), may hold values from 0 to 3
- a_theta: float32 [4, 5, 5], replicated, may hold values from -2.5 to 2.5
- a_axial: float32 [5, 5], replicated, may hold values from -2.5 to 2.5
- a_radial: float32 [5, 5], replicated, may hold values from -2.5 to 2.5
- mode_order: int32 [3, 128], replicated, may hold values from -32 to 32
- mode_radial: int32 [3, 128], replicated, may hold values from 0 to 7
- mode_plane: int32 [3, 128], replicated, may hold values from 0 to 1
- gust: float32 [3, 2, 128], replicated, may hold values from -6 to 6
- l_rows: float32 [2, 5], replicated, may hold values from -4 to 4
- r_cols: float32 [2, 5], replicated, may hold values from -4 to 4
Outputs:
- fields: float32 [3, 2, 5, 256, 64, 128], P(None, None, None, 'theta', 'xr')
- amplitudes: float32 [3, 2, 2, 128], replicated
Inputs may be any that keep to these rules, and one draw needn't show every extreme that they name: `mode_plane`: 0 names the inlet plane, 1 the exit plane.
All inputs are finite; a program needn't handle non-finite values.
Results may differ from a plain program's by a relative error of at most 0.0003.
Values sent between devices are 32-bit elements; how exact they have to be, the bound alone decides.
No kernel may reach another device: no remote copies, remote signals or barrier semaphores. Data moves between devices by JAX's collectives and lax.ppermute only.
A program may use at most 64 MiB of HBM per device.

v0:
```python
import math

import jax
import jax.numpy as jnp
from jax import lax
from jax.sharding import PartitionSpec as P

courant = 0.5
viscosity = 0.1
base_frequency = 0.5
highest = lax.Precision.HIGHEST


def extended(array, sides, width, wrap):
    for axis, dim in sides:
        devices, length = (lax.axis_size(axis), array.shape[dim])
        up = [(i, (i + 1) % devices) for i in range(devices if wrap else devices - 1)]
        down = [(j, i) for i, j in up]
        last = lax.slice_in_dim(array, length - width, length, axis=dim)
        initial = lax.slice_in_dim(array, 0, width, axis=dim)
        before = lax.ppermute(last, axis, up)
        after = lax.ppermute(initial, axis, down)
        array = jnp.concatenate([before, array, after], axis=dim)
    return array


def local_residual(
    field, theta_ext, axial_ext, freqs, forcing, damping, passage_matrix, a_axial, a_radial
):
    nharm, two, nvar, ctheta, caxial, nradial = field.shape
    npass = passage_matrix.shape[0]
    diff_theta = (theta_ext[:, :, :, 2:] - theta_ext[:, :, :, :-2]) * 0.5
    lap_theta = theta_ext[:, :, :, 2:] + theta_ext[:, :, :, :-2] - 2.0 * field
    diff_axial = (axial_ext[:, :, :, :, 2:] - axial_ext[:, :, :, :, :-2]) * 0.5
    lap_axial = axial_ext[:, :, :, :, 2:] + axial_ext[:, :, :, :, :-2] - 2.0 * field
    padded = jnp.pad(field, ((0, 0), (0, 0), (0, 0), (0, 0), (0, 0), (1, 1)))
    diff_radial = (padded[..., 2:] - padded[..., :-2]) * 0.5
    lap_radial = padded[..., 2:] + padded[..., :-2] - 2.0 * field
    turned = jnp.stack([-field[:, 1], field[:, 0]], axis=1)
    grouped = diff_theta.reshape(nharm, two, nvar, npass, ctheta // npass, caxial, nradial)
    flux = jnp.einsum("kvw,hpwkcxr->hpvkcxr", passage_matrix, grouped, precision=highest).reshape(
        field.shape
    )
    flux = flux + jnp.einsum("vw,hpwtxr->hpvtxr", a_axial, diff_axial, precision=highest)
    flux = flux + jnp.einsum("vw,hpwtxr->hpvtxr", a_radial, diff_radial, precision=highest)
    return (
        freqs[:, None, None, None, None, None] * turned
        + flux
        - viscosity * (lap_theta + lap_axial + lap_radial)
        + damping * field
        - forcing
    )


def local(
    state,
    source,
    sigma,
    stagger,
    a_theta,
    a_axial,
    a_radial,
    mode_order,
    mode_radial,
    mode_plane,
    gust,
    l_rows,
    r_cols,
):
    nharm, two, nvar, ctheta, caxial, nradial = state.shape
    total_theta = ctheta * lax.axis_size("theta")
    scale = 1.0 / math.sqrt(total_theta * nradial)
    freqs = base_frequency * (1.0 + jnp.arange(nharm).astype(jnp.float32))
    onehot = (stagger[:, None] == jnp.arange(a_theta.shape[0])[None, :]).astype(jnp.float32)
    passage_matrix = jnp.einsum("ks,svw->kvw", onehot, a_theta, precision=highest)
    step_size = courant / (1.0 + sigma)
    xr_index = lax.axis_index("xr")
    is_first = (xr_index == 0).astype(jnp.float32)
    is_last = (xr_index == lax.axis_size("xr") - 1).astype(jnp.float32)

    def rims(field):
        pieces_theta = []
        pieces_axial = []
        for harmonic in range(field.shape[0]):
            single = field[harmonic : harmonic + 1]
            pieces_theta.append(extended(single, (("theta", 3),), 1, True))
            pieces_axial.append(extended(single, (("xr", 4),), 1, False))
        theta_ext = jnp.concatenate(pieces_theta, axis=0)
        axial_ext = jnp.concatenate(pieces_axial, axis=0)
        return (theta_ext, axial_ext)

    def advance(field, theta_ext, axial_ext, factor):
        result = local_residual(
            field, theta_ext, axial_ext, freqs, source, sigma, passage_matrix, a_axial, a_radial
        )
        return state - factor * step_size * result

    theta_ext, axial_ext = rims(state)
    first = advance(state, theta_ext, axial_ext, 0.5)
    theta_ext, axial_ext = rims(first)
    second = advance(first, theta_ext, axial_ext, 1.0)
    inlet = is_first * jnp.einsum(
        "v,hpvtr->hptr", l_rows[0], second[:, :, :, :, 0], precision=highest
    )
    outlet = is_last * jnp.einsum(
        "v,hpvtr->hptr", l_rows[1], second[:, :, :, :, caxial - 1], precision=highest
    )
    plane_values = jnp.stack([inlet, outlet], axis=1)
    cells = lax.axis_index("theta") * ctheta + jnp.arange(ctheta)
    angle = (
        2.0
        * math.pi
        * jnp.mod(mode_order[:, :, None] * cells[None, None, :], total_theta).astype(jnp.float32)
        / total_theta
    )
    cos_table = jnp.cos(angle)
    sin_table = jnp.sin(angle)
    radial_pos = jnp.arange(nradial).astype(jnp.float32) + 0.5
    radial_table = jnp.where(
        mode_radial[:, :, None] == 0,
        1.0,
        math.sqrt(2.0)
        * jnp.cos(
            math.pi
            * mode_radial[:, :, None].astype(jnp.float32)
            * radial_pos[None, None, :]
            / nradial
        ),
    )
    projected = jnp.einsum("hbptr,hkr->hbptk", plane_values, radial_table, precision=highest)
    part_real = scale * (
        jnp.einsum("hbtk,hkt->hbk", projected[:, :, 0], cos_table, precision=highest)
        + jnp.einsum("hbtk,hkt->hbk", projected[:, :, 1], sin_table, precision=highest)
    )
    part_imag = scale * (
        jnp.einsum("hbtk,hkt->hbk", projected[:, :, 1], cos_table, precision=highest)
        - jnp.einsum("hbtk,hkt->hbk", projected[:, :, 0], sin_table, precision=highest)
    )
    amp_real, amp_imag = lax.psum((part_real, part_imag), ("theta", "xr"))
    weight = (mode_plane[:, None, :] == jnp.arange(2)[None, :, None]).astype(jnp.float32)
    miss_real = weight * (amp_real - gust[:, 0][:, None, :])
    miss_imag = weight * (amp_imag - gust[:, 1][:, None, :])
    coef_real = (
        miss_real[..., None] * cos_table[:, None] - miss_imag[..., None] * sin_table[:, None]
    )
    coef_imag = (
        miss_real[..., None] * sin_table[:, None] + miss_imag[..., None] * cos_table[:, None]
    )
    corr_real = jnp.einsum("hbkt,hkr->hbtr", coef_real, radial_table, precision=highest)
    corr_imag = jnp.einsum("hbkt,hkr->hbtr", coef_imag, radial_table, precision=highest)
    correction = scale * jnp.stack([corr_real, corr_imag], axis=2)
    measured = jnp.stack([weight * amp_real, weight * amp_imag], axis=2)
    corr_in, corr_out, measured = (
        is_first * correction[:, 0],
        is_last * correction[:, 1],
        measured,
    )
    second = second.at[:, :, :, :, 0, :].add(
        -r_cols[0][None, None, :, None, None] * corr_in[:, :, None]
    )
    second = second.at[:, :, :, :, caxial - 1, :].add(
        -r_cols[1][None, None, :, None, None] * corr_out[:, :, None]
    )
    return (second, measured)


def solution(mesh):
    placed = (
        P(None, None, None, "theta", "xr", None),
        P(None, None, None, "theta", "xr", None),
        P("theta", "xr", None),
        P("theta"),
        P(),
        P(),
        P(),
        P(),
        P(),
        P(),
        P(),
        P(),
        P(),
    )
    return jax.shard_map(
        local,
        mesh=mesh,
        in_specs=placed,
        out_specs=(P(None, None, None, "theta", "xr", None), P()),
        check_vma=False,
    )
```

profile of v0, /device:TPU:2, one launch (start us, length us, event | category | flops | bytes accessed | tf_op | source)
XLA Modules:
  0.0 196.7 jit_solution(7216474834089890822)
XLA Ops:
  0.6 1.8 copy.78
  2.5 0.7 fusion.131
  3.2 6.9 %collective-permute-start.1 = (f32[1,2,5,1,8,128]{5,2,4,3,1,0:T(8,128)}, f32[1,2,5,1,8,128]{5,2,4,3,1,0:T(8,128)S(1)}, u32[]{:S(2)}, u32[]{:S(2)}) collective-permute-start(f32[1,2,5,1,8,128]{5,2,4,3,1,0:T(8,128)} %get-tuple-element.66), channel_id=1, source_target_pairs={{8,0},{16,8},{24,16},{32,24},{40,32},{48,40},{56,48},{64,56},{72,6... | collective-permute-start | bytes 122888 | tf_op jit(solution)/shard_map/ppermute | solution.py:22
  10.1 5.4 %collective-permute-start.3 = (f32[1,2,5,1,8,128]{5,2,4,3,1,0:T(8,128)}, f32[1,2,5,1,8,128]{5,2,4,3,1,0:T(8,128)S(1)}, u32[]{:S(2)}, u32[]{:S(2)}) collective-permute-start(f32[1,2,5,1,8,128]{5,2,4,3,1,0:T(8,128)} %get-tuple-element.64), channel_id=1, source_target_pairs={{8,0},{16,8},{24,16},{32,24},{40,32},{48,40},{56,48},{64,56},{72,6... | collective-permute-start | bytes 122888 | tf_op jit(solution)/shard_map/ppermute | solution.py:22
  15.5 0.2 fusion.132
  15.6 0.8 fusion.130
  16.4 1.3 slice_negate_fusion.1
  17.7 0.6 convert_multiply_fusion
  18.3 0.5 broadcast_compare_fusion
  18.8 3.2 %fusion.24 = f32[3,2,8,8,128,5]{4,5,3,2,1,0:T(8,128)} fusion(f32[3,2,5,8,8,128]{5,2,4,3,1,0:T(8,128)S(1)} %copy.78, f32[5,5]{1,0:T(8,128)S(1)} %copy-done.12), kind=kOutput, calls=%fused_computation.41 | convolution fusion | flops 15237120 | bytes 1966180 | tf_op jit(solution)/shard_map/vw,hpwtxr->hpvtxr/dot_general | solution.py:45
  22.0 0.6 add_divide_fusion
  22.6 0.8 fusion.133
  23.4 1.3 negate_bitcast_fusion
  24.7 1.4 convolution_bitcast_fusion.2
  26.2 1.4 fusion.96
  27.6 0.6 copy_bitcast_fusion
  28.2 0.5 add_multiply_fusion
  28.7 5.4 %collective-permute-start.5 = (f32[1,2,5,1,8,128]{5,2,4,3,1,0:T(8,128)}, f32[1,2,5,1,8,128]{5,2,4,3,1,0:T(8,128)}, u32[]{:S(2)}, u32[]{:S(2)}) collective-permute-start(f32[1,2,5,1,8,128]{5,2,4,3,1,0:T(8,128)} %get-tuple-element.62), channel_id=1, source_target_pairs={{8,0},{16,8},{24,16},{32,24},{40,32},{48,40},{56,48},{64,56},{72,6... | collective-permute-start | bytes 122888 | tf_op jit(solution)/shard_map/ppermute | solution.py:22
  34.1 0.5 convert_add_fusion
  34.6 3.5 %collective-permute-start.10 = (f32[1,2,5,8,1,128]{5,2,4,3,1,0:T(8,128)}, f32[1,2,5,8,1,128]{5,2,4,3,1,0:T(8,128)S(1)}, u32[]{:S(2)}, u32[]{:S(2)}) collective-permute-start(f32[1,2,5,8,1,128]{5,2,4,3,1,0:T(8,128)} %get-tuple-element.57), channel_id=1, source_target_pairs={{0,1},{1,2},{2,3},{3,4},{4,5},{5,6},{6,7},{8,9},{9,10},{10,11},{11... | collective-permute-start | bytes 122888 | tf_op jit(solution)/shard_map/ppermute | solution.py:21
  38.1 4.5 %collective-permute-start.11 = (f32[1,2,5,8,1,128]{5,2,4,3,1,0:T(8,128)}, f32[1,2,5,8,1,128]{5,2,4,3,1,0:T(8,128)S(1)}, u32[]{:S(2)}, u32[]{:S(2)}) collective-permute-start(f32[1,2,5,8,1,128]{5,2,4,3,1,0:T(8,128)} %get-tuple-element.56), channel_id=1, source_target_pairs={{1,0},{2,1},{3,2},{4,3},{5,4},{6,5},{7,6},{9,8},{10,9},{11,10},{12... | collective-permute-start | bytes 122888 | tf_op jit(solution)/shard_map/ppermute | solution.py:22
  42.6 1.9 collective-permute-start.6
  44.5 6.0 %collective-permute-start.7 = (f32[1,2,5,8,1,128]{5,2,4,3,1,0:T(8,128)}, f32[1,2,5,8,1,128]{5,2,4,3,1,0:T(8,128)S(1)}, u32[]{:S(2)}, u32[]{:S(2)}) collective-permute-start(f32[1,2,5,8,1,128]{5,2,4,3,1,0:T(8,128)} %get-tuple-element.60), channel_id=1, source_target_pairs={{1,0},{2,1},{3,2},{4,3},{5,4},{6,5},{7,6},{9,8},{10,9},{11,10},{12... | collective-permute-start | bytes 122888 | tf_op jit(solution)/shard_map/ppermute | solution.py:22
  50.6 1.9 collective-permute-start.8
  52.5 1.1 maximum_maximum_fusion
  53.6 0.2 subtract_multiply_fusion.1
  53.8 0.6 copy-done.7
  54.4 6.2 %collective-permute-start.9 = (f32[1,2,5,8,1,128]{5,2,4,3,1,0:T(8,128)S(1)}, f32[1,2,5,8,1,128]{5,2,4,3,1,0:T(8,128)S(1)}, u32[]{:S(2)}, u32[]{:S(2)}) collective-permute-start(f32[1,2,5,8,1,128]{5,2,4,3,1,0:T(8,128)S(1)} %copy-done.7), channel_id=1, source_target_pairs={{1,0},{2,1},{3,2},{4,3},{5,4},{6,5},{7,6},{9,8},{10,9},{11,10},{12... | collective-permute-start | bytes 122888 | tf_op jit(solution)/shard_map/ppermute | solution.py:22
  60.6 1.5 fusion.34
  62.1 0.2 copy.61
  62.4 0.2 maximum_maximum_fusion.1
  62.6 0.6 copy-done.5
  63.2 0.4 copy-done.2
  63.6 0.5 copy-done.3
  64.1 0.2 copy-done.4
  64.3 4.0 %fusion.1 = f32[3,2,5,8,8,128]{5,2,4,3,1,0:T(8,128)S(1)} fusion(f32[3,2,5,8,8,128]{5,2,4,3,1,0:T(8,128)S(1)} %copy.78, f32[3,2,5,8,8,128]{5,4,3,2,1,0:T(8,128)S(1)} %copy-done.2, f32[3,1,5,8,8,128]{5,2,4,3,1,0:T(8,128)S(1)} %copy-done.5, f32[3,1,5,8,8,128]{5,2,4,3,1,0:T(8,128)S(1)} %copy-done.4, f32[3,2,8,8,128,5]{4,5,3,2,1,0:T(8,128)S(1)} %copy-done.3, ...), kind=kOutput, calls=%fused_computation.11 | convolution fusion | flops 20398080 | bytes 17175040 | tf_op jit(solution)/shard_map/vw,hpwtxr->hpvtxr/dot_general | solution.py:44
  68.5 0.2 slice_negate_fusion
  68.8 2.0 %fusion.14 = f32[3,2,8,8,128,5]{4,5,3,2,1,0:T(8,128)S(1)} fusion(f32[3,2,5,8,8,128]{5,2,4,3,1,0:T(8,128)S(1)} %fusion.1, f32[5,5]{1,0:T(8,128)S(1)} %copy-done.12), kind=kOutput, calls=%fused_computation.31 | convolution fusion | flops 15237120 | bytes 1966180 | tf_op jit(solution)/shard_map/vw,hpwtxr->hpvtxr/dot_general | solution.py:45
  70.8 5.4 %collective-permute-start.13 = (f32[1,2,5,1,8,128]{5,2,4,3,1,0:T(8,128)S(1)}, f32[1,2,5,1,8,128]{5,2,4,3,1,0:T(8,128)S(1)}, u32[]{:S(2)}, u32[]{:S(2)}) collective-permute-start(f32[1,2,5,1,8,128]{5,2,4,3,1,0:T(8,128)S(1)} %get-tuple-element.49), channel_id=1, source_target_pairs={{8,0},{16,8},{24,16},{32,24},{40,32},{48,40},{56,48},{64,56},{72,6... | collective-permute-start | bytes 122888 | tf_op jit(solution)/shard_map/ppermute | solution.py:22
  76.3 5.4 %collective-permute-start.15 = (f32[1,2,5,1,8,128]{5,2,4,3,1,0:T(8,128)S(1)}, f32[1,2,5,1,8,128]{5,2,4,3,1,0:T(8,128)S(1)}, u32[]{:S(2)}, u32[]{:S(2)}) collective-permute-start(f32[1,2,5,1,8,128]{5,2,4,3,1,0:T(8,128)S(1)} %get-tuple-element.47), channel_id=1, source_target_pairs={{8,0},{16,8},{24,16},{32,24},{40,32},{48,40},{56,48},{64,56},{72,6... | collective-permute-start | bytes 122888 | tf_op jit(solution)/shard_map/ppermute | solution.py:22
  81.6 5.4 %collective-permute-start.17 = (f32[1,2,5,1,8,128]{5,2,4,3,1,0:T(8,128)S(1)}, f32[1,2,5,1,8,128]{5,2,4,3,1,0:T(8,128)S(1)}, u32[]{:S(2)}, u32[]{:S(2)}) collective-permute-start(f32[1,2,5,1,8,128]{5,2,4,3,1,0:T(8,128)S(1)} %get-tuple-element.45), channel_id=1, source_target_pairs={{8,0},{16,8},{24,16},{32,24},{40,32},{48,40},{56,48},{64,56},{72,6... | collective-permute-start | bytes 122888 | tf_op jit(solution)/shard_map/ppermute | solution.py:22
  87.0 1.9 collective-permute-start.18
  89.0 6.0 %collective-permute-start.19 = (f32[1,2,5,8,1,128]{5,2,4,3,1,0:T(8,128)S(1)}, f32[1,2,5,8,1,128]{5,2,4,3,1,0:T(8,128)S(1)}, u32[]{:S(2)}, u32[]{:S(2)}) collective-permute-start(f32[1,2,5,8,1,128]{5,2,4,3,1,0:T(8,128)S(1)} %get-tuple-element.43), channel_id=1, source_target_pairs={{1,0},{2,1},{3,2},{4,3},{5,4},{6,5},{7,6},{9,8},{10,9},{11,10},{12... | collective-permute-start | bytes 122888 | tf_op jit(solution)/shard_map/ppermute | solution.py:22
  95.0 1.9 collective-permute-start.20
  97.0 6.0 %collective-permute-start.21 = (f32[1,2,5,8,1,128]{5,2,4,3,1,0:T(8,128)S(1)}, f32[1,2,5,8,1,128]{5,2,4,3,1,0:T(8,128)S(1)}, u32[]{:S(2)}, u32[]{:S(2)}) collective-permute-start(f32[1,2,5,8,1,128]{5,2,4,3,1,0:T(8,128)S(1)} %get-tuple-element.41), channel_id=1, source_target_pairs={{1,0},{2,1},{3,2},{4,3},{5,4},{6,5},{7,6},{9,8},{10,9},{11,10},{12... | collective-permute-start | bytes 122888 | tf_op jit(solution)/shard_map/ppermute | solution.py:22
  103.0 1.9 collective-permute-start.22
  104.9 0.2 maximum_maximum_fusion.2
  105.1 0.2 subtract_multiply_fusion
  105.4 6.0 %collective-permute-start.23 = (f32[1,2,5,8,1,128]{5,2,4,3,1,0:T(8,128)S(1)}, f32[1,2,5,8,1,128]{5,2,4,3,1,0:T(8,128)S(1)}, u32[]{:S(2)}, u32[]{:S(2)}) collective-permute-start(f32[1,2,5,8,1,128]{5,2,4,3,1,0:T(8,128)S(1)} %get-tuple-element.39), channel_id=1, source_target_pairs={{1,0},{2,1},{3,2},{4,3},{5,4},{6,5},{7,6},{9,8},{10,9},{11,10},{12... | collective-permute-start | bytes 122888 | tf_op jit(solution)/shard_map/ppermute | solution.py:22
  111.4 1.5 fusion.37
  113.0 0.3 collective-permute-done.23
  113.3 0.2 maximum_maximum_fusion.3
  113.5 0.7 copy-done.1
  114.2 4.1 %fusion.3 = f32[3,2,5,8,8,128]{5,2,4,3,1,0:T(8,128)S(1)} fusion(f32[3,2,5,8,8,128]{5,4,3,2,1,0:T(8,128)S(1)} %copy-done.2, f32[3,1,5,8,8,128]{5,2,4,3,1,0:T(8,128)S(1)} %get-tuple-element.54, f32[3,1,5,8,8,128]{5,2,4,3,1,0:T(8,128)S(1)} %get-tuple-element.53, f32[3,2,8,8,128,5]{4,5,3,2,1,0:T(8,128)S(1)} %fusion.14, ...), kind=kOutput, calls=%fused_computation.13 | convolution fusion | flops 20398080 | bytes 18747904 | tf_op jit(solution)/shard_map/vw,hpwtxr->hpvtxr/dot_general | solution.py:44
  118.4 0.3 fusion.50
  118.7 0.3 fusion.45
  119.0 1.1 fusion.46
  120.2 72.3 %all-reduce.2 = (f32[3,2,128]{2,1,0:T(2,128)S(1)}, f32[3,2,128]{2,1,0:T(2,128)S(1)}) all-reduce(f32[3,2,128]{2,1,0:T(2,128)S(1)} %multiply_bitcast_fusion.2, f32[3,2,128]{2,1,0:T(2,128)S(1)} %multiply_bitcast_fusion.3), channel_id=1, replica_groups=mesh['theta'=32,'xr'=8] {'theta','xr'}, use_global_device_ids=true, to_apply=%region_1.2 | all-reduce | flops 1536 | bytes 12288 | tf_op jit(solution)/shard_map/psum | solution.py:139
  192.6 1.0 convolution_bitcast_fusion.1
  193.6 1.0 convolution_bitcast_fusion
  194.7 0.1 add_dynamic-update-slice_fusion
  194.8 0.1 fusion.44
  195.0 1.1 copy.82
  196.1 0.6 pad_maximum_fusion
  (85 shorter events, 0.6 us)
Async XLA Ops:
  0.6 24.1 %copy-start = (f32[4,5,5]{2,0,1:T(4,128)S(1)}, f32[4,5,5]{2,0,1:T(4,128)}, u32[]{:S(2)}) copy-start(f32[4,5,5]{2,0,1:T(4,128)} %param.21) | copy-start | bytes 1204
  3.2 25.5 %collective-permute-start = (f32[1,2,5,1,8,128]{5,2,4,3,1,0:T(8,128)}, f32[1,2,5,1,8,128]{5,2,4,3,1,0:T(8,128)S(1)}, u32[]{:S(2)}, u32[]{:S(2)}) collective-permute-start(f32[1,2,5,1,8,128]{5,2,4,3,1,0:T(8,128)} %get-tuple-element.61), channel_id=1, source_target_pairs={{0,8},{8,16},{16,24},{24,32},{32,40},{40,48},{48,56},{56,64},{64,7... | collective-permute-start | bytes 122888 | tf_op jit(solution)/shard_map/ppermute | solution.py:21
  3.2 31.4 %collective-permute-start.1 = (f32[1,2,5,1,8,128]{5,2,4,3,1,0:T(8,128)}, f32[1,2,5,1,8,128]{5,2,4,3,1,0:T(8,128)S(1)}, u32[]{:S(2)}, u32[]{:S(2)}) collective-permute-start(f32[1,2,5,1,8,128]{5,2,4,3,1,0:T(8,128)} %get-tuple-element.66), channel_id=1, source_target_pairs={{8,0},{16,8},{24,16},{32,24},{40,32},{48,40},{56,48},{64,56},{72,6... | collective-permute-start | bytes 122888 | tf_op jit(solution)/shard_map/ppermute | solution.py:22
  10.1 28.0 %collective-permute-start.2 = (f32[1,2,5,1,8,128]{5,2,4,3,1,0:T(8,128)}, f32[1,2,5,1,8,128]{5,2,4,3,1,0:T(8,128)S(1)}, u32[]{:S(2)}, u32[]{:S(2)}) collective-permute-start(f32[1,2,5,1,8,128]{5,2,4,3,1,0:T(8,128)} %get-tuple-element.65), channel_id=1, source_target_pairs={{0,8},{8,16},{16,24},{24,32},{32,40},{40,48},{48,56},{56,64},{64,7... | collective-permute-start | bytes 122888 | tf_op jit(solution)/shard_map/ppermute | solution.py:21
  10.1 32.5 %collective-permute-start.3 = (f32[1,2,5,1,8,128]{5,2,4,3,1,0:T(8,128)}, f32[1,2,5,1,8,128]{5,2,4,3,1,0:T(8,128)S(1)}, u32[]{:S(2)}, u32[]{:S(2)}) collective-permute-start(f32[1,2,5,1,8,128]{5,2,4,3,1,0:T(8,128)} %get-tuple-element.64), channel_id=1, source_target_pairs={{8,0},{16,8},{24,16},{32,24},{40,32},{48,40},{56,48},{64,56},{72,6... | collective-permute-start | bytes 122888 | tf_op jit(solution)/shard_map/ppermute | solution.py:22
  15.5 29.1 %collective-permute-start.4 = (f32[1,2,5,1,8,128]{5,2,4,3,1,0:T(8,128)}, f32[1,2,5,1,8,128]{5,2,4,3,1,0:T(8,128)S(1)}, u32[]{:S(2)}, u32[]{:S(2)}) collective-permute-start(f32[1,2,5,1,8,128]{5,2,4,3,1,0:T(8,128)} %get-tuple-element.63), channel_id=1, source_target_pairs={{0,8},{8,16},{16,24},{24,32},{32,40},{40,48},{48,56},{56,64},{64,7... | collective-permute-start | bytes 122888 | tf_op jit(solution)/shard_map/ppermute | solution.py:21
  16.4 1.3 copy-start.15
  16.4 2.4 %copy-start.12 = (f32[5,5]{1,0:T(8,128)S(1)}, f32[5,5]{1,0:T(8,128)}, u32[]{:S(2)}) copy-start(f32[5,5]{1,0:T(8,128)} %param.23) | copy-start | bytes 304
  18.8 3.2 %copy-start.6 = (f32[8,8,128]{2,1,0:T(8,128)S(1)}, f32[8,8,128]{2,1,0:T(8,128)}, u32[]{:S(2)}) copy-start(f32[8,8,128]{2,1,0:T(8,128)} %param.19) | copy-start | bytes 98308
  28.7 21.8 %collective-permute-start.5 = (f32[1,2,5,1,8,128]{5,2,4,3,1,0:T(8,128)}, f32[1,2,5,1,8,128]{5,2,4,3,1,0:T(8,128)}, u32[]{:S(2)}, u32[]{:S(2)}) collective-permute-start(f32[1,2,5,1,8,128]{5,2,4,3,1,0:T(8,128)} %get-tuple-element.62), channel_id=1, source_target_pairs={{8,0},{16,8},{24,16},{32,24},{40,32},{48,40},{56,48},{64,56},{72,6... | collective-permute-start | bytes 122888 | tf_op jit(solution)/shard_map/ppermute | solution.py:22
  34.6 19.2 %collective-permute-start.10 = (f32[1,2,5,8,1,128]{5,2,4,3,1,0:T(8,128)}, f32[1,2,5,8,1,128]{5,2,4,3,1,0:T(8,128)S(1)}, u32[]{:S(2)}, u32[]{:S(2)}) collective-permute-start(f32[1,2,5,8,1,128]{5,2,4,3,1,0:T(8,128)} %get-tuple-element.57), channel_id=1, source_target_pairs={{0,1},{1,2},{2,3},{3,4},{4,5},{5,6},{6,7},{8,9},{9,10},{10,11},{11... | collective-permute-start | bytes 122888 | tf_op jit(solution)/shard_map/ppermute | solution.py:21
  38.1 24.2 %collective-permute-start.11 = (f32[1,2,5,8,1,128]{5,2,4,3,1,0:T(8,128)}, f32[1,2,5,8,1,128]{5,2,4,3,1,0:T(8,128)S(1)}, u32[]{:S(2)}, u32[]{:S(2)}) collective-permute-start(f32[1,2,5,8,1,128]{5,2,4,3,1,0:T(8,128)} %get-tuple-element.56), channel_id=1, source_target_pairs={{1,0},{2,1},{3,2},{4,3},{5,4},{6,5},{7,6},{9,8},{10,9},{11,10},{12... | collective-permute-start | bytes 122888 | tf_op jit(solution)/shard_map/ppermute | solution.py:22
  42.6 19.8 %collective-permute-start.6 = (f32[1,2,5,8,1,128]{5,2,4,3,1,0:T(8,128)}, f32[1,2,5,8,1,128]{5,2,4,3,1,0:T(8,128)S(1)}, u32[]{:S(2)}, u32[]{:S(2)}) collective-permute-start(f32[1,2,5,8,1,128]{5,2,4,3,1,0:T(8,128)} %get-tuple-element.55), channel_id=1, source_target_pairs={{0,1},{1,2},{2,3},{3,4},{4,5},{5,6},{6,7},{8,9},{9,10},{10,11},{11... | collective-permute-start | bytes 122888 | tf_op jit(solution)/shard_map/ppermute | solution.py:21
  44.5 17.8 %collective-permute-start.7 = (f32[1,2,5,8,1,128]{5,2,4,3,1,0:T(8,128)}, f32[1,2,5,8,1,128]{5,2,4,3,1,0:T(8,128)S(1)}, u32[]{:S(2)}, u32[]{:S(2)}) collective-permute-start(f32[1,2,5,8,1,128]{5,2,4,3,1,0:T(8,128)} %get-tuple-element.60), channel_id=1, source_target_pairs={{1,0},{2,1},{3,2},{4,3},{5,4},{6,5},{7,6},{9,8},{10,9},{11,10},{12... | collective-permute-start | bytes 122888 | tf_op jit(solution)/shard_map/ppermute | solution.py:22
  50.6 11.8 %collective-permute-start.8 = (f32[1,2,5,8,1,128]{5,2,4,3,1,0:T(8,128)}, f32[1,2,5,8,1,128]{5,2,4,3,1,0:T(8,128)S(1)}, u32[]{:S(2)}, u32[]{:S(2)}) collective-permute-start(f32[1,2,5,8,1,128]{5,2,4,3,1,0:T(8,128)} %get-tuple-element.59), channel_id=1, source_target_pairs={{0,1},{1,2},{2,3},{3,4},{4,5},{5,6},{6,7},{8,9},{9,10},{10,11},{11... | collective-permute-start | bytes 122888 | tf_op jit(solution)/shard_map/ppermute | solution.py:21
  53.6 0.8 copy-start.7
  53.6 7.0 %copy-start.8 = (f32[2,5,5,1,1,1,1]{2,0,1,6,5,4,3:T(2,128)S(1)}, f32[2,5,5,1,1,1,1]{2,0,1,6,5,4,3:T(2,128)}, u32[]{:S(2)}) copy-start(f32[2,5,5,1,1,1,1]{2,0,1,6,5,4,3:T(2,128)} %convolution_bitcast_fusion.2) | copy-start | bytes 604
  54.4 8.0 %collective-permute-start.9 = (f32[1,2,5,8,1,128]{5,2,4,3,1,0:T(8,128)S(1)}, f32[1,2,5,8,1,128]{5,2,4,3,1,0:T(8,128)S(1)}, u32[]{:S(2)}, u32[]{:S(2)}) collective-permute-start(f32[1,2,5,8,1,128]{5,2,4,3,1,0:T(8,128)S(1)} %copy-done.7), channel_id=1, source_target_pairs={{1,0},{2,1},{3,2},{4,3},{5,4},{6,5},{7,6},{9,8},{10,9},{11,10},{12... | collective-permute-start | bytes 122888 | tf_op jit(solution)/shard_map/ppermute | solution.py:22
  62.1 1.1 copy-start.5
  62.3 1.3 copy-start.2
  62.3 1.8 copy-start.3
  62.3 2.0 %copy-start.4 = (f32[3,1,5,8,8,128]{5,2,4,3,1,0:T(8,128)S(1)}, f32[3,1,5,8,8,128]{5,2,4,3,1,0:T(8,128)}, u32[]{:S(2)}) copy-start(f32[3,1,5,8,8,128]{5,2,4,3,1,0:T(8,128)} %get-tuple-element.70) | copy-start | bytes 1474564
  62.3 2.0 %copy-start.11 = (f32[8,8,128]{2,1,0:T(8,128)S(1)}, f32[8,8,128]{2,1,0:T(8,128)}, u32[]{:S(2)}) copy-start(f32[8,8,128]{2,1,0:T(8,128)} %get-tuple-element.75) | copy-start | bytes 98308
  62.3 2.0 copy-start.16
  62.3 2.0 copy-start.17
  68.7 12.9 %collective-permute-start.12 = (f32[1,2,5,1,8,128]{5,2,4,3,1,0:T(8,128)S(1)}, f32[1,2,5,1,8,128]{5,2,4,3,1,0:T(8,128)S(1)}, u32[]{:S(2)}, u32[]{:S(2)}) collective-permute-start(f32[1,2,5,1,8,128]{5,2,4,3,1,0:T(8,128)S(1)} %get-tuple-element.44), channel_id=1, source_target_pairs={{0,8},{8,16},{16,24},{24,32},{32,40},{40,48},{48,56},{56,64},{64,7... | collective-permute-start | bytes 122888 | tf_op jit(solution)/shard_map/ppermute | solution.py:21
  70.8 16.2 %collective-permute-start.13 = (f32[1,2,5,1,8,128]{5,2,4,3,1,0:T(8,128)S(1)}, f32[1,2,5,1,8,128]{5,2,4,3,1,0:T(8,128)S(1)}, u32[]{:S(2)}, u32[]{:S(2)}) collective-permute-start(f32[1,2,5,1,8,128]{5,2,4,3,1,0:T(8,128)S(1)} %get-tuple-element.49), channel_id=1, source_target_pairs={{8,0},{16,8},{24,16},{32,24},{40,32},{48,40},{56,48},{64,56},{72,6... | collective-permute-start | bytes 122888 | tf_op jit(solution)/shard_map/ppermute | solution.py:22
  76.3 12.7 %collective-permute-start.14 = (f32[1,2,5,1,8,128]{5,2,4,3,1,0:T(8,128)S(1)}, f32[1,2,5,1,8,128]{5,2,4,3,1,0:T(8,128)S(1)}, u32[]{:S(2)}, u32[]{:S(2)}) collective-permute-start(f32[1,2,5,1,8,128]{5,2,4,3,1,0:T(8,128)S(1)} %get-tuple-element.48), channel_id=1, source_target_pairs={{0,8},{8,16},{16,24},{24,32},{32,40},{40,48},{48,56},{56,64},{64,7... | collective-permute-start | bytes 122888 | tf_op jit(solution)/shard_map/ppermute | solution.py:21
  76.3 18.8 %collective-permute-start.15 = (f32[1,2,5,1,8,128]{5,2,4,3,1,0:T(8,128)S(1)}, f32[1,2,5,1,8,128]{5,2,4,3,1,0:T(8,128)S(1)}, u32[]{:S(2)}, u32[]{:S(2)}) collective-permute-start(f32[1,2,5,1,8,128]{5,2,4,3,1,0:T(8,128)S(1)} %get-tuple-element.47), channel_id=1, source_target_pairs={{8,0},{16,8},{24,16},{32,24},{40,32},{48,40},{56,48},{64,56},{72,6... | collective-permute-start | bytes 122888 | tf_op jit(solution)/shard_map/ppermute | solution.py:22
  81.6 15.3 %collective-permute-start.16 = (f32[1,2,5,1,8,128]{5,2,4,3,1,0:T(8,128)S(1)}, f32[1,2,5,1,8,128]{5,2,4,3,1,0:T(8,128)S(1)}, u32[]{:S(2)}, u32[]{:S(2)}) collective-permute-start(f32[1,2,5,1,8,128]{5,2,4,3,1,0:T(8,128)S(1)} %get-tuple-element.46), channel_id=1, source_target_pairs={{0,8},{8,16},{16,24},{24,32},{32,40},{40,48},{48,56},{56,64},{64,7... | collective-permute-start | bytes 122888 | tf_op jit(solution)/shard_map/ppermute | solution.py:21
  81.6 21.4 %collective-permute-start.17 = (f32[1,2,5,1,8,128]{5,2,4,3,1,0:T(8,128)S(1)}, f32[1,2,5,1,8,128]{5,2,4,3,1,0:T(8,128)S(1)}, u32[]{:S(2)}, u32[]{:S(2)}) collective-permute-start(f32[1,2,5,1,8,128]{5,2,4,3,1,0:T(8,128)S(1)} %get-tuple-element.45), channel_id=1, source_target_pairs={{8,0},{16,8},{24,16},{32,24},{40,32},{48,40},{56,48},{64,56},{72,6... | collective-permute-start | bytes 122888 | tf_op jit(solution)/shard_map/ppermute | solution.py:22
  87.0 18.3 %collective-permute-start.18 = (f32[1,2,5,8,1,128]{5,2,4,3,1,0:T(8,128)S(1)}, f32[1,2,5,8,1,128]{5,2,4,3,1,0:T(8,128)S(1)}, u32[]{:S(2)}, u32[]{:S(2)}) collective-permute-start(f32[1,2,5,8,1,128]{5,2,4,3,1,0:T(8,128)S(1)} %get-tuple-element.38), channel_id=1, source_target_pairs={{0,1},{1,2},{2,3},{3,4},{4,5},{5,6},{6,7},{8,9},{9,10},{10,11},{11... | collective-permute-start | bytes 122888 | tf_op jit(solution)/shard_map/ppermute | solution.py:21
  89.0 24.0 %collective-permute-start.19 = (f32[1,2,5,8,1,128]{5,2,4,3,1,0:T(8,128)S(1)}, f32[1,2,5,8,1,128]{5,2,4,3,1,0:T(8,128)S(1)}, u32[]{:S(2)}, u32[]{:S(2)}) collective-permute-start(f32[1,2,5,8,1,128]{5,2,4,3,1,0:T(8,128)S(1)} %get-tuple-element.43), channel_id=1, source_target_pairs={{1,0},{2,1},{3,2},{4,3},{5,4},{6,5},{7,6},{9,8},{10,9},{11,10},{12... | collective-permute-start | bytes 122888 | tf_op jit(solution)/shard_map/ppermute | solution.py:22
  95.0 18.0 %collective-permute-start.20 = (f32[1,2,5,8,1,128]{5,2,4,3,1,0:T(8,128)S(1)}, f32[1,2,5,8,1,128]{5,2,4,3,1,0:T(8,128)S(1)}, u32[]{:S(2)}, u32[]{:S(2)}) collective-permute-start(f32[1,2,5,8,1,128]{5,2,4,3,1,0:T(8,128)S(1)} %get-tuple-element.42), channel_id=1, source_target_pairs={{0,1},{1,2},{2,3},{3,4},{4,5},{5,6},{6,7},{8,9},{9,10},{10,11},{11... | collective-permute-start | bytes 122888 | tf_op jit(solution)/shard_map/ppermute | solution.py:21
  97.0 16.1 %collective-permute-start.21 = (f32[1,2,5,8,1,128]{5,2,4,3,1,0:T(8,128)S(1)}, f32[1,2,5,8,1,128]{5,2,4,3,1,0:T(8,128)S(1)}, u32[]{:S(2)}, u32[]{:S(2)}) collective-permute-start(f32[1,2,5,8,1,128]{5,2,4,3,1,0:T(8,128)S(1)} %get-tuple-element.41), channel_id=1, source_target_pairs={{1,0},{2,1},{3,2},{4,3},{5,4},{6,5},{7,6},{9,8},{10,9},{11,10},{12... | collective-permute-start | bytes 122888 | tf_op jit(solution)/shard_map/ppermute | solution.py:22
  103.0 10.0 %collective-permute-start.22 = (f32[1,2,5,8,1,128]{5,2,4,3,1,0:T(8,128)S(1)}, f32[1,2,5,8,1,128]{5,2,4,3,1,0:T(8,128)S(1)}, u32[]{:S(2)}, u32[]{:S(2)}) collective-permute-start(f32[1,2,5,8,1,128]{5,2,4,3,1,0:T(8,128)S(1)} %get-tuple-element.40), channel_id=1, source_target_pairs={{0,1},{1,2},{2,3},{3,4},{4,5},{5,6},{6,7},{8,9},{9,10},{10,11},{11... | collective-permute-start | bytes 122888 | tf_op jit(solution)/shard_map/ppermute | solution.py:21
  105.4 7.9 %collective-permute-start.23 = (f32[1,2,5,8,1,128]{5,2,4,3,1,0:T(8,128)S(1)}, f32[1,2,5,8,1,128]{5,2,4,3,1,0:T(8,128)S(1)}, u32[]{:S(2)}, u32[]{:S(2)}) collective-permute-start(f32[1,2,5,8,1,128]{5,2,4,3,1,0:T(8,128)S(1)} %get-tuple-element.39), channel_id=1, source_target_pairs={{1,0},{2,1},{3,2},{4,3},{5,4},{6,5},{7,6},{9,8},{10,9},{11,10},{12... | collective-permute-start | bytes 122888 | tf_op jit(solution)/shard_map/ppermute | solution.py:22
  113.0 1.2 copy-start.1
  114.2 4.2 %copy-start.18 = (f32[2,5]{1,0:T(2,128)S(1)}, f32[2,5]{1,0:T(2,128)}, u32[]{:S(2)}) copy-start(f32[2,5]{1,0:T(2,128)} %param.28) | copy-start | bytes 124
  114.2 4.8 %copy-start.22 = (f32[3,128]{1,0:T(4,128)S(1)}, f32[3,128]{1,0:T(4,128)}, u32[]{:S(2)}) copy-start(f32[3,128]{1,0:T(4,128)} %convert_multiply_fusion) | copy-start | bytes 4612
  114.2 4.8 %copy-start.23 = (pred[3,128]{1,0:T(4,128)(4,1)S(1)}, pred[3,128]{1,0:T(4,128)(4,1)}, u32[]{:S(2)}) copy-start(pred[3,128]{1,0:T(4,128)(4,1)} %broadcast_compare_fusion) | copy-start | bytes 1156
  114.2 4.8 %copy-start.24 = (f32[128]{0:T(128)S(1)}, f32[128]{0:T(128)}, u32[]{:S(2)}) copy-start(f32[128]{0:T(128)} %convert_add_fusion) | copy-start | bytes 1540
  114.2 6.0 %copy-start.9 = (f32[3,128,8]{1,2,0:T(8,128)S(1)}, f32[3,128,8]{1,2,0:T(8,128)}, u32[]{:S(2)}) copy-start(f32[3,128,8]{1,2,0:T(8,128)} %get-tuple-element.82) | copy-start | bytes 36868
  114.2 6.0 %copy-start.10 = (f32[3,128,8]{1,2,0:T(8,128)S(1)}, f32[3,128,8]{1,2,0:T(8,128)}, u32[]{:S(2)}) copy-start(f32[3,128,8]{1,2,0:T(8,128)} %get-tuple-element.83) | copy-start | bytes 36868
  114.2 78.4 %copy-start.13 = (f32[3,128]{1,0:T(4,128)S(1)}, f32[3,128]{1,0:T(4,128)}, u32[]{:S(2)}) copy-start(f32[3,128]{1,0:T(4,128)} %get-tuple-element.90) | copy-start | bytes 4612
  114.2 78.4 %copy-start.14 = (f32[3,128]{1,0:T(4,128)S(1)}, f32[3,128]{1,0:T(4,128)}, u32[]{:S(2)}) copy-start(f32[3,128]{1,0:T(4,128)} %get-tuple-element.91) | copy-start | bytes 4612
  114.2 78.4 %copy-start.21 = (s32[3,128]{1,0:T(4,128)S(1)}, s32[3,128]{1,0:T(4,128)}, u32[]{:S(2)}) copy-start(s32[3,128]{1,0:T(4,128)} %param.26) | copy-start | bytes 4612
  118.3 76.4 %copy-start.20 = (f32[5]{0:T(128)S(1)}, f32[5]{0:T(128)}, u32[]{:S(2)}) copy-start(f32[5]{0:T(128)} %get-tuple-element.87) | copy-start | bytes 64
  118.4 76.5 %copy-start.19 = (f32[5]{0:T(128)S(1)}, f32[5]{0:T(128)}, u32[]{:S(2)}) copy-start(f32[5]{0:T(128)} %get-tuple-element.86) | copy-start | bytes 64
where the time goes:
time: 201 us; the launch traced here: 197 us
  starting transfers between devices  81.7 us (41%)
  blocking collectives  72.3 us (36%)
  matrix products  21.5 us (11%)
  other arithmetic  10 us (5%)
  local copies, waits for them, and re-layouts  9.46 us (5%)
    psum x1, blocking collectives, local(): amp_real, amp_imag = lax.psum((part_real, part_imag), ('theta', 'xr'))  72.3 us
    ppermute x12, starting transfers between devices, extended(): after = lax.ppermute(initial, axis, down)  68.5 us
    ppermute x12, starting transfers between devices, extended(): before = lax.ppermute(last, axis, up)  13.2 us
    dot_general x2, matrix products, local_residual(): jnp.einsum('vw,hpwtxr->hpvtxr', a_axial, diff_axial, precision=highest)  8.11 us
    unnamed x53, local copies, waits for them, and re-layouts  6.58 us
    dot_general x2, matrix products, local_residual(): jnp.einsum('vw,hpwtxr->hpvtxr', a_radial, diff_radial, precision=highest)  5.24 us
  transfers between devices with their start and end apart: 24, of which 1 were waited for; matrix products, arithmetic and copies ran while one was open for 11% of the time, Pallas kernels for 0%

commit v1 on v0

v1 whole, which is shorter than its diff:
```python
import functools
import math

import jax
import jax.numpy as jnp
from jax import lax
from jax.experimental import pallas as pl
from jax.experimental.pallas import tpu as pltpu
from jax.sharding import PartitionSpec as P

courant = 0.5
viscosity = 0.1
base_frequency = 0.5
highest = lax.Precision.HIGHEST
VM = pltpu.VMEM
SM = pltpu.SMEM


def spec(space):
    return pl.BlockSpec(memory_space=space)


def params():
    return pltpu.CompilerParams(vmem_limit_bytes=40 * 1024 * 1024)


def write_faces(place, u_ref, te_ref, to_ref, xe_ref, xo_ref):
    nhp, nvar = u_ref.shape[0], u_ref.shape[1]
    todd = lax.rem(place[0], 2)
    xodd = lax.rem(place[1], 2)
    for out_ref, layer in ((te_ref, 1 - todd), (to_ref, todd)):
        start = pl.multiple_of(layer * 56, 8)
        out_ref[...] = u_ref[:, :, pl.ds(start, 8), :]
    for out_ref, row in ((xe_ref, 1 - xodd), (xo_ref, xodd)):
        for i in range(nhp):
            for v in range(nvar):
                out_ref[i, v] = u_ref[i, v, pl.ds(row * 7, 8, stride=8), :]


def pack_kernel(place, u_ref, te_ref, to_ref, xe_ref, xo_ref):
    write_faces(place, u_ref, te_ref, to_ref, xe_ref, xo_ref)


def step(factor, place, stagger, a_theta, a_axial, a_radial, u_ref, base_ref, src_ref, sig_ref, te, to, xe, xo, out_ref):
    nhp, nvar, rows, nr = u_ref.shape
    tcells = rows // 8
    cpp = tcells // stagger.shape[0]
    todd = lax.rem(place[0], 2) == 1
    xodd = lax.rem(place[1], 2) == 1
    shape = (nhp, 8, nr)
    row = lax.broadcasted_iota(jnp.int32, shape, 1)
    lane = lax.broadcasted_iota(jnp.int32, shape, 2)
    axial = [[0.5 * a_axial[v, w] for w in range(nvar)] for v in range(nvar)]
    radial = [[0.5 * a_radial[v, w] for w in range(nvar)] for v in range(nvar)]
    for t in range(tcells):
        setting = stagger[t // cpp]
        tile = slice(8 * t, 8 * t + 8)
        sig = sig_ref[tile, :][None]
        own = sig + 6.0 * viscosity
        scaled = (factor * courant) / (1.0 + sig)
        acc = [None] * nvar
        for w in range(nvar):
            u = u_ref[:, w, tile, :]
            if t == 0:
                tm = jnp.where(todd, te[:, w], to[:, w])
            else:
                tm = u_ref[:, w, 8 * t - 8 : 8 * t, :]
            if t == tcells - 1:
                tp = jnp.where(todd, to[:, w], te[:, w])
            else:
                tp = u_ref[:, w, 8 * t + 8 : 8 * t + 16, :]
            e = xe[:, w, t : t + 1, :]
            o = xo[:, w, t : t + 1, :]
            xlo = jnp.where(xodd, e, o)
            xhi = jnp.where(xodd, o, e)
            xm = jnp.where(row == 0, jnp.broadcast_to(xlo, shape), pltpu.roll(u, 1, 1))
            xp = jnp.where(row == 7, jnp.broadcast_to(xhi, shape), pltpu.roll(u, 7, 1))
            rm = jnp.where(lane == 0, 0.0, pltpu.roll(u, 1, 2))
            rp = jnp.where(lane == nr - 1, 0.0, pltpu.roll(u, nr - 1, 2))
            dt_, dx_, dr_ = tp - tm, xp - xm, rp - rm
            near = ((tp + tm) + (xp + xm)) + (rp + rm)
            turned = []
            for h in range(nhp // 2):
                freq = base_frequency * (1.0 + h)
                turned.append(-freq * u[2 * h + 1 : 2 * h + 2])
                turned.append(freq * u[2 * h : 2 * h + 1])
            local_part = (own * u - viscosity * near) + (jnp.concatenate(turned, axis=0) - src_ref[:, w, tile, :])
            for v in range(nvar):
                flux = (0.5 * a_theta[setting, v, w]) * dt_ + axial[v][w] * dx_ + radial[v][w] * dr_
                if v == w:
                    flux = flux + local_part
                acc[v] = flux if acc[v] is None else acc[v] + flux
        for v in range(nvar):
            out_ref[:, v, tile, :] = base_ref[:, v, tile, :] - scaled * acc[v]


def first_kernel(
    place, stagger, a_theta, a_axial, a_radial, u_ref, src_ref, sig_ref, te, to, xe, xo, out_ref, te2, to2, xe2, xo2
):
    step(0.5, place, stagger, a_theta, a_axial, a_radial, u_ref, u_ref, src_ref, sig_ref, te, to, xe, xo, out_ref)
    write_faces(place, out_ref, te2, to2, xe2, xo2)


def tables(place, order, tcells, tdevices):
    nharm, nmode = order.shape
    total = tcells * tdevices
    cell = place[0] * tcells + lax.broadcasted_iota(jnp.int32, (tcells, nmode), 0)
    cos, sin = [], []
    for h in range(nharm):
        turns = lax.rem(order[h : h + 1, :] * cell + 64 * total, total)
        angle = 2.0 * math.pi * turns.astype(jnp.float32) / total
        cos.append(jnp.cos(angle))
        sin.append(jnp.sin(angle))
    return cos, sin


def radial_table(nrad, nr):
    n = lax.broadcasted_iota(jnp.int32, (nrad, nr), 0)
    pos = lax.broadcasted_iota(jnp.int32, (nrad, nr), 1).astype(jnp.float32) + 0.5
    wave = math.sqrt(2.0) * jnp.cos(math.pi * n.astype(jnp.float32) * pos / nr)
    return jnp.where(n == 0, 1.0, wave)


def second_kernel(
    tdevices,
    xdevices,
    nrad,
    place,
    stagger,
    a_theta,
    a_axial,
    a_radial,
    l_rows,
    u_ref,
    base_ref,
    src_ref,
    sig_ref,
    te,
    to,
    xe,
    xo,
    order,
    radial,
    plane,
    out_ref,
    part_ref,
):
    step(1.0, place, stagger, a_theta, a_axial, a_radial, u_ref, base_ref, src_ref, sig_ref, te, to, xe, xo, out_ref)
    nhp, nvar, rows, nr = out_ref.shape
    nharm, nmode = order.shape
    tcells = rows // 8
    scale = 1.0 / math.sqrt(tcells * tdevices * nr)
    last = (place[1] == xdevices - 1).astype(jnp.int32)
    holds = jnp.logical_or(place[1] == 0, place[1] == xdevices - 1)
    values = []
    for i in range(nhp):
        c = None
        for v in range(nvar):
            term = l_rows[last, v] * out_ref[i, v, pl.ds(last * 7, tcells, stride=8), :]
            c = term if c is None else c + term
        values.append(c)
    values = jnp.concatenate(values, axis=0)
    waves = radial_table(nrad, nr)
    nt = (((1,), (1,)), ((), ()))
    grouped = lax.dot_general(values, waves, nt, precision=highest, preferred_element_type=jnp.float32)
    cos, sin = tables(place, order, tcells, tdevices)
    out = []
    for h in range(nharm):
        pick = (lax.broadcasted_iota(jnp.int32, (nrad, nmode), 0) == radial[h : h + 1, :]).astype(jnp.float32)
        mine = jnp.logical_and(plane[h : h + 1, :] == last, holds)
        both = jnp.dot(
            grouped[2 * tcells * h : 2 * tcells * (h + 1)], pick, precision=highest, preferred_element_type=jnp.float32
        )
        re, im = both[:tcells], both[tcells:]
        part_re = scale * jnp.sum(re * cos[h] + im * sin[h], axis=0, keepdims=True)
        part_im = scale * jnp.sum(im * cos[h] - re * sin[h], axis=0, keepdims=True)
        out.append(jnp.where(mine, part_re, 0.0))
        out.append(jnp.where(mine, part_im, 0.0))
    out.append(jnp.zeros((8 - nhp, nmode), jnp.float32))
    block = jnp.concatenate(out, axis=0)
    for d in range(tdevices):
        part_ref[d] = block


def correct_kernel(
    tdevices, xdevices, nrad, place, r_cols, got_ref, gust, second_ref, order, radial, plane, out_ref, amp_ref
):
    nhp, nvar, rows, nr = out_ref.shape
    nharm, nmode = order.shape
    tcells = rows // 8
    scale = 1.0 / math.sqrt(tcells * tdevices * nr)
    last = (place[1] == xdevices - 1).astype(jnp.int32)
    holds = jnp.logical_or(place[1] == 0, place[1] == xdevices - 1)
    amp = jnp.sum(got_ref[...], axis=0)
    for d in range(xdevices):
        amp_ref[d] = amp
    out_ref[...] = second_ref[...]

    @pl.when(holds)
    def _():
        waves = radial_table(nrad, nr)
        cos, sin = tables(place, order, tcells, tdevices)
        for h in range(nharm):
            pick = (lax.broadcasted_iota(jnp.int32, (nrad, nmode), 0) == radial[h : h + 1, :]).astype(jnp.float32)
            mine = plane[h : h + 1, :] == last
            miss_re = jnp.where(mine, amp[2 * h : 2 * h + 1] - gust[h, 0:1, :], 0.0)
            miss_im = jnp.where(mine, amp[2 * h + 1 : 2 * h + 2] - gust[h, 1:2, :], 0.0)
            coef = jnp.concatenate([miss_re * cos[h] - miss_im * sin[h], miss_re * sin[h] + miss_im * cos[h]], axis=0)
            nt = (((1,), (1,)), ((), ()))
            grouped = lax.dot_general(coef, pick, nt, precision=highest, preferred_element_type=jnp.float32)
            q = scale * jnp.dot(grouped, waves, precision=highest, preferred_element_type=jnp.float32)
            for p in range(2):
                for v in range(nvar):
                    at = pl.ds(last * 7, tcells, stride=8)
                    out_ref[2 * h + p, v, at, :] = (
                        second_ref[2 * h + p, v, at, :] - r_cols[last, v] * q[p * tcells : (p + 1) * tcells]
                    )


def local(
    state, source, sigma, stagger, a_theta, a_axial, a_radial, mode_order, mode_radial, mode_plane, gust, l_rows, r_cols
):
    nharm, two, nvar, ctheta, caxial, nradial = state.shape
    nhp = nharm * two
    tdev, xdev = lax.axis_size("theta"), lax.axis_size("xr")
    nrad = 8
    block = (nhp, nvar, ctheta * caxial, nradial)
    u = state.reshape(block)
    src = source.reshape(block)
    sig = sigma.reshape(ctheta * caxial, nradial)
    place = jnp.stack([lax.axis_index("theta"), lax.axis_index("xr")]).astype(jnp.int32)
    f32 = jnp.float32
    face = jax.ShapeDtypeStruct((nhp, nvar, 8, nradial), f32)
    whole = jax.ShapeDtypeStruct(block, f32)

    even_t = [(i, i ^ 1) for i in range(tdev)]
    odd_t = [(i, (i + 1) % tdev if i % 2 else (i - 1) % tdev) for i in range(tdev)]
    even_x = [(i, i ^ 1) for i in range(xdev)]
    odd_x = [(i, i + 1 if i % 2 else i - 1) for i in range(1, xdev - 1)]

    def swap(te, to, xe, xo):
        return (
            lax.ppermute(te, "theta", even_t),
            lax.ppermute(to, "theta", odd_t),
            lax.ppermute(xe, "xr", even_x),
            lax.ppermute(xo, "xr", odd_x),
        )

    faces = pl.pallas_call(
        pack_kernel,
        in_specs=[spec(SM), spec(VM)],
        out_specs=[spec(VM)] * 4,
        out_shape=[face] * 4,
        compiler_params=params(),
        name="pack_faces",
    )(place, u)
    faces = swap(*faces)
    first, *faces = pl.pallas_call(
        first_kernel,
        in_specs=[spec(SM)] * 5 + [spec(VM)] * 7,
        out_specs=[spec(VM)] * 5,
        out_shape=[whole] + [face] * 4,
        compiler_params=params(),
        name="first_step",
    )(place, stagger, a_theta, a_axial, a_radial, u, src, sig, *faces)
    faces = swap(*faces)
    second, part = pl.pallas_call(
        functools.partial(second_kernel, tdev, xdev, nrad),
        in_specs=[spec(SM)] * 6 + [spec(VM)] * 11,
        out_specs=[spec(VM)] * 2,
        out_shape=[whole, jax.ShapeDtypeStruct((tdev, 8, mode_order.shape[1]), f32)],
        compiler_params=params(),
        name="second_step",
    )(
        place, stagger, a_theta, a_axial, a_radial, l_rows, first, u, src, sig, *faces, mode_order, mode_radial, mode_plane
    )
    got = lax.all_to_all(part, "theta", 0, 0, tiled=True)
    fields, amp = pl.pallas_call(
        functools.partial(correct_kernel, tdev, xdev, nrad),
        in_specs=[spec(SM)] * 2 + [spec(VM)] * 6,
        out_specs=[spec(VM)] * 2,
        out_shape=[whole, jax.ShapeDtypeStruct((xdev, 8, mode_order.shape[1]), f32)],
        compiler_params=params(),
        name="correct_planes",
    )(place, r_cols, got, gust, second, mode_order, mode_radial, mode_plane)
    amp = lax.all_to_all(amp, "xr", 0, 0, tiled=True)
    amp = jnp.sum(amp, axis=0)[:nhp].reshape(nharm, 1, two, -1)
    weight = (mode_plane[:, None, None, :] == jnp.arange(2)[None, :, None, None]).astype(f32)
    return fields.reshape(state.shape), weight * amp


def solution(mesh):
    placed = (
        P(None, None, None, "theta", "xr", None),
        P(None, None, None, "theta", "xr", None),
        P("theta", "xr", None),
        P("theta"),
        P(),
        P(),
        P(),
        P(),
        P(),
        P(),
        P(),
        P(),
        P(),
    )
    return jax.shard_map(
        local,
        mesh=mesh,
        in_specs=placed,
        out_specs=(P(None, None, None, "theta", "xr", None), P()),
        check_vma=False,
    )
```

time: 201 us -> 67.7 us (0.34); the launches traced: 197 us -> 67.4 us
  starting transfers between devices: 81.7 us -> 25.3 us
  blocking collectives: 72.3 us -> 16.1 us
  matrix products: 21.5 us -> 0 us
  waiting for transfers between devices: 0.32 us -> 13.1 us
  other arithmetic: 10 us -> 0.69 us
  Pallas kernels: 0 us -> 8.73 us
  local copies, waits for them, and re-layouts: 9.46 us -> 2.58 us
    psum x1 -> x0, blocking collectives: 72.3 us -> none  [local(): amp_real, amp_imag = lax.psum((part_real, part_imag), ('theta', 'xr'))]
    ppermute x24 -> x8, starting transfers between devices: 81.7 us -> 20.4 us  [the longest x2 10 us: swap(): lax.ppermute(xo, 'xr', odd_x)]
    dot_general x12 -> x0, matrix products: 21.5 us -> none  [the longest x2 8.11 us: local_residual(): jnp.einsum('vw,hpwtxr->hpvtxr', a_axial, diff_axial, precision=highest)]
    all_to_all x0 -> x1, blocking collectives: none -> 16.1 us  [local(): got = lax.all_to_all(part, 'theta', 0, 0, tiled=True)]
    pallas_call x0 -> x4, Pallas kernels: none -> 8.73 us  [the longest x1 3.45 us: local(): pl.pallas_call(functools.partial(second_kernel, tdev, xdev, nrad), in_spe...]
    ppermute x24 -> x8, waiting for transfers between devices: 0.32 us -> 8.3 us  [the longest x2 6.4 us: swap(): lax.ppermute(xo, 'xr', odd_x)]
    all_to_all x0 -> x1, starting transfers between devices: none -> 4.89 us  [local(): amp = lax.all_to_all(amp, 'xr', 0, 0, tiled=True)]
    all_to_all x0 -> x1, waiting for transfers between devices: none -> 4.84 us  [local(): amp = lax.all_to_all(amp, 'xr', 0, 0, tiled=True)]
  transfers between devices with their start and end apart: 24 -> 9, of which waited for: 1 -> 4; matrix products, arithmetic and copies ran while one was open for 11% -> 0% of each run, Pallas kernels for 0% -> 0%
where the time goes in v1:
time: 67.7 us; the launch traced here: 67.4 us
  starting transfers between devices  25.3 us (37%)
  blocking collectives  16.1 us (24%)
  waiting for transfers between devices  13.1 us (19%)
  Pallas kernels  8.73 us (13%)
  local copies, waits for them, and re-layouts  2.58 us (4%)
  between operations  0.82 us (1%)
  other arithmetic  0.69 us (1%)
    all_to_all x1, blocking collectives, local(): got = lax.all_to_all(part, 'theta', 0, 0, tiled=True)  16.1 us
    ppermute x2, starting transfers between devices, swap(): lax.ppermute(xo, 'xr', odd_x)  10 us
    ppermute x2, starting transfers between devices, swap(): lax.ppermute(to, 'theta', odd_t)  8.62 us
    ppermute x2, waiting for transfers between devices, swap(): lax.ppermute(xo, 'xr', odd_x)  6.4 us
    all_to_all x1, starting transfers between devices, local(): amp = lax.all_to_all(amp, 'xr', 0, 0, tiled=True)  4.89 us
    all_to_all x1, waiting for transfers between devices, local(): amp = lax.all_to_all(amp, 'xr', 0, 0, tiled=True)  4.84 us
    pallas_call x1, Pallas kernels, local(): pl.pallas_call(functools.partial(second_kernel, tdev, xdev, nrad), in_spe...  3.45 us
    pallas_call x1, Pallas kernels, local(): pl.pallas_call(first_kernel, in_specs=[spec(SM)] * 5 + [spec(VM)] * 7, ou...  3.07 us
  transfers between devices with their start and end apart: 9, of which 4 were waited for; matrix products, arithmetic and copies ran while one was open for 0% of the time, Pallas kernels for 0%

profile of v1, /device:TPU:2, one launch (start us, length us, event | category | flops | bytes accessed | tf_op | source)
XLA Modules:
  0.0 67.4 jit_solution(15821472868724680938)
XLA Ops:
  0.6 0.0 copy-start.12
  0.6 0.0 copy-start.5
  0.7 0.1 pad_add_fusion.place
  0.7 0.0 copy-start
  0.7 1.2 %copy-done = f32[3,2,5,8,8,128]{5,4,3,2,1,0:T(8,128)S(1)} copy-done((f32[3,2,5,8,8,128]{5,4,3,2,1,0:T(8,128)S(1)}, f32[3,2,5,8,8,128]{5,4,3,2,1,0:T(8,128)}, u32[]{:S(2)}) %copy-start) | copy-done | bytes 983064
  1.9 0.0 copy-start.1
  1.9 0.6 pack_faces.1
  2.6 0.0 copy-start.2
  2.6 0.1 collective-permute-start
  2.7 7.5 %collective-permute-start.1 = (f32[6,5,8,128]{3,2,1,0:T(8,128)S(1)}, f32[6,5,8,128]{3,2,1,0:T(8,128)S(1)}, u32[]{:S(2)}, u32[]{:S(2)}) collective-permute-start(f32[6,5,8,128]{3,2,1,0:T(8,128)S(1)} %get-tuple-element.16), channel_id=1, source_target_pairs={{0,248},{8,16},{16,8},{24,32},{32,24},{40,48},{48,40},{56,64},{64,... | collective-permute-start | bytes 368648 | tf_op jit(solution)/shard_map/ppermute | solution.py:244
  10.2 1.6 %collective-permute-start.2 = (f32[6,5,8,128]{3,2,1,0:T(8,128)S(1)}, f32[6,5,8,128]{3,2,1,0:T(8,128)S(1)}, u32[]{:S(2)}, u32[]{:S(2)}) collective-permute-start(f32[6,5,8,128]{3,2,1,0:T(8,128)S(1)} %get-tuple-element.17), channel_id=1, source_target_pairs={{0,1},{1,0},{2,3},{3,2},{4,5},{5,4},{6,7},{7,6},{8,9},{9,8},{10,11... | collective-permute-start | bytes 368648 | tf_op jit(solution)/shard_map/ppermute | solution.py:245
  11.8 4.9 %collective-permute-start.3 = (f32[6,5,8,128]{3,2,1,0:T(8,128)S(1)}, f32[6,5,8,128]{3,2,1,0:T(8,128)S(1)}, u32[]{:S(2)}, u32[]{:S(2)}) collective-permute-start(f32[6,5,8,128]{3,2,1,0:T(8,128)S(1)} %get-tuple-element.18), channel_id=1, source_target_pairs={{1,2},{2,1},{3,4},{4,3},{5,6},{6,5},{9,10},{10,9},{11,12},{12,11},... | collective-permute-start | bytes 368648 | tf_op jit(solution)/shard_map/ppermute | solution.py:246
  16.7 0.0 copy-done.12
  16.8 0.0 copy-start.4
  16.8 0.0 collective-permute-done.te
  16.8 0.0 collective-permute-done.1.to
  16.8 0.0 collective-permute-done.2.xe
  16.8 3.9 %collective-permute-done.3.xo = f32[6,5,8,128]{3,2,1,0:T(8,128)S(1)} collective-permute-done((f32[6,5,8,128]{3,2,1,0:T(8,128)S(1)}, f32[6,5,8,128]{3,2,1,0:T(8,128)S(1)}, u32[]{:S(2)}, u32[]{:S(2)}) %collective-permute-start.3) | collective-permute-done | bytes 122912 | tf_op jit(solution)/shard_map/ppermute | solution.py:246
  20.7 0.0 copy-start.9
  20.7 0.0 copy-done.5
  20.7 0.0 copy-done.1
  20.7 0.0 copy-done.2
  20.7 0.0 copy-done.4
  20.7 0.6 copy-done.9
  21.3 3.1 %first_step.1 = (f32[6,5,64,128]{3,2,1,0:T(8,128)S(1)}, f32[6,5,8,128]{3,2,1,0:T(8,128)S(1)}, f32[6,5,8,128]{3,2,1,0:T(8,128)S(1)}, f32[6,5,8,128]{3,2,1,0:T(8,128)S(1)}, f32[6,5,8,128]{3,2,1,0:T(8,128)S(1)}) custom-call(s32[2]{0:T(128)S(1)} %pad_add_fusion.place, s32[2]{0:T(128)S(1)} %copy-done.9, f32[4,5,5]{2,1,0:T(8,128)S(1)} %copy.16.a_theta, ...), custom_call_target="tpu_custom_call" | custom-call | tf_op jit(solution)/shard_map/first_step/pallas_call | solution.py:258
  24.4 0.1 collective-permute-start.4
  24.5 0.0 copy-start.7
  24.5 1.1 %collective-permute-start.5 = (f32[6,5,8,128]{3,2,1,0:T(8,128)S(1)}, f32[6,5,8,128]{3,2,1,0:T(8,128)S(1)}, u32[]{:S(2)}, u32[]{:S(2)}) collective-permute-start(f32[6,5,8,128]{3,2,1,0:T(8,128)S(1)} %get-tuple-element.21), channel_id=1, source_target_pairs={{0,248},{8,16},{16,8},{24,32},{32,24},{40,48},{48,40},{56,64},{64,... | collective-permute-start | bytes 368648 | tf_op jit(solution)/shard_map/ppermute | solution.py:244
  25.6 0.0 copy-start.6
  25.6 0.0 copy-start.3
  25.6 0.0 collective-permute-start.6
  25.6 0.0 copy-start.10
  25.6 5.1 %collective-permute-start.7 = (f32[6,5,8,128]{3,2,1,0:T(8,128)S(1)}, f32[6,5,8,128]{3,2,1,0:T(8,128)S(1)}, u32[]{:S(2)}, u32[]{:S(2)}) collective-permute-start(f32[6,5,8,128]{3,2,1,0:T(8,128)S(1)} %get-tuple-element.23), channel_id=1, source_target_pairs={{1,2},{2,1},{3,4},{4,3},{5,6},{6,5},{9,10},{10,9},{11,12},{12,11},... | collective-permute-start | bytes 368648 | tf_op jit(solution)/shard_map/ppermute | solution.py:246
  30.7 0.0 collective-permute-done.4.te
  30.7 1.9 %collective-permute-done.5.to = f32[6,5,8,128]{3,2,1,0:T(8,128)S(1)} collective-permute-done((f32[6,5,8,128]{3,2,1,0:T(8,128)S(1)}, f32[6,5,8,128]{3,2,1,0:T(8,128)S(1)}, u32[]{:S(2)}, u32[]{:S(2)}) %collective-permute-start.5) | collective-permute-done | bytes 122912 | tf_op jit(solution)/shard_map/ppermute | solution.py:244
  32.6 0.0 collective-permute-done.6.xe
  32.6 2.6 %collective-permute-done.7.xo = f32[6,5,8,128]{3,2,1,0:T(8,128)S(1)} collective-permute-done((f32[6,5,8,128]{3,2,1,0:T(8,128)S(1)}, f32[6,5,8,128]{3,2,1,0:T(8,128)S(1)}, u32[]{:S(2)}, u32[]{:S(2)}) %collective-permute-start.7) | collective-permute-done | bytes 122912 | tf_op jit(solution)/shard_map/ppermute | solution.py:246
  35.2 0.0 copy-done.7
  35.2 0.0 copy-done.6
  35.2 0.0 copy-done.3
  35.2 0.0 copy-done.10
  35.2 3.4 %second_step.1 = (f32[6,5,64,128]{3,2,1,0:T(8,128)S(1)}, f32[32,8,128]{2,1,0:T(8,128)S(1)}) custom-call(s32[2]{0:T(128)S(1)} %pad_add_fusion.place, s32[2]{0:T(128)S(1)} %copy-done.9, f32[4,5,5]{2,1,0:T(8,128)S(1)} %copy.16.a_theta, f32[5,5]{1,0:T(8,128)S(1)} %copy-done.4, f32[5,5]{1,0:T(8,128)S(1)} %copy-done.5, f32[2,5]{1,0:T(2,128)S(1)} %copy-done.10, ...), custom_call_target="tpu_custom_call" | custom-call | tf_op jit(solution)/shard_map/second_step/pallas_call | solution.py:267
  38.6 0.0 copy-start.8
  38.7 16.1 %all_to_all.10.got_ref = f32[32,8,128]{2,1,0:T(8,128)S(1)} all-to-all(f32[32,8,128]{2,1,0:T(8,128)S(1)} %get-tuple-element.24), channel_id=1, replica_groups=mesh['theta'=32,'xr'=8] {'theta'}, dimensions={0} | all-to-all | bytes 262144 | tf_op jit(solution)/shard_map/all_to_all | solution.py:277
  54.7 0.0 copy-start.11
  54.8 0.0 copy-done.8
  54.8 0.7 %copy-done.11 = f32[2,5]{1,0:T(2,128)S(1)} copy-done((f32[2,5]{1,0:T(2,128)S(1)}, f32[2,5]{1,0:T(2,128)}, u32[]{:S(2)}) %copy-start.11) | copy-done | bytes 64
  55.4 1.6 %correct_planes.1 = (f32[6,5,64,128]{3,2,1,0:T(8,128)}, f32[8,8,128]{2,1,0:T(8,128)}) custom-call(s32[2]{0:T(128)S(1)} %pad_add_fusion.place, f32[2,5]{1,0:T(2,128)S(1)} %copy-done.11, f32[32,8,128]{2,1,0:T(8,128)S(1)} %all_to_all.10.got_ref, f32[3,2,128]{2,1,0:T(2,128)S(1)} %copy-done.8, f32[6,5,64,128]{3,2,1,0:T(8,128)S(1)} %get-tuple-element.25.second_ref, ...), custom_call_target="tpu_custom_call" | custom-call | tf_op jit(solution)/shard_map/correct_planes/pallas_call | solution.py:278
  57.0 4.9 %all-to-all-start.1 = ((f32[8,8,128]{2,1,0:T(8,128)}), f32[8,8,128]{2,1,0:T(8,128)S(1)}, u32[]{:S(2)}, u32[]{:S(2)}) async-start(f32[8,8,128]{2,1,0:T(8,128)} %get-tuple-element.27), calls=%async_computation.1 | async-start | bytes 65536 | tf_op jit(solution)/shard_map/all_to_all | solution.py:286
  61.9 4.8 %all-to-all-done.1 = f32[8,8,128]{2,1,0:T(8,128)S(1)} async-done(((f32[8,8,128]{2,1,0:T(8,128)}), f32[8,8,128]{2,1,0:T(8,128)S(1)}, u32[]{:S(2)}, u32[]{:S(2)}) %all-to-all-start.1) | async-done | bytes 32800 | tf_op jit(solution)/shard_map/all_to_all | solution.py:286
  66.8 0.6 broadcast_multiply_fusion
  (4 shorter events, 0.0 us)
Async XLA Ops:
  0.6 16.1 %copy-start.12 = (f32[4,5,5]{2,0,1:T(4,128)S(1)}, f32[4,5,5]{2,0,1:T(4,128)}, u32[]{:S(2)}) copy-start(f32[4,5,5]{2,0,1:T(4,128)} %param.17) | copy-start | bytes 1204
  0.6 20.0 %copy-start.5 = (f32[5,5]{1,0:T(8,128)S(1)}, f32[5,5]{1,0:T(8,128)}, u32[]{:S(2)}) copy-start(f32[5,5]{1,0:T(8,128)} %a_radial.3) | copy-start | bytes 304
  0.7 1.2 %copy-start = (f32[3,2,5,8,8,128]{5,4,3,2,1,0:T(8,128)S(1)}, f32[3,2,5,8,8,128]{5,4,3,2,1,0:T(8,128)}, u32[]{:S(2)}) copy-start(f32[3,2,5,8,8,128]{5,4,3,2,1,0:T(8,128)} %param.13) | copy-start | bytes 2949124
  1.9 18.7 %copy-start.1 = (f32[3,2,5,8,8,128]{5,4,3,2,1,0:T(8,128)S(1)}, f32[3,2,5,8,8,128]{5,4,3,2,1,0:T(8,128)}, u32[]{:S(2)}) copy-start(f32[3,2,5,8,8,128]{5,4,3,2,1,0:T(8,128)} %param.14) | copy-start | bytes 2949124
  2.6 18.1 %copy-start.2 = (f32[8,8,128]{2,1,0:T(8,128)S(1)}, f32[8,8,128]{2,1,0:T(8,128)}, u32[]{:S(2)}) copy-start(f32[8,8,128]{2,1,0:T(8,128)} %param.15) | copy-start | bytes 98308
  2.6 14.2 %collective-permute-start = (f32[6,5,8,128]{3,2,1,0:T(8,128)S(1)}, f32[6,5,8,128]{3,2,1,0:T(8,128)S(1)}, u32[]{:S(2)}, u32[]{:S(2)}) collective-permute-start(f32[6,5,8,128]{3,2,1,0:T(8,128)S(1)} %get-tuple-element.15), channel_id=1, source_target_pairs={{0,8},{8,0},{16,24},{24,16},{32,40},{40,32},{48,56},{56,48},{64,72... | collective-permute-start | bytes 368648 | tf_op jit(solution)/shard_map/ppermute | solution.py:243
  2.7 14.1 %collective-permute-start.1 = (f32[6,5,8,128]{3,2,1,0:T(8,128)S(1)}, f32[6,5,8,128]{3,2,1,0:T(8,128)S(1)}, u32[]{:S(2)}, u32[]{:S(2)}) collective-permute-start(f32[6,5,8,128]{3,2,1,0:T(8,128)S(1)} %get-tuple-element.16), channel_id=1, source_target_pairs={{0,248},{8,16},{16,8},{24,32},{32,24},{40,48},{48,40},{56,64},{64,... | collective-permute-start | bytes 368648 | tf_op jit(solution)/shard_map/ppermute | solution.py:244
  10.2 6.6 %collective-permute-start.2 = (f32[6,5,8,128]{3,2,1,0:T(8,128)S(1)}, f32[6,5,8,128]{3,2,1,0:T(8,128)S(1)}, u32[]{:S(2)}, u32[]{:S(2)}) collective-permute-start(f32[6,5,8,128]{3,2,1,0:T(8,128)S(1)} %get-tuple-element.17), channel_id=1, source_target_pairs={{0,1},{1,0},{2,3},{3,2},{4,5},{5,4},{6,7},{7,6},{8,9},{9,8},{10,11... | collective-permute-start | bytes 368648 | tf_op jit(solution)/shard_map/ppermute | solution.py:245
  11.8 8.9 %collective-permute-start.3 = (f32[6,5,8,128]{3,2,1,0:T(8,128)S(1)}, f32[6,5,8,128]{3,2,1,0:T(8,128)S(1)}, u32[]{:S(2)}, u32[]{:S(2)}) collective-permute-start(f32[6,5,8,128]{3,2,1,0:T(8,128)S(1)} %get-tuple-element.18), channel_id=1, source_target_pairs={{1,2},{2,1},{3,4},{4,3},{5,6},{6,5},{9,10},{10,9},{11,12},{12,11},... | collective-permute-start | bytes 368648 | tf_op jit(solution)/shard_map/ppermute | solution.py:246
  16.8 3.9 %copy-start.4 = (f32[5,5]{1,0:T(8,128)S(1)}, f32[5,5]{1,0:T(8,128)}, u32[]{:S(2)}) copy-start(f32[5,5]{1,0:T(8,128)} %a_axial.3) | copy-start | bytes 304
  20.7 0.7 copy-start.9
  24.4 6.3 %collective-permute-start.4 = (f32[6,5,8,128]{3,2,1,0:T(8,128)S(1)}, f32[6,5,8,128]{3,2,1,0:T(8,128)S(1)}, u32[]{:S(2)}, u32[]{:S(2)}) collective-permute-start(f32[6,5,8,128]{3,2,1,0:T(8,128)S(1)} %get-tuple-element.20), channel_id=1, source_target_pairs={{0,8},{8,0},{16,24},{24,16},{32,40},{40,32},{48,56},{56,48},{64,72... | collective-permute-start | bytes 368648 | tf_op jit(solution)/shard_map/ppermute | solution.py:243
  24.5 10.7 %copy-start.7 = (s32[3,128]{1,0:T(4,128)S(1)}, s32[3,128]{1,0:T(4,128)}, u32[]{:S(2)}) copy-start(s32[3,128]{1,0:T(4,128)} %radial.3) | copy-start | bytes 4612
  24.5 8.1 %collective-permute-start.5 = (f32[6,5,8,128]{3,2,1,0:T(8,128)S(1)}, f32[6,5,8,128]{3,2,1,0:T(8,128)S(1)}, u32[]{:S(2)}, u32[]{:S(2)}) collective-permute-start(f32[6,5,8,128]{3,2,1,0:T(8,128)S(1)} %get-tuple-element.21), channel_id=1, source_target_pairs={{0,248},{8,16},{16,8},{24,32},{32,24},{40,48},{48,40},{56,64},{64,... | collective-permute-start | bytes 368648 | tf_op jit(solution)/shard_map/ppermute | solution.py:244
  25.6 9.6 %copy-start.6 = (s32[3,128]{1,0:T(4,128)S(1)}, s32[3,128]{1,0:T(4,128)}, u32[]{:S(2)}) copy-start(s32[3,128]{1,0:T(4,128)} %order.3) | copy-start | bytes 4612
  25.6 9.6 %copy-start.3 = (s32[3,128]{1,0:T(4,128)S(1)}, s32[3,128]{1,0:T(4,128)}, u32[]{:S(2)}) copy-start(s32[3,128]{1,0:T(4,128)} %plane.3) | copy-start | bytes 4612
  25.6 7.0 %collective-permute-start.6 = (f32[6,5,8,128]{3,2,1,0:T(8,128)S(1)}, f32[6,5,8,128]{3,2,1,0:T(8,128)S(1)}, u32[]{:S(2)}, u32[]{:S(2)}) collective-permute-start(f32[6,5,8,128]{3,2,1,0:T(8,128)S(1)} %get-tuple-element.22), channel_id=1, source_target_pairs={{0,1},{1,0},{2,3},{3,2},{4,5},{5,4},{6,7},{7,6},{8,9},{9,8},{10,11... | collective-permute-start | bytes 368648 | tf_op jit(solution)/shard_map/ppermute | solution.py:245
  25.6 9.6 %copy-start.10 = (f32[2,5]{1,0:T(2,128)S(1)}, f32[2,5]{1,0:T(2,128)}, u32[]{:S(2)}) copy-start(f32[2,5]{1,0:T(2,128)} %l_rows.1) | copy-start | bytes 124
  25.6 9.6 %collective-permute-start.7 = (f32[6,5,8,128]{3,2,1,0:T(8,128)S(1)}, f32[6,5,8,128]{3,2,1,0:T(8,128)S(1)}, u32[]{:S(2)}, u32[]{:S(2)}) collective-permute-start(f32[6,5,8,128]{3,2,1,0:T(8,128)S(1)} %get-tuple-element.23), channel_id=1, source_target_pairs={{1,2},{2,1},{3,4},{4,3},{5,6},{6,5},{9,10},{10,9},{11,12},{12,11},... | collective-permute-start | bytes 368648 | tf_op jit(solution)/shard_map/ppermute | solution.py:246
  38.6 16.1 %copy-start.8 = (f32[3,2,128]{2,1,0:T(2,128)S(1)}, f32[3,2,128]{2,1,0:T(2,128)}, u32[]{:S(2)}) copy-start(f32[3,2,128]{2,1,0:T(2,128)} %gust.1) | copy-start | bytes 9220
  54.7 0.7 %copy-start.11 = (f32[2,5]{1,0:T(2,128)S(1)}, f32[2,5]{1,0:T(2,128)}, u32[]{:S(2)}) copy-start(f32[2,5]{1,0:T(2,128)} %r_cols.1) | copy-start | bytes 124
  57.0 9.7 %all-to-all-start.1 = ((f32[8,8,128]{2,1,0:T(8,128)}), f32[8,8,128]{2,1,0:T(8,128)S(1)}, u32[]{:S(2)}, u32[]{:S(2)}) async-start(f32[8,8,128]{2,1,0:T(8,128)} %get-tuple-element.27), calls=%async_computation.1 | async-start | bytes 65536 | tf_op jit(solution)/shard_map/all_to_all | solution.py:286

commit v2 on v1

v2 whole, which is shorter than its diff:
```python
import functools
import math

import jax
import jax.numpy as jnp
from jax import lax
from jax.experimental import pallas as pl
from jax.experimental.pallas import tpu as pltpu
from jax.sharding import PartitionSpec as P

courant = 0.5
viscosity = 0.1
base_frequency = 0.5
highest = lax.Precision.HIGHEST
VM = pltpu.VMEM
SM = pltpu.SMEM
planes_first = True
wide = ("pack_faces", "plane_part", "mode_tables", "first_step")


def spec(space):
    return pl.BlockSpec(memory_space=space)


def params(name):
    size = 60 if name in wide else 16
    return pltpu.CompilerParams(vmem_limit_bytes=size * 1024 * 1024)


def write_faces(place, u_ref, te_ref, to_ref, xe_ref, xo_ref):
    nhp, nvar = u_ref.shape[0], u_ref.shape[1]
    todd = lax.rem(place[0], 2)
    xodd = lax.rem(place[1], 2)
    for out_ref, layer in ((te_ref, 1 - todd), (to_ref, todd)):
        start = pl.multiple_of(layer * 56, 8)
        out_ref[0:nhp] = u_ref[:, :, pl.ds(start, 8), :]
    for out_ref, row in ((xe_ref, 1 - xodd), (xo_ref, xodd)):
        for i in range(nhp):
            for v in range(nvar):
                out_ref[i, v] = u_ref[i, v, pl.ds(row * 7, 8, stride=8), :]


def pack_kernel(place, stagger, u_ref, sig_ref, te_ref, to_ref, xe_ref, xo_ref):
    write_faces(place, u_ref, te_ref, to_ref, xe_ref, xo_ref)
    nhp = u_ref.shape[0]
    nr = u_ref.shape[3]
    npass = stagger.shape[0]
    todd = lax.rem(place[0], 2)
    for out_ref, layer in ((te_ref, 1 - todd), (to_ref, todd)):
        start = pl.multiple_of(layer * 48, 8)
        out_ref[nhp, 0] = sig_ref[pl.ds(start, 8), :]
        out_ref[nhp, 1] = sig_ref[pl.ds(start + 8, 8), :]
        setting = stagger[layer * (npass - 1)].astype(jnp.float32)
        for i in range(2, out_ref.shape[1]):
            out_ref[nhp, i] = jnp.full((8, nr), setting, jnp.float32)


def step(factor, place, stagger, a_theta, a_axial, a_radial, u_ref, base_ref, src_ref, sig_ref, te, to, xe, xo, out_ref):
    nhp, nvar, rows, nr = u_ref.shape
    tcells = rows // 8
    cpp = tcells // stagger.shape[0]
    todd = lax.rem(place[0], 2) == 1
    xodd = lax.rem(place[1], 2) == 1
    shape = (nhp, 8, nr)
    row = lax.broadcasted_iota(jnp.int32, shape, 1)
    lane = lax.broadcasted_iota(jnp.int32, shape, 2)
    axial = [[0.5 * a_axial[v, w] for w in range(nvar)] for v in range(nvar)]
    radial = [[0.5 * a_radial[v, w] for w in range(nvar)] for v in range(nvar)]
    for t in range(tcells):
        setting = stagger[t // cpp]
        tile = slice(8 * t, 8 * t + 8)
        sig = sig_ref[tile, :][None]
        own = sig + 6.0 * viscosity
        scaled = (factor * courant) / (1.0 + sig)
        acc = [None] * nvar
        for w in range(nvar):
            u = u_ref[:, w, tile, :]
            if t == 0:
                tm = jnp.where(todd, te[0:nhp, w], to[0:nhp, w])
            else:
                tm = u_ref[:, w, 8 * t - 8 : 8 * t, :]
            if t == tcells - 1:
                tp = jnp.where(todd, to[0:nhp, w], te[0:nhp, w])
            else:
                tp = u_ref[:, w, 8 * t + 8 : 8 * t + 16, :]
            e = xe[:, w, t : t + 1, :]
            o = xo[:, w, t : t + 1, :]
            xlo = jnp.where(xodd, e, o)
            xhi = jnp.where(xodd, o, e)
            xm = jnp.where(row == 0, jnp.broadcast_to(xlo, shape), pltpu.roll(u, 1, 1))
            xp = jnp.where(row == 7, jnp.broadcast_to(xhi, shape), pltpu.roll(u, 7, 1))
            rm = jnp.where(lane == 0, 0.0, pltpu.roll(u, 1, 2))
            rp = jnp.where(lane == nr - 1, 0.0, pltpu.roll(u, nr - 1, 2))
            dt_, dx_, dr_ = tp - tm, xp - xm, rp - rm
            near = ((tp + tm) + (xp + xm)) + (rp + rm)
            turned = []
            for h in range(nhp // 2):
                freq = base_frequency * (1.0 + h)
                turned.append(-freq * u[2 * h + 1 : 2 * h + 2])
                turned.append(freq * u[2 * h : 2 * h + 1])
            local_part = (own * u - viscosity * near) + (jnp.concatenate(turned, axis=0) - src_ref[:, w, tile, :])
            for v in range(nvar):
                flux = (0.5 * a_theta[setting, v, w]) * dt_ + axial[v][w] * dx_ + radial[v][w] * dr_
                if v == w:
                    flux = flux + local_part
                acc[v] = flux if acc[v] is None else acc[v] + flux
        for v in range(nvar):
            out_ref[:, v, tile, :] = base_ref[:, v, tile, :] - scaled * acc[v]


def first_kernel(
    place, stagger, a_theta, a_axial, a_radial, u_ref, src_ref, sig_ref, te, to, xe, xo, after, out_ref, te2, to2, xe2, xo2
):
    step(0.5, place, stagger, a_theta, a_axial, a_radial, u_ref, u_ref, src_ref, sig_ref, te, to, xe, xo, out_ref)
    write_faces(place, out_ref, te2, to2, xe2, xo2)


def second_kernel(
    place, stagger, a_theta, a_axial, a_radial, u_ref, base_ref, src_ref, sig_ref, te, to, xe, xo, out_ref
):
    step(1.0, place, stagger, a_theta, a_axial, a_radial, u_ref, base_ref, src_ref, sig_ref, te, to, xe, xo, out_ref)


def table_kernel(tdevices, place, order, radial, cos_ref, sin_ref, wave_ref, pick_ref):
    nharm, nmode = order.shape
    tcells = 8
    total = tcells * tdevices
    row = lax.broadcasted_iota(jnp.int32, (2 * tcells, nmode), 0)
    cell = place[0] * tcells + jnp.where(row < 12, row, row - 16)
    nrad, nr = wave_ref.shape
    wave_ref[...] = radial_table(nrad, nr)
    for h in range(nharm):
        turns = lax.rem(order[h : h + 1, :] * cell + 64 * total, total)
        angle = 2.0 * math.pi * turns.astype(jnp.float32) / total
        cos_ref[h] = jnp.cos(angle)
        sin_ref[h] = jnp.sin(angle)
        n = lax.broadcasted_iota(jnp.int32, (nrad, nmode), 0)
        pick_ref[h] = (n == radial[h : h + 1, :]).astype(jnp.float32)


def radial_table(nrad, nr):
    n = lax.broadcasted_iota(jnp.int32, (nrad, nr), 0)
    pos = lax.broadcasted_iota(jnp.int32, (nrad, nr), 1).astype(jnp.float32) + 0.5
    wave = math.sqrt(2.0) * jnp.cos(math.pi * n.astype(jnp.float32) * pos / nr)
    return jnp.where(n == 0, 1.0, wave)


def turn(u):
    out = []
    for h in range(u.shape[0] // 2):
        freq = base_frequency * (1.0 + h)
        out.append(-freq * u[2 * h + 1 : 2 * h + 2])
        out.append(freq * u[2 * h : 2 * h + 1])
    return jnp.concatenate(out, axis=0)


def plane_part(last, tdevices, stagger, a_theta, a_axial, a_radial, l_rows, u_ref, src_ref, sig_ref, lo, hi, refs):
    plane, cos_ref, sin_ref, wave_ref, pick_ref, part_ref = refs
    nhp, nvar, rows, nr = u_ref.shape
    nharm, nmode = plane.shape
    nset = a_theta.shape[0]
    scale = 1.0 / math.sqrt(8 * tdevices * nr)
    shape = (nhp, 8, nr)
    row = lax.broadcasted_iota(jnp.int32, shape, 1)
    lane = lax.broadcasted_iota(jnp.int32, shape, 2)
    row1, row2 = row[0], lax.broadcasted_iota(jnp.int32, (8, nr), 0)
    side = (1 - 2 * last).astype(jnp.float32)
    at = [last * 7 + j * (1 - 2 * last) for j in range(3)]

    def own_rows(ref, v, j):
        return jnp.stack([ref[i, v, pl.ds(at[j], 8, stride=8), :] for i in range(nhp)])

    def shift_r(u):
        return (
            jnp.where(lane == 0, 0.0, pltpu.roll(u, 1, 2)),
            jnp.where(lane == nr - 1, 0.0, pltpu.roll(u, nr - 1, 2)),
        )

    def row_of(face, i, j):
        return jnp.broadcast_to(face(i, pl.ds(at[j], 1)), (8, nr))

    settings = jnp.where(row2 < 4, hi(2, slice(0, 8)), lo(2, slice(0, 8)))
    table = [[None] * nvar for _ in range(nvar)]
    outer = [[None] * nvar for _ in range(nvar)]
    for v in range(nvar):
        for w in range(nvar):
            table[v][w] = jnp.where(row2 < 4, 0.5 * a_theta[stagger[0], v, w], 0.5 * a_theta[stagger[1], v, w])[None]
            value = jnp.full((8, nr), 0.5 * a_theta[nset - 1, v, w], jnp.float32)
            for s in range(nset - 1):
                value = jnp.where(settings == float(s), 0.5 * a_theta[s, v, w], value)
            outer[v][w] = value[None]
    axial = [[0.5 * side * a_axial[v, w] for w in range(nvar)] for v in range(nvar)]
    radial = [[0.5 * a_radial[v, w] for w in range(nvar)] for v in range(nvar)]
    weight = [l_rows[last, v] for v in range(nvar)]

    sig, sig_out, step_in, step_out = [], [], [], []
    for j in range(2):
        sig.append(sig_ref[pl.ds(at[j], 8, stride=8), :][None])
        edge = jnp.where(row2 == 0, row_of(hi, 0, j), row_of(hi, 1, j))
        edge = jnp.where(row2 == 6, row_of(lo, 0, j), edge)
        edge = jnp.where(row2 == 7, row_of(lo, 1, j), edge)
        sig_out.append(edge[None])
        step_in.append(courant / (1.0 + sig[j]))
        step_out.append(courant / (1.0 + sig_out[j]))

    state = [[own_rows(u_ref, v, j) for v in range(nvar)] for j in range(3)]
    source = [[own_rows(src_ref, v, j) for v in range(nvar)] for j in range(2)]
    first, first_out = [], []
    for j in range(2):
        acc, acc_out = [None] * nvar, [None] * nvar
        for w in range(nvar):
            u = state[j][w]
            up, down = pltpu.roll(u, 7, 1), pltpu.roll(u, 1, 1)
            tp, tm = jnp.where(row == 7, 0.0, up), jnp.where(row == 0, 0.0, down)
            tp_out, tm_out = jnp.where(row == 7, up, 0.0), jnp.where(row == 0, down, 0.0)
            rm, rp = shift_r(u)
            inner = state[j + 1][w]
            if j == 0:
                dx_, nx = inner, inner
            else:
                dx_, nx = inner - state[0][w], inner + state[0][w]
            dt_, dr_ = tp - tm, rp - rm
            dt_out = tp_out - tm_out
            near = (tp + tm) + nx + (rp + rm)
            part = ((sig[j] + 6.0 * viscosity) * u - viscosity * near) + (turn(u) - source[j][w])
            for v in range(nvar):
                flux = table[v][w] * dt_ + axial[v][w] * dx_ + radial[v][w] * dr_
                flux_out = outer[v][w] * dt_out
                if v == w:
                    flux = flux + part
                    flux_out = flux_out - viscosity * (tp_out + tm_out)
                acc[v] = flux if acc[v] is None else acc[v] + flux
                acc_out[v] = flux_out if acc_out[v] is None else acc_out[v] + flux_out
        first.append([state[j][v] - (0.5 * step_in[j]) * acc[v] for v in range(nvar)])
        first_out.append([-(0.5 * step_out[j]) * acc_out[v] for v in range(nvar)])

    zero = jnp.zeros(shape, jnp.float32)
    base, total, total_out, mean, mean_out = zero, zero, zero, zero, zero
    for w in range(nvar):
        f, g = first[0][w], first_out[0][w]
        fd, fu, gd, gu = pltpu.roll(f, 1, 1), pltpu.roll(f, 7, 1), pltpu.roll(g, 1, 1), pltpu.roll(g, 7, 1)
        lt = sum(weight[v] * table[v][w] for v in range(nvar))
        lt_out = sum(weight[v] * outer[v][w] for v in range(nvar))
        lx = sum(weight[v] * axial[v][w] for v in range(nvar))
        lr = sum(weight[v] * radial[v][w] for v in range(nvar))
        for inside in (True, False):
            here, beside = (f, first[1][w]) if inside else (g, first_out[1][w])
            if inside:
                tm, tp = jnp.where(row == 0, gd, fd), jnp.where(row == 7, gu, fu)
            else:
                tm, tp = jnp.where(row == 0, fd, gd), jnp.where(row == 7, fu, gu)
            rm, rp = shift_r(here)
            near = (tp + tm) + beside + (rp + rm)
            term = (lt if inside else lt_out) * (tp - tm) + lx * beside + lr * (rp - rm)
            s = (sig if inside else sig_out)[0] + 6.0 * viscosity
            if inside:
                total = total + term + weight[w] * ((s * here - viscosity * near) - source[0][w])
                mean = mean + weight[w] * here
                base = base + weight[w] * state[0][w]
            else:
                total_out = total_out + term + weight[w] * (s * here - viscosity * near)
                mean_out = mean_out + weight[w] * here
    values = base - step_in[0] * (total + turn(mean))
    values_out = -step_out[0] * (total_out + turn(mean_out))
    values = jnp.stack([values, values_out], axis=1).reshape(nhp * 16, nr)
    nt = (((1,), (1,)), ((), ()))
    grouped = lax.dot_general(values, wave_ref[...], nt, precision=highest, preferred_element_type=jnp.float32)
    for h in range(nharm):
        mine = plane[h : h + 1, :] == last
        both = jnp.dot(
            grouped[32 * h : 32 * h + 32], pick_ref[h], precision=highest, preferred_element_type=jnp.float32
        )
        re, im = both[:16], both[16:]
        cos, sin = cos_ref[h], sin_ref[h]
        part_re = scale * jnp.sum(re * cos + im * sin, axis=0, keepdims=True)
        part_im = scale * jnp.sum(im * cos - re * sin, axis=0, keepdims=True)
        part_re, part_im = jnp.where(mine, part_re, 0.0), jnp.where(mine, part_im, 0.0)
        part_ref[:, 2 * h] = jnp.broadcast_to(part_re, (tdevices, nmode))
        part_ref[:, 2 * h + 1] = jnp.broadcast_to(part_im, (tdevices, nmode))
    part_ref[:, nhp:] = jnp.zeros((tdevices, 8 - nhp, nmode), jnp.float32)


def plane_kernel(
    tdevices,
    xdevices,
    place,
    stagger,
    a_theta,
    a_axial,
    a_radial,
    l_rows,
    u_ref,
    src_ref,
    sig_ref,
    te,
    to,
    plane,
    cos_ref,
    sin_ref,
    wave_ref,
    pick_ref,
    after,
    after2,
    after3,
    part_ref,
):
    nhp = u_ref.shape[0]
    last = (place[1] == xdevices - 1).astype(jnp.int32)
    holds = jnp.logical_or(place[1] == 0, place[1] == xdevices - 1)
    todd = lax.rem(place[0], 2) == 1

    def lo(i, rows):
        return jnp.where(todd, te[nhp, i, rows, :], to[nhp, i, rows, :])

    def hi(i, rows):
        return jnp.where(todd, to[nhp, i, rows, :], te[nhp, i, rows, :])

    @pl.when(holds)
    def _():
        refs = (plane, cos_ref, sin_ref, wave_ref, pick_ref, part_ref)
        plane_part(
            last, tdevices, stagger, a_theta, a_axial, a_radial, l_rows, u_ref, src_ref, sig_ref, lo, hi, refs
        )

    @pl.when(jnp.logical_not(holds))
    def _():
        part_ref[...] = jnp.zeros(part_ref.shape, jnp.float32)


def share_kernel(xdevices, got_ref, amp_ref):
    amp = jnp.sum(got_ref[...], axis=0)
    for d in range(xdevices):
        amp_ref[d] = amp


def finish_kernel(got_ref, plane, out_ref):
    amp = jnp.sum(got_ref[...], axis=0)
    for h in range(plane.shape[0]):
        for b in range(2):
            out_ref[h, b] = jnp.where(plane[h : h + 1, :] == b, amp[2 * h : 2 * h + 2], 0.0)


def correct_kernel(
    tdevices,
    xdevices,
    place,
    r_cols,
    got_ref,
    gust,
    second_ref,
    plane,
    cos_ref,
    sin_ref,
    wave_ref,
    pick_ref,
    out_ref,
):
    nhp, nvar, rows, nr = out_ref.shape
    nharm, nmode = plane.shape
    scale = 1.0 / math.sqrt(8 * tdevices * nr)
    last = (place[1] == xdevices - 1).astype(jnp.int32)
    holds = jnp.logical_or(place[1] == 0, place[1] == xdevices - 1)
    out_ref[...] = second_ref[...]

    @pl.when(holds)
    def _():
        amp = jnp.sum(got_ref[...], axis=0)
        for h in range(nharm):
            cos, sin = cos_ref[h, 0:8], sin_ref[h, 0:8]
            mine = plane[h : h + 1, :] == last
            miss_re = jnp.where(mine, amp[2 * h : 2 * h + 1] - gust[h, 0:1, :], 0.0)
            miss_im = jnp.where(mine, amp[2 * h + 1 : 2 * h + 2] - gust[h, 1:2, :], 0.0)
            coef = jnp.concatenate([miss_re * cos - miss_im * sin, miss_re * sin + miss_im * cos], axis=0)
            nt = (((1,), (1,)), ((), ()))
            grouped = lax.dot_general(coef, pick_ref[h], nt, precision=highest, preferred_element_type=jnp.float32)
            q = scale * jnp.dot(grouped, wave_ref[...], precision=highest, preferred_element_type=jnp.float32)
            for p in range(2):
                for v in range(nvar):
                    at = pl.ds(last * 7, 8, stride=8)
                    out_ref[2 * h + p, v, at, :] = (
                        second_ref[2 * h + p, v, at, :] - r_cols[last, v] * q[p * 8 : (p + 1) * 8]
                    )


def call(kernel, name, scalars, arrays, outs, unread=0):
    single = not isinstance(outs, (list, tuple))
    out = pl.pallas_call(
        kernel,
        in_specs=[spec(SM)] * len(scalars)
        + [spec(VM)] * (len(arrays) - unread)
        + [spec(pl.ANY)] * unread,
        out_specs=spec(VM) if single else [spec(VM)] * len(outs),
        out_shape=outs,
        compiler_params=params(name),
        name=name,
    )(*scalars, *arrays)
    return out


def local(
    state, source, sigma, stagger, a_theta, a_axial, a_radial, mode_order, mode_radial, mode_plane, gust, l_rows, r_cols
):
    nharm, two, nvar, ctheta, caxial, nradial = state.shape
    nhp, nmode = nharm * two, mode_order.shape[1]
    tdev, xdev = lax.axis_size("theta"), lax.axis_size("xr")
    nrad = 8
    block = (nhp, nvar, ctheta * caxial, nradial)
    u = state.reshape(block)
    src = source.reshape(block)
    sig = sigma.reshape(ctheta * caxial, nradial)
    place = jnp.stack([lax.axis_index("theta"), lax.axis_index("xr")]).astype(jnp.int32)

    def array(*shape):
        return jax.ShapeDtypeStruct(shape, jnp.float32)

    face = array(nhp, nvar, 8, nradial)
    packed = array(nhp + 1, nvar, 8, nradial)
    whole = array(*block)

    even_t = [(i, i ^ 1) for i in range(tdev)]
    odd_t = [(i, (i + 1) % tdev if i % 2 else (i - 1) % tdev) for i in range(tdev)]
    even_x = [(i, i ^ 1) for i in range(xdev)]
    odd_x = [(i, i + 1 if i % 2 else i - 1) for i in range(1, xdev - 1)]

    def swap(te, to, xe, xo):
        return (
            lax.ppermute(te, "theta", even_t),
            lax.ppermute(to, "theta", odd_t),
            lax.ppermute(xe, "xr", even_x),
            lax.ppermute(xo, "xr", odd_x),
        )

    coefs = (place, stagger, a_theta, a_axial, a_radial)
    faces = call(pack_kernel, "pack_faces", (place, stagger), (u, sig), [packed] * 2 + [face] * 2)
    faces = swap(*faces)
    tabs = call(
        functools.partial(table_kernel, tdev),
        "mode_tables",
        (place,),
        (mode_order, mode_radial),
        [array(nharm, 16, nmode)] * 2 + [array(nrad, nradial), array(nharm, nrad, nmode)],
    )

    def planes(after):
        return call(
            functools.partial(plane_kernel, tdev, xdev),
            "plane_part",
            (*coefs, l_rows),
            (u, src, sig, faces[0], faces[1], mode_plane, *tabs, after, faces[2], faces[3]),
            array(tdev, 8, nmode),
            3,
        )

    def first_step(after):
        return call(first_kernel, "first_step", coefs, (u, src, sig, *faces, after), [whole] + [face] * 4, 1)

    if planes_first:
        part = planes(sigma)
        first, *faces2 = first_step(part)
    else:
        first, *faces2 = first_step(sigma)
        part = planes(first)
    got = lax.all_to_all(part, "theta", 0, 0, tiled=True)
    faces2 = swap(*faces2)
    second = call(second_kernel, "second_step", coefs, (first, u, src, sig, *faces2), whole)
    amp = call(functools.partial(share_kernel, xdev), "share_amplitudes", (), (got,), array(xdev, 8, nmode))
    amp = lax.all_to_all(amp, "xr", 0, 0, tiled=True)
    fields = call(
        functools.partial(correct_kernel, tdev, xdev),
        "correct_planes",
        (place, r_cols),
        (got, gust, second, mode_plane, *tabs),
        whole,
    )
    amplitudes = call(finish_kernel, "finish_amplitudes", (), (amp, mode_plane), array(nharm, 2, two, nmode))
    return fields.reshape(state.shape), amplitudes


def solution(mesh):
    placed = (
        P(None, None, None, "theta", "xr", None),
        P(None, None, None, "theta", "xr", None),
        P("theta", "xr", None),
        P("theta"),
        P(),
        P(),
        P(),
        P(),
        P(),
        P(),
        P(),
        P(),
        P(),
    )
    return jax.shard_map(
        local,
        mesh=mesh,
        in_specs=placed,
        out_specs=(P(None, None, None, "theta", "xr", None), P()),
        check_vma=False,
    )
```

time: 67.7 us -> 56.5 us (0.83)
  blocking collectives: 16.1 us -> 0 us
  waiting for transfers between devices: 13.1 us -> 2.08 us
  Pallas kernels: 8.73 us -> 16.4 us
  starting transfers between devices: 25.3 us -> 32.7 us
    all_to_all x1 -> x0, blocking collectives: 16.1 us -> none  [local(): got = lax.all_to_all(part, 'theta', 0, 0, tiled=True)]
    pallas_call x4 -> x8, Pallas kernels: 8.73 us -> 16.4 us  [call(): pl.pallas_call(kernel, in_specs=[spec(SM)] * len(scalars) + [spec(VM)] *...]
    all_to_all x1, waiting for transfers between devices: 4.84 us -> 0.01 us  [local(): amp = lax.all_to_all(amp, 'xr', 0, 0, tiled=True)]
    ppermute x2, waiting for transfers between devices: 6.4 us -> 2.06 us  [swap(): lax.ppermute(xo, 'xr', odd_x)]
    ppermute x2, starting transfers between devices: 8.62 us -> 12.9 us  [swap(): lax.ppermute(to, 'theta', odd_t)]
    all_to_all x0 -> x1, starting transfers between devices: none -> 4.13 us  [local(): got = lax.all_to_all(part, 'theta', 0, 0, tiled=True)]
    ppermute x2, waiting for transfers between devices: 1.89 us -> 0.01 us  [swap(): lax.ppermute(to, 'theta', odd_t)]
    all_to_all x1, starting transfers between devices: 4.89 us -> 3.92 us  [local(): amp = lax.all_to_all(amp, 'xr', 0, 0, tiled=True)]
  transfers between devices with their start and end apart: 9 -> 10, of which waited for: 4 -> 1; matrix products, arithmetic and copies ran while one was open for 0% -> 1% of each run, Pallas kernels for 0% -> 20%
where the time goes in v2:
time: 56.5 us; the launch traced here: 55.9 us
  starting transfers between devices  32.7 us (58%)
  Pallas kernels  16.4 us (29%)
  local copies, waits for them, and re-layouts  3.18 us (6%)
  waiting for transfers between devices  2.08 us (4%)
  between operations  0.9 us (2%)
  other arithmetic  0.65 us (1%)
    pallas_call x8, Pallas kernels, call(): pl.pallas_call(kernel, in_specs=[spec(SM)] * len(scalars) + [spec(VM)] *...  16.4 us
    ppermute x2, starting transfers between devices, swap(): lax.ppermute(to, 'theta', odd_t)  12.9 us
    ppermute x2, starting transfers between devices, swap(): lax.ppermute(xo, 'xr', odd_x)  9.89 us
    all_to_all x1, starting transfers between devices, local(): got = lax.all_to_all(part, 'theta', 0, 0, tiled=True)  4.13 us
    all_to_all x1, starting transfers between devices, local(): amp = lax.all_to_all(amp, 'xr', 0, 0, tiled=True)  3.92 us
    unnamed x43, local copies, waits for them, and re-layouts  3.18 us
    ppermute x2, waiting for transfers between devices, swap(): lax.ppermute(xo, 'xr', odd_x)  2.06 us
    ppermute x2, starting transfers between devices, swap(): lax.ppermute(xe, 'xr', even_x)  1.58 us
  transfers between devices with their start and end apart: 10, of which 1 were waited for; matrix products, arithmetic and copies ran while one was open for 1% of the time, Pallas kernels for 20%

profile of v2, /device:TPU:2, one launch (start us, length us, event | category | flops | bytes accessed | tf_op | source)
XLA Modules:
  0.0 55.9 jit_solution(14493369165054416469)
XLA Ops:
  0.6 0.7 %pad_add_fusion.place = s32[2]{0:T(128)} fusion(s32[1]{0:T(128)} %bitcast.1, s32[1]{0:T(128)} %bitcast), kind=kLoop, calls=%fused_computation | loop fusion | flops 2 | bytes 16 | tf_op jit(solution)/shard_map/stack | solution.py:411
  1.3 0.0 copy-start.20
  1.3 2.1 %pack_faces.1 = (f32[7,5,8,128]{3,2,1,0:T(8,128)}, f32[7,5,8,128]{3,2,1,0:T(8,128)}, f32[6,5,8,128]{3,2,1,0:T(8,128)}, f32[6,5,8,128]{3,2,1,0:T(8,128)}) custom-call(s32[2]{0:T(128)} %pad_add_fusion.place, s32[2]{0:T(128)} %stagger.7, f32[6,5,64,128]{3,2,1,0:T(8,128)} %bitcast.6, f32[64,128]{1,0:T(8,128)} %bitcast.13), custom_call_target="tpu_custom_call" | custom-call | tf_op jit(solution)/shard_map/pack_faces/pallas_call | solution.py:387
  3.4 0.0 collective-permute-start
  3.4 7.5 %collective-permute-start.1 = (f32[7,5,8,128]{3,2,1,0:T(8,128)}, f32[7,5,8,128]{3,2,1,0:T(8,128)S(1)}, u32[]{:S(2)}, u32[]{:S(2)}) collective-permute-start(f32[7,5,8,128]{3,2,1,0:T(8,128)} %get-tuple-element.16), channel_id=1, source_target_pairs={{0,248},{8,16},{16,8},{24,32},{32,24},{40,48},{48,40},{56,64},{64,... | collective-permute-start | bytes 430088 | tf_op jit(solution)/shard_map/ppermute | solution.py:428
  10.9 1.6 %collective-permute-start.2 = (f32[6,5,8,128]{3,2,1,0:T(8,128)}, f32[6,5,8,128]{3,2,1,0:T(8,128)S(1)}, u32[]{:S(2)}, u32[]{:S(2)}) collective-permute-start(f32[6,5,8,128]{3,2,1,0:T(8,128)} %get-tuple-element.21), channel_id=1, source_target_pairs={{0,1},{1,0},{2,3},{3,2},{4,5},{5,4},{6,7},{7,6},{8,9},{9,8},{10,11... | collective-permute-start | bytes 368648 | tf_op jit(solution)/shard_map/ppermute | solution.py:429
  12.5 4.9 %collective-permute-start.3 = (f32[6,5,8,128]{3,2,1,0:T(8,128)}, f32[6,5,8,128]{3,2,1,0:T(8,128)S(1)}, u32[]{:S(2)}, u32[]{:S(2)}) collective-permute-start(f32[6,5,8,128]{3,2,1,0:T(8,128)} %get-tuple-element.22), channel_id=1, source_target_pairs={{1,2},{2,1},{3,4},{4,3},{5,6},{6,5},{9,10},{10,9},{11,12},{12,11},... | collective-permute-start | bytes 368648 | tf_op jit(solution)/shard_map/ppermute | solution.py:430
  17.5 0.0 copy-done.20
  17.5 0.6 %copy.15.a_theta = f32[4,5,5]{2,1,0:T(8,128)} copy(f32[4,5,5]{2,0,1:T(4,128)S(1)} %copy-done.20) | data formatting | bytes 800 | tf_op args[4]
  18.1 1.4 %mode_tables.1 = (f32[3,16,128]{2,1,0:T(8,128)}, f32[3,16,128]{2,1,0:T(8,128)}, f32[8,128]{1,0:T(8,128)}, f32[3,8,128]{2,1,0:T(8,128)}) custom-call(s32[2]{0:T(128)} %pad_add_fusion.place, s32[3,128]{1,0:T(4,128)} %order.1, s32[3,128]{1,0:T(4,128)} %radial.1), custom_call_target="tpu_custom_call" | custom-call | tf_op jit(solution)/shard_map/mode_tables/pallas_call | solution.py:387
  19.5 0.0 collective-permute-done.2.after2.xe
  19.5 0.0 copy-start.18
  19.5 2.1 %collective-permute-done.3.after3.xo = f32[6,5,8,128]{3,2,1,0:T(8,128)S(1)} collective-permute-done((f32[6,5,8,128]{3,2,1,0:T(8,128)}, f32[6,5,8,128]{3,2,1,0:T(8,128)S(1)}, u32[]{:S(2)}, u32[]{:S(2)}) %collective-permute-start.3) | collective-permute-done | bytes 122912 | tf_op jit(solution)/shard_map/ppermute | solution.py:430
  21.6 0.0 copy-start.19
  21.6 0.0 collective-permute-done.te
  21.6 0.0 copy-start.16
  21.6 0.0 collective-permute-done.1.to
  21.6 0.0 copy-start.17
  21.6 0.0 copy-done.18
  21.6 0.6 %copy-done.19 = f32[6,5,8,128]{3,2,1,0:T(8,128)} copy-done((f32[6,5,8,128]{3,2,1,0:T(8,128)}, f32[6,5,8,128]{3,2,1,0:T(8,128)S(1)}, u32[]{:S(2)}) %copy-start.19) | copy-done | bytes 122904
  22.2 0.1 copy-done.16
  22.3 0.1 copy-done.17
  22.4 2.3 %plane_part.1.after = f32[32,8,128]{2,1,0:T(8,128)} custom-call(s32[2]{0:T(128)} %pad_add_fusion.place, s32[2]{0:T(128)} %stagger.7, f32[4,5,5]{2,1,0:T(8,128)} %copy.15.a_theta, f32[5,5]{1,0:T(8,128)} %a_axial.5, f32[5,5]{1,0:T(8,128)} %a_radial.5, f32[2,5]{1,0:T(2,128)} %l_rows.1, f32[6,5,64,128]{3,2,1,0:T(8,128)} %bitcast.7, f32[6,5,64,128]{3,2,1,0:T(8,128)} %bitcast.10, ...), custom_call_target="tpu_custom_call" | custom-call | tf_op jit(solution)/shard_map/plane_part/pallas_call | solution.py:387
  24.7 4.1 %all-to-all-start = ((f32[32,8,128]{2,1,0:T(8,128)}), f32[32,8,128]{2,1,0:T(8,128)S(1)}, u32[]{:S(2)}, u32[]{:S(2)}) async-start(f32[32,8,128]{2,1,0:T(8,128)} %plane_part.1.after), calls=%async_computation | async-start | bytes 262144 | tf_op jit(solution)/shard_map/all_to_all | solution.py:463
  28.8 0.0 copy-start
  28.8 0.0 copy-start.1
  28.8 4.9 %first_step.1 = (f32[6,5,64,128]{3,2,1,0:T(8,128)}, f32[6,5,8,128]{3,2,1,0:T(8,128)}, f32[6,5,8,128]{3,2,1,0:T(8,128)}, f32[6,5,8,128]{3,2,1,0:T(8,128)}, f32[6,5,8,128]{3,2,1,0:T(8,128)}) custom-call(s32[2]{0:T(128)} %pad_add_fusion.place, s32[2]{0:T(128)} %stagger.7, f32[4,5,5]{2,1,0:T(8,128)} %copy.15.a_theta, f32[5,5]{1,0:T(8,128)} %a_axial.5, ...), custom_call_target="tpu_custom_call" | custom-call | tf_op jit(solution)/shard_map/first_step/pallas_call | solution.py:387
  33.7 0.3 collective-permute-start.4
  33.9 5.3 %collective-permute-start.5 = (f32[6,5,8,128]{3,2,1,0:T(8,128)}, f32[6,5,8,128]{3,2,1,0:T(8,128)S(1)}, u32[]{:S(2)}, u32[]{:S(2)}) collective-permute-start(f32[6,5,8,128]{3,2,1,0:T(8,128)} %get-tuple-element.25), channel_id=1, source_target_pairs={{0,248},{8,16},{16,8},{24,32},{32,24},{40,48},{48,40},{56,64},{64,... | collective-permute-start | bytes 368648 | tf_op jit(solution)/shard_map/ppermute | solution.py:428
  39.3 0.0 collective-permute-start.6
  39.3 4.9 %collective-permute-start.7 = (f32[6,5,8,128]{3,2,1,0:T(8,128)}, f32[6,5,8,128]{3,2,1,0:T(8,128)S(1)}, u32[]{:S(2)}, u32[]{:S(2)}) collective-permute-start(f32[6,5,8,128]{3,2,1,0:T(8,128)} %get-tuple-element.27), channel_id=1, source_target_pairs={{1,2},{2,1},{3,4},{4,3},{5,6},{6,5},{9,10},{10,9},{11,12},{12,11},... | collective-permute-start | bytes 368648 | tf_op jit(solution)/shard_map/ppermute | solution.py:430
  44.2 0.0 all-to-all-done.got_ref
  44.2 0.6 %share_amplitudes.1 = f32[8,8,128]{2,1,0:T(8,128)} custom-call(f32[32,8,128]{2,1,0:T(8,128)S(1)} %all-to-all-done.got_ref), custom_call_target="tpu_custom_call" | custom-call | tf_op jit(solution)/shard_map/share_amplitudes/pallas_call | solution.py:387
  44.9 0.0 copy-start.3
  44.9 0.0 copy-start.4
  44.9 0.0 copy-start.8
  44.9 3.9 %all-to-all-start.1 = ((f32[8,8,128]{2,1,0:T(8,128)}), f32[8,8,128]{2,1,0:T(8,128)S(1)}, u32[]{:S(2)}, u32[]{:S(2)}) async-start(f32[8,8,128]{2,1,0:T(8,128)} %share_amplitudes.1), calls=%async_computation.1 | async-start | bytes 65536 | tf_op jit(solution)/shard_map/all_to_all | solution.py:467
  48.8 0.0 collective-permute-done.4.te
  48.8 0.0 collective-permute-done.5.to
  48.8 0.0 collective-permute-done.6.xe
  48.8 0.0 collective-permute-done.7.xo
  48.8 0.0 copy-done
  48.9 0.0 copy-done.1
  48.9 0.0 copy-done.3
  48.9 0.0 copy-done.4
  48.9 0.0 copy-done.8
  48.9 0.0 copy-done.9
  48.9 0.6 %copy-done.11 = s32[2]{0:T(128)S(1)} copy-done((s32[2]{0:T(128)S(1)}, s32[2]{0:T(128)}, u32[]{:S(2)}) %copy-start.11) | copy-done | bytes 32
  49.5 0.0 copy-done.13
  49.5 1.2 %copy-done.2 = f32[6,5,64,128]{3,2,1,0:T(8,128)S(1)} copy-done((f32[6,5,64,128]{3,2,1,0:T(8,128)S(1)}, f32[6,5,64,128]{3,2,1,0:T(8,128)}, u32[]{:S(2)}) %copy-start.2) | copy-done | bytes 983064
  50.7 0.0 copy-start.12
  50.7 0.0 copy-start.14
  50.7 0.0 copy-start.15
  50.7 2.9 %second_step.1.second_ref = f32[6,5,64,128]{3,2,1,0:T(8,128)S(1)} custom-call(s32[2]{0:T(128)S(1)} %copy-done.11, s32[2]{0:T(128)S(1)} %copy-done.13, f32[4,5,5]{2,1,0:T(8,128)S(1)} %copy-done.4, f32[5,5]{1,0:T(8,128)S(1)} %copy-done.8, f32[5,5]{1,0:T(8,128)S(1)} %copy-done.9, f32[6,5,64,128]{3,2,1,0:T(8,128)S(1)} %copy-done.2, ...), custom_call_target="tpu_custom_call" | custom-call | tf_op jit(solution)/shard_map/second_step/pallas_call | solution.py:387
  53.6 0.0 copy-done.5
  53.6 0.0 copy-done.6
  53.6 0.0 copy-done.7
  53.6 0.0 copy-done.10
  53.7 0.0 copy-done.12
  53.7 0.0 copy-done.14
  53.7 0.0 copy-done.15
  53.7 1.6 %correct_planes.1 = f32[6,5,64,128]{3,2,1,0:T(8,128)} custom-call(s32[2]{0:T(128)S(1)} %copy-done.11, f32[2,5]{1,0:T(2,128)S(1)} %copy-done.15, f32[32,8,128]{2,1,0:T(8,128)S(1)} %all-to-all-done.got_ref, f32[3,2,128]{2,1,0:T(2,128)S(1)} %copy-done.14, f32[6,5,64,128]{3,2,1,0:T(8,128)S(1)} %second_step.1.second_ref, s32[3,128]{1,0:T(4,128)S(1)} %copy-done.10, ...), custom_call_target="tpu_custom_call" | custom-call | tf_op jit(solution)/shard_map/correct_planes/pallas_call | solution.py:387
  55.2 0.0 all-to-all-done.1.got_ref
  55.3 0.6 %finish_amplitudes.1 = f32[3,2,2,128]{3,2,1,0:T(2,128)} custom-call(f32[8,8,128]{2,1,0:T(8,128)S(1)} %all-to-all-done.1.got_ref, s32[3,128]{1,0:T(4,128)S(1)} %copy-done.10), custom_call_target="tpu_custom_call" | custom-call | tf_op jit(solution)/shard_map/finish_amplitudes/pallas_call | solution.py:387
  (8 shorter events, 0.0 us)
Async XLA Ops:
  1.3 16.2 %copy-start.20 = (f32[4,5,5]{2,0,1:T(4,128)S(1)}, f32[4,5,5]{2,0,1:T(4,128)}, u32[]{:S(2)}) copy-start(f32[4,5,5]{2,0,1:T(4,128)} %param.17) | copy-start | bytes 1204
  3.4 18.2 %collective-permute-start = (f32[7,5,8,128]{3,2,1,0:T(8,128)}, f32[7,5,8,128]{3,2,1,0:T(8,128)S(1)}, u32[]{:S(2)}, u32[]{:S(2)}) collective-permute-start(f32[7,5,8,128]{3,2,1,0:T(8,128)} %get-tuple-element.15), channel_id=1, source_target_pairs={{0,8},{8,0},{16,24},{24,16},{32,40},{40,32},{48,56},{56,48},{64,72... | collective-permute-start | bytes 430088 | tf_op jit(solution)/shard_map/ppermute | solution.py:427
  3.4 18.2 %collective-permute-start.1 = (f32[7,5,8,128]{3,2,1,0:T(8,128)}, f32[7,5,8,128]{3,2,1,0:T(8,128)S(1)}, u32[]{:S(2)}, u32[]{:S(2)}) collective-permute-start(f32[7,5,8,128]{3,2,1,0:T(8,128)} %get-tuple-element.16), channel_id=1, source_target_pairs={{0,248},{8,16},{16,8},{24,32},{32,24},{40,48},{48,40},{56,64},{64,... | collective-permute-start | bytes 430088 | tf_op jit(solution)/shard_map/ppermute | solution.py:428
  10.9 8.6 %collective-permute-start.2 = (f32[6,5,8,128]{3,2,1,0:T(8,128)}, f32[6,5,8,128]{3,2,1,0:T(8,128)S(1)}, u32[]{:S(2)}, u32[]{:S(2)}) collective-permute-start(f32[6,5,8,128]{3,2,1,0:T(8,128)} %get-tuple-element.21), channel_id=1, source_target_pairs={{0,1},{1,0},{2,3},{3,2},{4,5},{5,4},{6,7},{7,6},{8,9},{9,8},{10,11... | collective-permute-start | bytes 368648 | tf_op jit(solution)/shard_map/ppermute | solution.py:429
  12.5 9.1 %collective-permute-start.3 = (f32[6,5,8,128]{3,2,1,0:T(8,128)}, f32[6,5,8,128]{3,2,1,0:T(8,128)S(1)}, u32[]{:S(2)}, u32[]{:S(2)}) collective-permute-start(f32[6,5,8,128]{3,2,1,0:T(8,128)} %get-tuple-element.22), channel_id=1, source_target_pairs={{1,2},{2,1},{3,4},{4,3},{5,6},{6,5},{9,10},{10,9},{11,12},{12,11},... | collective-permute-start | bytes 368648 | tf_op jit(solution)/shard_map/ppermute | solution.py:430
  19.5 2.1 %copy-start.18 = (f32[6,5,8,128]{3,2,1,0:T(8,128)}, f32[6,5,8,128]{3,2,1,0:T(8,128)S(1)}, u32[]{:S(2)}) copy-start(f32[6,5,8,128]{3,2,1,0:T(8,128)S(1)} %collective-permute-done.2.after2.xe) | copy-start | bytes 368644
  21.6 0.6 %copy-start.19 = (f32[6,5,8,128]{3,2,1,0:T(8,128)}, f32[6,5,8,128]{3,2,1,0:T(8,128)S(1)}, u32[]{:S(2)}) copy-start(f32[6,5,8,128]{3,2,1,0:T(8,128)S(1)} %collective-permute-done.3.after3.xo) | copy-start | bytes 368644
  21.6 0.7 %copy-start.16 = (f32[7,5,8,128]{3,2,1,0:T(8,128)}, f32[7,5,8,128]{3,2,1,0:T(8,128)S(1)}, u32[]{:S(2)}) copy-start(f32[7,5,8,128]{3,2,1,0:T(8,128)S(1)} %collective-permute-done.te) | copy-start | bytes 430084
  21.6 0.8 %copy-start.17 = (f32[7,5,8,128]{3,2,1,0:T(8,128)}, f32[7,5,8,128]{3,2,1,0:T(8,128)S(1)}, u32[]{:S(2)}) copy-start(f32[7,5,8,128]{3,2,1,0:T(8,128)S(1)} %collective-permute-done.1.to) | copy-start | bytes 430084
  24.7 19.6 %all-to-all-start = ((f32[32,8,128]{2,1,0:T(8,128)}), f32[32,8,128]{2,1,0:T(8,128)S(1)}, u32[]{:S(2)}, u32[]{:S(2)}) async-start(f32[32,8,128]{2,1,0:T(8,128)} %plane_part.1.after), calls=%async_computation | async-start | bytes 262144 | tf_op jit(solution)/shard_map/all_to_all | solution.py:463
  28.8 20.1 %copy-start = (f32[3,2,5,8,8,128]{5,4,3,2,1,0:T(8,128)S(1)}, f32[3,2,5,8,8,128]{5,4,3,2,1,0:T(8,128)}, u32[]{:S(2)}) copy-start(f32[3,2,5,8,8,128]{5,4,3,2,1,0:T(8,128)} %param.13) | copy-start | bytes 2949124
  28.8 20.1 %copy-start.1 = (f32[3,2,5,8,8,128]{5,4,3,2,1,0:T(8,128)S(1)}, f32[3,2,5,8,8,128]{5,4,3,2,1,0:T(8,128)}, u32[]{:S(2)}) copy-start(f32[3,2,5,8,8,128]{5,4,3,2,1,0:T(8,128)} %param.14) | copy-start | bytes 2949124
  33.7 15.1 %collective-permute-start.4 = (f32[6,5,8,128]{3,2,1,0:T(8,128)}, f32[6,5,8,128]{3,2,1,0:T(8,128)S(1)}, u32[]{:S(2)}, u32[]{:S(2)}) collective-permute-start(f32[6,5,8,128]{3,2,1,0:T(8,128)} %get-tuple-element.24), channel_id=1, source_target_pairs={{0,8},{8,0},{16,24},{24,16},{32,40},{40,32},{48,56},{56,48},{64,72... | collective-permute-start | bytes 368648 | tf_op jit(solution)/shard_map/ppermute | solution.py:427
  33.9 14.9 %collective-permute-start.5 = (f32[6,5,8,128]{3,2,1,0:T(8,128)}, f32[6,5,8,128]{3,2,1,0:T(8,128)S(1)}, u32[]{:S(2)}, u32[]{:S(2)}) collective-permute-start(f32[6,5,8,128]{3,2,1,0:T(8,128)} %get-tuple-element.25), channel_id=1, source_target_pairs={{0,248},{8,16},{16,8},{24,32},{32,24},{40,48},{48,40},{56,64},{64,... | collective-permute-start | bytes 368648 | tf_op jit(solution)/shard_map/ppermute | solution.py:428
  39.3 9.6 %collective-permute-start.6 = (f32[6,5,8,128]{3,2,1,0:T(8,128)}, f32[6,5,8,128]{3,2,1,0:T(8,128)S(1)}, u32[]{:S(2)}, u32[]{:S(2)}) collective-permute-start(f32[6,5,8,128]{3,2,1,0:T(8,128)} %get-tuple-element.26), channel_id=1, source_target_pairs={{0,1},{1,0},{2,3},{3,2},{4,5},{5,4},{6,7},{7,6},{8,9},{9,8},{10,11... | collective-permute-start | bytes 368648 | tf_op jit(solution)/shard_map/ppermute | solution.py:429
  39.3 9.6 %collective-permute-start.7 = (f32[6,5,8,128]{3,2,1,0:T(8,128)}, f32[6,5,8,128]{3,2,1,0:T(8,128)S(1)}, u32[]{:S(2)}, u32[]{:S(2)}) collective-permute-start(f32[6,5,8,128]{3,2,1,0:T(8,128)} %get-tuple-element.27), channel_id=1, source_target_pairs={{1,2},{2,1},{3,4},{4,3},{5,6},{6,5},{9,10},{10,9},{11,12},{12,11},... | collective-permute-start | bytes 368648 | tf_op jit(solution)/shard_map/ppermute | solution.py:430
  44.9 4.0 %copy-start.3 = (f32[8,8,128]{2,1,0:T(8,128)S(1)}, f32[8,8,128]{2,1,0:T(8,128)}, u32[]{:S(2)}) copy-start(f32[8,8,128]{2,1,0:T(8,128)} %after.1) | copy-start | bytes 98308
  44.9 4.0 %copy-start.4 = (f32[4,5,5]{2,1,0:T(8,128)S(1)}, f32[4,5,5]{2,1,0:T(8,128)}, u32[]{:S(2)}) copy-start(f32[4,5,5]{2,1,0:T(8,128)} %copy.15.a_theta) | copy-start | bytes 1204
  44.9 4.0 %copy-start.8 = (f32[5,5]{1,0:T(8,128)S(1)}, f32[5,5]{1,0:T(8,128)}, u32[]{:S(2)}) copy-start(f32[5,5]{1,0:T(8,128)} %a_axial.5) | copy-start | bytes 304
  44.9 4.0 %copy-start.9 = (f32[5,5]{1,0:T(8,128)S(1)}, f32[5,5]{1,0:T(8,128)}, u32[]{:S(2)}) copy-start(f32[5,5]{1,0:T(8,128)} %a_radial.5) | copy-start | bytes 304
  44.9 10.4 %all-to-all-start.1 = ((f32[8,8,128]{2,1,0:T(8,128)}), f32[8,8,128]{2,1,0:T(8,128)S(1)}, u32[]{:S(2)}, u32[]{:S(2)}) async-start(f32[8,8,128]{2,1,0:T(8,128)} %share_amplitudes.1), calls=%async_computation.1 | async-start | bytes 65536 | tf_op jit(solution)/shard_map/all_to_all | solution.py:467
  48.8 0.7 %copy-start.11 = (s32[2]{0:T(128)S(1)}, s32[2]{0:T(128)}, u32[]{:S(2)}) copy-start(s32[2]{0:T(128)} %pad_add_fusion.place) | copy-start | bytes 28
  48.8 0.7 %copy-start.13 = (s32[2]{0:T(128)S(1)}, s32[2]{0:T(128)}, u32[]{:S(2)}) copy-start(s32[2]{0:T(128)} %stagger.7) | copy-start | bytes 28
  49.5 1.2 %copy-start.2 = (f32[6,5,64,128]{3,2,1,0:T(8,128)S(1)}, f32[6,5,64,128]{3,2,1,0:T(8,128)}, u32[]{:S(2)}) copy-start(f32[6,5,64,128]{3,2,1,0:T(8,128)} %get-tuple-element.23.u_ref) | copy-start | bytes 2949124
  50.7 2.9 %copy-start.5 = (f32[3,16,128]{2,1,0:T(8,128)S(1)}, f32[3,16,128]{2,1,0:T(8,128)}, u32[]{:S(2)}) copy-start(f32[3,16,128]{2,1,0:T(8,128)} %get-tuple-element.17.cos_ref) | copy-start | bytes 73732
  50.7 2.9 %copy-start.6 = (f32[3,16,128]{2,1,0:T(8,128)S(1)}, f32[3,16,128]{2,1,0:T(8,128)}, u32[]{:S(2)}) copy-start(f32[3,16,128]{2,1,0:T(8,128)} %get-tuple-element.18.sin_ref) | copy-start | bytes 73732
  50.7 3.0 %copy-start.7 = (f32[3,8,128]{2,1,0:T(8,128)S(1)}, f32[3,8,128]{2,1,0:T(8,128)}, u32[]{:S(2)}) copy-start(f32[3,8,128]{2,1,0:T(8,128)} %get-tuple-element.20.pick_ref) | copy-start | bytes 36868
  50.7 3.0 %copy-start.10 = (s32[3,128]{1,0:T(4,128)S(1)}, s32[3,128]{1,0:T(4,128)}, u32[]{:S(2)}) copy-start(s32[3,128]{1,0:T(4,128)} %plane.5) | copy-start | bytes 4612
  50.7 3.0 %copy-start.12 = (f32[8,128]{1,0:T(8,128)S(1)}, f32[8,128]{1,0:T(8,128)}, u32[]{:S(2)}) copy-start(f32[8,128]{1,0:T(8,128)} %get-tuple-element.19.wave_ref) | copy-start | bytes 12292
  50.7 3.0 %copy-start.14 = (f32[3,2,128]{2,1,0:T(2,128)S(1)}, f32[3,2,128]{2,1,0:T(2,128)}, u32[]{:S(2)}) copy-start(f32[3,2,128]{2,1,0:T(2,128)} %gust.1) | copy-start | bytes 9220
  50.7 3.0 %copy-start.15 = (f32[2,5]{1,0:T(2,128)S(1)}, f32[2,5]{1,0:T(2,128)}, u32[]{:S(2)}) copy-start(f32[2,5]{1,0:T(2,128)} %r_cols.1) | copy-start | bytes 124

commit v3 on v2

--- a/solution.py
+++ b/solution.py
@@ -15,7 +15,11 @@
 VM = pltpu.VMEM
 SM = pltpu.SMEM
 planes_first = True
-wide = ("pack_faces", "plane_part", "mode_tables", "first_step")
+wide = ("pack_faces", "plane_part", "mode_tables", "first_step", "second_step")
+
+
+def where():
+    return lax.axis_index("theta"), lax.axis_index("xr")
 
 
 def spec(space):
@@ -40,7 +44,8 @@
                 out_ref[i, v] = u_ref[i, v, pl.ds(row * 7, 8, stride=8), :]
 
 
-def pack_kernel(place, stagger, u_ref, sig_ref, te_ref, to_ref, xe_ref, xo_ref):
+def pack_kernel(stagger, u_ref, sig_ref, te_ref, to_ref, xe_ref, xo_ref):
+    place = where()
     write_faces(place, u_ref, te_ref, to_ref, xe_ref, xo_ref)
     nhp = u_ref.shape[0]
     nr = u_ref.shape[3]
@@ -108,20 +113,15 @@
             out_ref[:, v, tile, :] = base_ref[:, v, tile, :] - scaled * acc[v]
 
 
-def first_kernel(
-    place, stagger, a_theta, a_axial, a_radial, u_ref, src_ref, sig_ref, te, to, xe, xo, after, out_ref, te2, to2, xe2, xo2
+def first_kernel(stagger, a_theta, a_axial, a_radial, u_ref, src_ref, sig_ref, te, to, xe, xo, after, out_ref, te2, to2, xe2, xo2
 ):
+    place = where()
     step(0.5, place, stagger, a_theta, a_axial, a_radial, u_ref, u_ref, src_ref, sig_ref, te, to, xe, xo, out_ref)
     write_faces(place, out_ref, te2, to2, xe2, xo2)
 
 
-def second_kernel(
-    place, stagger, a_theta, a_axial, a_radial, u_ref, base_ref, src_ref, sig_ref, te, to, xe, xo, out_ref
-):
-    step(1.0, place, stagger, a_theta, a_axial, a_radial, u_ref, base_ref, src_ref, sig_ref, te, to, xe, xo, out_ref)
-
-
-def table_kernel(tdevices, place, order, radial, cos_ref, sin_ref, wave_ref, pick_ref):
+def table_kernel(tdevices, order, radial, cos_ref, sin_ref, wave_ref, pick_ref):
+    place = where()
     nharm, nmode = order.shape
     tcells = 8
     total = tcells * tdevices
@@ -283,7 +283,6 @@
 def plane_kernel(
     tdevices,
     xdevices,
-    place,
     stagger,
     a_theta,
     a_axial,
@@ -304,6 +303,7 @@
     after3,
     part_ref,
 ):
+    place = where()
     nhp = u_ref.shape[0]
     last = (place[1] == xdevices - 1).astype(jnp.int32)
     holds = jnp.logical_or(place[1] == 0, place[1] == xdevices - 1)
@@ -340,14 +340,24 @@
             out_ref[h, b] = jnp.where(plane[h : h + 1, :] == b, amp[2 * h : 2 * h + 2], 0.0)
 
 
-def correct_kernel(
+def second_kernel(
     tdevices,
     xdevices,
-    place,
+    stagger,
+    a_theta,
+    a_axial,
+    a_radial,
     r_cols,
+    u_ref,
+    base_ref,
+    src_ref,
+    sig_ref,
+    te,
+    to,
+    xe,
+    xo,
     got_ref,
     gust,
-    second_ref,
     plane,
     cos_ref,
     sin_ref,
@@ -355,12 +365,13 @@
     pick_ref,
     out_ref,
 ):
+    place = where()
+    step(1.0, place, stagger, a_theta, a_axial, a_radial, u_ref, base_ref, src_ref, sig_ref, te, to, xe, xo, out_ref)
     nhp, nvar, rows, nr = out_ref.shape
     nharm, nmode = plane.shape
     scale = 1.0 / math.sqrt(8 * tdevices * nr)
     last = (place[1] == xdevices - 1).astype(jnp.int32)
     holds = jnp.logical_or(place[1] == 0, place[1] == xdevices - 1)
-    out_ref[...] = second_ref[...]
 
     @pl.when(holds)
     def _():
@@ -378,7 +389,7 @@
                 for v in range(nvar):
                     at = pl.ds(last * 7, 8, stride=8)
                     out_ref[2 * h + p, v, at, :] = (
-                        second_ref[2 * h + p, v, at, :] - r_cols[last, v] * q[p * 8 : (p + 1) * 8]
+                        out_ref[2 * h + p, v, at, :] - r_cols[last, v] * q[p * 8 : (p + 1) * 8]
                     )
 
 
@@ -408,7 +419,6 @@
     u = state.reshape(block)
     src = source.reshape(block)
     sig = sigma.reshape(ctheta * caxial, nradial)
-    place = jnp.stack([lax.axis_index("theta"), lax.axis_index("xr")]).astype(jnp.int32)
 
     def array(*shape):
         return jax.ShapeDtypeStruct(shape, jnp.float32)
@@ -430,13 +440,13 @@
             lax.ppermute(xo, "xr", odd_x),
         )
 
-    coefs = (place, stagger, a_theta, a_axial, a_radial)
-    faces = call(pack_kernel, "pack_faces", (place, stagger), (u, sig), [packed] * 2 + [face] * 2)
+    coefs = (stagger, a_theta, a_axial, a_radial)
+    faces = call(pack_kernel, "pack_faces", (stagger,), (u, sig), [packed] * 2 + [face] * 2)
     faces = swap(*faces)
     tabs = call(
         functools.partial(table_kernel, tdev),
         "mode_tables",
-        (place,),
+        (),
         (mode_order, mode_radial),
         [array(nharm, 16, nmode)] * 2 + [array(nrad, nradial), array(nharm, nrad, nmode)],
     )
@@ -462,14 +472,13 @@
         part = planes(first)
     got = lax.all_to_all(part, "theta", 0, 0, tiled=True)
     faces2 = swap(*faces2)
-    second = call(second_kernel, "second_step", coefs, (first, u, src, sig, *faces2), whole)
     amp = call(functools.partial(share_kernel, xdev), "share_amplitudes", (), (got,), array(xdev, 8, nmode))
     amp = lax.all_to_all(amp, "xr", 0, 0, tiled=True)
     fields = call(
-        functools.partial(correct_kernel, tdev, xdev),
-        "correct_planes",
-        (place, r_cols),
-        (got, gust, second, mode_plane, *tabs),
+        functools.partial(second_kernel, tdev, xdev),
+        "second_step",
+        (*coefs, r_cols),
+        (first, u, src, sig, *faces2, got, gust, mode_plane, *tabs),
         whole,
     )
     amplitudes = call(finish_kernel, "finish_amplitudes", (), (amp, mode_plane), array(nharm, 2, two, nmode))

time: 56.5 us -> 54.7 us (0.968)
  local copies, waits for them, and re-layouts: 3.18 us -> 2.05 us
  other arithmetic: 0.65 us -> 0 us
    unnamed x43 -> x23, local copies, waits for them, and re-layouts: 3.18 us -> 2.05 us
    another operation x1 -> x0, other arithmetic: 0.65 us -> none  [local(): jnp.stack([lax.axis_index('theta'), lax.axis_index('xr')]).astype(jnp.int32)]
    pallas_call x8 -> x7, Pallas kernels: 16.4 us -> 16.7 us  [call(): pl.pallas_call(kernel, in_specs=[spec(SM)] * len(scalars) + [spec(VM)] *...]
  transfers between devices with their start and end apart: 10 -> 10, of which waited for: 1 -> 1; matrix products, arithmetic and copies ran while one was open for 1% -> 1% of each run, Pallas kernels for 20% -> 22%
where the time goes in v3:
time: 54.7 us; the launch traced here: 54.2 us
  starting transfers between devices  32.5 us (59%)
  Pallas kernels  16.7 us (31%)
  waiting for transfers between devices  2.09 us (4%)
  local copies, waits for them, and re-layouts  2.05 us (4%)
  between operations  0.79 us (1%)
    pallas_call x7, Pallas kernels, call(): pl.pallas_call(kernel, in_specs=[spec(SM)] * len(scalars) + [spec(VM)] *...  16.7 us
    ppermute x2, starting transfers between devices, swap(): lax.ppermute(to, 'theta', odd_t)  12.9 us
    ppermute x2, starting transfers between devices, swap(): lax.ppermute(xo, 'xr', odd_x)  9.89 us
    all_to_all x1, starting transfers between devices, local(): got = lax.all_to_all(part, 'theta', 0, 0, tiled=True)  4.11 us
    all_to_all x1, starting transfers between devices, local(): amp = lax.all_to_all(amp, 'xr', 0, 0, tiled=True)  3.78 us
    ppermute x2, waiting for transfers between devices, swap(): lax.ppermute(xo, 'xr', odd_x)  2.07 us
    unnamed x23, local copies, waits for them, and re-layouts  2.05 us
    ppermute x2, starting transfers between devices, swap(): lax.ppermute(xe, 'xr', even_x)  1.58 us
  transfers between devices with their start and end apart: 10, of which 1 were waited for; matrix products, arithmetic and copies ran while one was open for 1% of the time, Pallas kernels for 22%

profile of v3, /device:TPU:2, one launch (start us, length us, event | category | flops | bytes accessed | tf_op | source)
XLA Modules:
  0.0 54.2 jit_solution(3886064127001068322)
XLA Ops:
  0.6 0.0 copy-start.10
  0.6 2.1 %pack_faces.1 = (f32[7,5,8,128]{3,2,1,0:T(8,128)}, f32[7,5,8,128]{3,2,1,0:T(8,128)}, f32[6,5,8,128]{3,2,1,0:T(8,128)}, f32[6,5,8,128]{3,2,1,0:T(8,128)}) custom-call(s32[2]{0:T(128)} %stagger.7, f32[6,5,64,128]{3,2,1,0:T(8,128)} %bitcast.4, f32[64,128]{1,0:T(8,128)} %bitcast.12), custom_call_target="tpu_custom_call" | custom-call | tf_op jit(solution)/shard_map/pack_faces/pallas_call | solution.py:398
  2.7 0.0 collective-permute-start
  2.8 7.5 %collective-permute-start.1 = (f32[7,5,8,128]{3,2,1,0:T(8,128)}, f32[7,5,8,128]{3,2,1,0:T(8,128)S(1)}, u32[]{:S(2)}, u32[]{:S(2)}) collective-permute-start(f32[7,5,8,128]{3,2,1,0:T(8,128)} %get-tuple-element.16), channel_id=1, source_target_pairs={{0,248},{8,16},{16,8},{24,32},{32,24},{40,48},{48,40},{56,64},{64,... | collective-permute-start | bytes 430088 | tf_op jit(solution)/shard_map/ppermute | solution.py:438
  10.3 1.6 %collective-permute-start.2 = (f32[6,5,8,128]{3,2,1,0:T(8,128)}, f32[6,5,8,128]{3,2,1,0:T(8,128)S(1)}, u32[]{:S(2)}, u32[]{:S(2)}) collective-permute-start(f32[6,5,8,128]{3,2,1,0:T(8,128)} %get-tuple-element.17), channel_id=1, source_target_pairs={{0,1},{1,0},{2,3},{3,2},{4,5},{5,4},{6,7},{7,6},{8,9},{9,8},{10,11... | collective-permute-start | bytes 368648 | tf_op jit(solution)/shard_map/ppermute | solution.py:439
  11.9 4.9 %collective-permute-start.3 = (f32[6,5,8,128]{3,2,1,0:T(8,128)}, f32[6,5,8,128]{3,2,1,0:T(8,128)S(1)}, u32[]{:S(2)}, u32[]{:S(2)}) collective-permute-start(f32[6,5,8,128]{3,2,1,0:T(8,128)} %get-tuple-element.18), channel_id=1, source_target_pairs={{1,2},{2,1},{3,4},{4,3},{5,6},{6,5},{9,10},{10,9},{11,12},{12,11},... | collective-permute-start | bytes 368648 | tf_op jit(solution)/shard_map/ppermute | solution.py:440
  16.8 0.0 copy-done.10
  16.8 0.6 %copy.17.a_theta = f32[4,5,5]{2,1,0:T(8,128)} copy(f32[4,5,5]{2,0,1:T(4,128)S(1)} %copy-done.10) | data formatting | bytes 800 | tf_op args[4]
  17.4 1.4 %mode_tables.1 = (f32[3,16,128]{2,1,0:T(8,128)}, f32[3,16,128]{2,1,0:T(8,128)}, f32[8,128]{1,0:T(8,128)}, f32[3,8,128]{2,1,0:T(8,128)}) custom-call(s32[3,128]{1,0:T(4,128)} %order.1, s32[3,128]{1,0:T(4,128)} %radial.1), custom_call_target="tpu_custom_call" | custom-call | tf_op jit(solution)/shard_map/mode_tables/pallas_call | solution.py:398
  18.9 0.0 collective-permute-done.2.after2.xe
  18.9 0.0 copy-start.4
  18.9 2.1 %collective-permute-done.3.after3.xo = f32[6,5,8,128]{3,2,1,0:T(8,128)S(1)} collective-permute-done((f32[6,5,8,128]{3,2,1,0:T(8,128)}, f32[6,5,8,128]{3,2,1,0:T(8,128)S(1)}, u32[]{:S(2)}, u32[]{:S(2)}) %collective-permute-start.3) | collective-permute-done | bytes 122912 | tf_op jit(solution)/shard_map/ppermute | solution.py:440
  20.9 0.0 copy-start.5
  20.9 0.0 collective-permute-done.te
  20.9 0.0 copy-start.2
  20.9 0.0 collective-permute-done.1.to
  21.0 0.0 copy-start.3
  21.0 0.0 copy-done.4
  21.0 0.6 %copy-done.5 = f32[6,5,8,128]{3,2,1,0:T(8,128)} copy-done((f32[6,5,8,128]{3,2,1,0:T(8,128)}, f32[6,5,8,128]{3,2,1,0:T(8,128)S(1)}, u32[]{:S(2)}) %copy-start.5) | copy-done | bytes 122904
  21.6 0.1 copy-done.2
  21.6 0.0 copy-done.3
  21.7 2.3 %plane_part.1.after = f32[32,8,128]{2,1,0:T(8,128)} custom-call(s32[2]{0:T(128)} %stagger.7, f32[4,5,5]{2,1,0:T(8,128)} %copy.17.a_theta, f32[5,5]{1,0:T(8,128)} %a_axial.5, f32[5,5]{1,0:T(8,128)} %a_radial.5, f32[2,5]{1,0:T(2,128)} %l_rows.1, f32[6,5,64,128]{3,2,1,0:T(8,128)} %bitcast.5, f32[6,5,64,128]{3,2,1,0:T(8,128)} %bitcast.8, f32[64,128]{1,0:T(8,128)} %bitcast.13, ...), custom_call_target="tpu_custom_call" | custom-call | tf_op jit(solution)/shard_map/plane_part/pallas_call | solution.py:398
  24.0 4.1 %all-to-all-start = ((f32[32,8,128]{2,1,0:T(8,128)}), f32[32,8,128]{2,1,0:T(8,128)S(1)}, u32[]{:S(2)}, u32[]{:S(2)}) async-start(f32[32,8,128]{2,1,0:T(8,128)} %plane_part.1.after), calls=%async_computation | async-start | bytes 262144 | tf_op jit(solution)/shard_map/all_to_all | solution.py:473
  28.1 4.8 %first_step.1 = (f32[6,5,64,128]{3,2,1,0:T(8,128)}, f32[6,5,8,128]{3,2,1,0:T(8,128)}, f32[6,5,8,128]{3,2,1,0:T(8,128)}, f32[6,5,8,128]{3,2,1,0:T(8,128)}, f32[6,5,8,128]{3,2,1,0:T(8,128)}) custom-call(s32[2]{0:T(128)} %stagger.7, f32[4,5,5]{2,1,0:T(8,128)} %copy.17.a_theta, f32[5,5]{1,0:T(8,128)} %a_axial.5, f32[5,5]{1,0:T(8,128)} %a_radial.5, ...), custom_call_target="tpu_custom_call" | custom-call | tf_op jit(solution)/shard_map/first_step/pallas_call | solution.py:398
  32.8 0.3 collective-permute-start.4
  33.1 5.3 %collective-permute-start.5 = (f32[6,5,8,128]{3,2,1,0:T(8,128)}, f32[6,5,8,128]{3,2,1,0:T(8,128)S(1)}, u32[]{:S(2)}, u32[]{:S(2)}) collective-permute-start(f32[6,5,8,128]{3,2,1,0:T(8,128)} %get-tuple-element.25), channel_id=1, source_target_pairs={{0,248},{8,16},{16,8},{24,32},{32,24},{40,48},{48,40},{56,64},{64,... | collective-permute-start | bytes 368648 | tf_op jit(solution)/shard_map/ppermute | solution.py:438
  38.4 0.0 collective-permute-start.6
  38.5 4.9 %collective-permute-start.7 = (f32[6,5,8,128]{3,2,1,0:T(8,128)}, f32[6,5,8,128]{3,2,1,0:T(8,128)S(1)}, u32[]{:S(2)}, u32[]{:S(2)}) collective-permute-start(f32[6,5,8,128]{3,2,1,0:T(8,128)} %get-tuple-element.27), channel_id=1, source_target_pairs={{1,2},{2,1},{3,4},{4,3},{5,6},{6,5},{9,10},{10,9},{11,12},{12,11},... | collective-permute-start | bytes 368648 | tf_op jit(solution)/shard_map/ppermute | solution.py:440
  43.4 0.0 all-to-all-done.got_ref
  43.4 0.0 copy-start
  43.4 0.7 %share_amplitudes.1 = f32[8,8,128]{2,1,0:T(8,128)} custom-call(f32[32,8,128]{2,1,0:T(8,128)S(1)} %all-to-all-done.got_ref), custom_call_target="tpu_custom_call" | custom-call | tf_op jit(solution)/shard_map/share_amplitudes/pallas_call | solution.py:398
  44.1 3.8 %all-to-all-start.1 = ((f32[8,8,128]{2,1,0:T(8,128)}), f32[8,8,128]{2,1,0:T(8,128)S(1)}, u32[]{:S(2)}, u32[]{:S(2)}) async-start(f32[8,8,128]{2,1,0:T(8,128)} %share_amplitudes.1), calls=%async_computation.1 | async-start | bytes 65536 | tf_op jit(solution)/shard_map/all_to_all | solution.py:476
  47.9 0.0 collective-permute-done.4.te
  47.9 0.0 copy-start.6
  47.9 0.0 collective-permute-done.5.to
  47.9 0.0 copy-start.7
  47.9 0.0 collective-permute-done.6.xe
  47.9 0.0 copy-start.8
  47.9 0.0 collective-permute-done.7.xo
  47.9 0.0 copy-start.9
  47.9 0.0 copy-done
  47.9 0.6 %copy-done.6 = f32[6,5,8,128]{3,2,1,0:T(8,128)} copy-done((f32[6,5,8,128]{3,2,1,0:T(8,128)}, f32[6,5,8,128]{3,2,1,0:T(8,128)S(1)}, u32[]{:S(2)}) %copy-start.6) | copy-done | bytes 122904
  48.5 0.1 copy-done.7
  48.6 0.0 copy-done.8
  48.6 0.0 copy-done.9
  48.7 0.0 copy-start.1
  48.7 4.9 %second_step.1 = f32[6,5,64,128]{3,2,1,0:T(8,128)} custom-call(s32[2]{0:T(128)} %stagger.7, f32[4,5,5]{2,1,0:T(8,128)} %copy.17.a_theta, f32[5,5]{1,0:T(8,128)} %a_axial.5, f32[5,5]{1,0:T(8,128)} %a_radial.5, f32[2,5]{1,0:T(2,128)} %r_cols.1, f32[6,5,64,128]{3,2,1,0:T(8,128)} %get-tuple-element.23.u_ref, f32[6,5,64,128]{3,2,1,0:T(8,128)} %bitcast.7, ...), custom_call_target="tpu_custom_call" | custom-call | tf_op jit(solution)/shard_map/second_step/pallas_call | solution.py:398
  53.5 0.0 all-to-all-done.1.got_ref
  53.5 0.0 copy-done.1
  53.6 0.6 %finish_amplitudes.1 = f32[3,2,2,128]{3,2,1,0:T(2,128)} custom-call(f32[8,8,128]{2,1,0:T(8,128)S(1)} %all-to-all-done.1.got_ref, s32[3,128]{1,0:T(4,128)S(1)} %copy-done.1), custom_call_target="tpu_custom_call" | custom-call | tf_op jit(solution)/shard_map/finish_amplitudes/pallas_call | solution.py:398
Async XLA Ops:
  0.6 16.2 %copy-start.10 = (f32[4,5,5]{2,0,1:T(4,128)S(1)}, f32[4,5,5]{2,0,1:T(4,128)}, u32[]{:S(2)}) copy-start(f32[4,5,5]{2,0,1:T(4,128)} %param.17) | copy-start | bytes 1204
  2.7 18.2 %collective-permute-start = (f32[7,5,8,128]{3,2,1,0:T(8,128)}, f32[7,5,8,128]{3,2,1,0:T(8,128)S(1)}, u32[]{:S(2)}, u32[]{:S(2)}) collective-permute-start(f32[7,5,8,128]{3,2,1,0:T(8,128)} %get-tuple-element.15), channel_id=1, source_target_pairs={{0,8},{8,0},{16,24},{24,16},{32,40},{40,32},{48,56},{56,48},{64,72... | collective-permute-start | bytes 430088 | tf_op jit(solution)/shard_map/ppermute | solution.py:437
  2.8 18.2 %collective-permute-start.1 = (f32[7,5,8,128]{3,2,1,0:T(8,128)}, f32[7,5,8,128]{3,2,1,0:T(8,128)S(1)}, u32[]{:S(2)}, u32[]{:S(2)}) collective-permute-start(f32[7,5,8,128]{3,2,1,0:T(8,128)} %get-tuple-element.16), channel_id=1, source_target_pairs={{0,248},{8,16},{16,8},{24,32},{32,24},{40,48},{48,40},{56,64},{64,... | collective-permute-start | bytes 430088 | tf_op jit(solution)/shard_map/ppermute | solution.py:438
  10.3 8.6 %collective-permute-start.2 = (f32[6,5,8,128]{3,2,1,0:T(8,128)}, f32[6,5,8,128]{3,2,1,0:T(8,128)S(1)}, u32[]{:S(2)}, u32[]{:S(2)}) collective-permute-start(f32[6,5,8,128]{3,2,1,0:T(8,128)} %get-tuple-element.17), channel_id=1, source_target_pairs={{0,1},{1,0},{2,3},{3,2},{4,5},{5,4},{6,7},{7,6},{8,9},{9,8},{10,11... | collective-permute-start | bytes 368648 | tf_op jit(solution)/shard_map/ppermute | solution.py:439
  11.9 9.1 %collective-permute-start.3 = (f32[6,5,8,128]{3,2,1,0:T(8,128)}, f32[6,5,8,128]{3,2,1,0:T(8,128)S(1)}, u32[]{:S(2)}, u32[]{:S(2)}) collective-permute-start(f32[6,5,8,128]{3,2,1,0:T(8,128)} %get-tuple-element.18), channel_id=1, source_target_pairs={{1,2},{2,1},{3,4},{4,3},{5,6},{6,5},{9,10},{10,9},{11,12},{12,11},... | collective-permute-start | bytes 368648 | tf_op jit(solution)/shard_map/ppermute | solution.py:440
  18.9 2.1 %copy-start.4 = (f32[6,5,8,128]{3,2,1,0:T(8,128)}, f32[6,5,8,128]{3,2,1,0:T(8,128)S(1)}, u32[]{:S(2)}) copy-start(f32[6,5,8,128]{3,2,1,0:T(8,128)S(1)} %collective-permute-done.2.after2.xe) | copy-start | bytes 368644
  20.9 0.6 %copy-start.5 = (f32[6,5,8,128]{3,2,1,0:T(8,128)}, f32[6,5,8,128]{3,2,1,0:T(8,128)S(1)}, u32[]{:S(2)}) copy-start(f32[6,5,8,128]{3,2,1,0:T(8,128)S(1)} %collective-permute-done.3.after3.xo) | copy-start | bytes 368644
  20.9 0.7 %copy-start.2 = (f32[7,5,8,128]{3,2,1,0:T(8,128)}, f32[7,5,8,128]{3,2,1,0:T(8,128)S(1)}, u32[]{:S(2)}) copy-start(f32[7,5,8,128]{3,2,1,0:T(8,128)S(1)} %collective-permute-done.te) | copy-start | bytes 430084
  21.0 0.7 %copy-start.3 = (f32[7,5,8,128]{3,2,1,0:T(8,128)}, f32[7,5,8,128]{3,2,1,0:T(8,128)S(1)}, u32[]{:S(2)}) copy-start(f32[7,5,8,128]{3,2,1,0:T(8,128)S(1)} %collective-permute-done.1.to) | copy-start | bytes 430084
  24.0 19.4 %all-to-all-start = ((f32[32,8,128]{2,1,0:T(8,128)}), f32[32,8,128]{2,1,0:T(8,128)S(1)}, u32[]{:S(2)}, u32[]{:S(2)}) async-start(f32[32,8,128]{2,1,0:T(8,128)} %plane_part.1.after), calls=%async_computation | async-start | bytes 262144 | tf_op jit(solution)/shard_map/all_to_all | solution.py:473
  32.8 15.0 %collective-permute-start.4 = (f32[6,5,8,128]{3,2,1,0:T(8,128)}, f32[6,5,8,128]{3,2,1,0:T(8,128)S(1)}, u32[]{:S(2)}, u32[]{:S(2)}) collective-permute-start(f32[6,5,8,128]{3,2,1,0:T(8,128)} %get-tuple-element.24), channel_id=1, source_target_pairs={{0,8},{8,0},{16,24},{24,16},{32,40},{40,32},{48,56},{56,48},{64,72... | collective-permute-start | bytes 368648 | tf_op jit(solution)/shard_map/ppermute | solution.py:437
  33.1 14.8 %collective-permute-start.5 = (f32[6,5,8,128]{3,2,1,0:T(8,128)}, f32[6,5,8,128]{3,2,1,0:T(8,128)S(1)}, u32[]{:S(2)}, u32[]{:S(2)}) collective-permute-start(f32[6,5,8,128]{3,2,1,0:T(8,128)} %get-tuple-element.25), channel_id=1, source_target_pairs={{0,248},{8,16},{16,8},{24,32},{32,24},{40,48},{48,40},{56,64},{64,... | collective-permute-start | bytes 368648 | tf_op jit(solution)/shard_map/ppermute | solution.py:438
  38.4 9.4 %collective-permute-start.6 = (f32[6,5,8,128]{3,2,1,0:T(8,128)}, f32[6,5,8,128]{3,2,1,0:T(8,128)S(1)}, u32[]{:S(2)}, u32[]{:S(2)}) collective-permute-start(f32[6,5,8,128]{3,2,1,0:T(8,128)} %get-tuple-element.26), channel_id=1, source_target_pairs={{0,1},{1,0},{2,3},{3,2},{4,5},{5,4},{6,7},{7,6},{8,9},{9,8},{10,11... | collective-permute-start | bytes 368648 | tf_op jit(solution)/shard_map/ppermute | solution.py:439
  38.5 9.5 %collective-permute-start.7 = (f32[6,5,8,128]{3,2,1,0:T(8,128)}, f32[6,5,8,128]{3,2,1,0:T(8,128)S(1)}, u32[]{:S(2)}, u32[]{:S(2)}) collective-permute-start(f32[6,5,8,128]{3,2,1,0:T(8,128)} %get-tuple-element.27), channel_id=1, source_target_pairs={{1,2},{2,1},{3,4},{4,3},{5,6},{6,5},{9,10},{10,9},{11,12},{12,11},... | collective-permute-start | bytes 368648 | tf_op jit(solution)/shard_map/ppermute | solution.py:440
  43.4 4.5 %copy-start = (f32[32,8,128]{2,1,0:T(8,128)}, f32[32,8,128]{2,1,0:T(8,128)S(1)}, u32[]{:S(2)}) copy-start(f32[32,8,128]{2,1,0:T(8,128)S(1)} %all-to-all-done.got_ref) | copy-start | bytes 393220
  44.1 9.5 %all-to-all-start.1 = ((f32[8,8,128]{2,1,0:T(8,128)}), f32[8,8,128]{2,1,0:T(8,128)S(1)}, u32[]{:S(2)}, u32[]{:S(2)}) async-start(f32[8,8,128]{2,1,0:T(8,128)} %share_amplitudes.1), calls=%async_computation.1 | async-start | bytes 65536 | tf_op jit(solution)/shard_map/all_to_all | solution.py:476
  47.9 0.6 %copy-start.6 = (f32[6,5,8,128]{3,2,1,0:T(8,128)}, f32[6,5,8,128]{3,2,1,0:T(8,128)S(1)}, u32[]{:S(2)}) copy-start(f32[6,5,8,128]{3,2,1,0:T(8,128)S(1)} %collective-permute-done.4.te) | copy-start | bytes 368644
  47.9 0.7 %copy-start.7 = (f32[6,5,8,128]{3,2,1,0:T(8,128)}, f32[6,5,8,128]{3,2,1,0:T(8,128)S(1)}, u32[]{:S(2)}) copy-start(f32[6,5,8,128]{3,2,1,0:T(8,128)S(1)} %collective-permute-done.5.to) | copy-start | bytes 368644
  47.9 0.7 %copy-start.8 = (f32[6,5,8,128]{3,2,1,0:T(8,128)}, f32[6,5,8,128]{3,2,1,0:T(8,128)S(1)}, u32[]{:S(2)}) copy-start(f32[6,5,8,128]{3,2,1,0:T(8,128)S(1)} %collective-permute-done.6.xe) | copy-start | bytes 368644
  47.9 0.7 %copy-start.9 = (f32[6,5,8,128]{3,2,1,0:T(8,128)}, f32[6,5,8,128]{3,2,1,0:T(8,128)S(1)}, u32[]{:S(2)}) copy-start(f32[6,5,8,128]{3,2,1,0:T(8,128)S(1)} %collective-permute-done.7.xo) | copy-start | bytes 368644
  48.7 4.9 %copy-start.1 = (s32[3,128]{1,0:T(4,128)S(1)}, s32[3,128]{1,0:T(4,128)}, u32[]{:S(2)}) copy-start(s32[3,128]{1,0:T(4,128)} %plane.5) | copy-start | bytes 4612

commit v4 on v3

--- a/solution.py
+++ b/solution.py
@@ -120,8 +120,17 @@
     write_faces(place, out_ref, te2, to2, xe2, xo2)
 
 
-def table_kernel(tdevices, order, radial, cos_ref, sin_ref, wave_ref, pick_ref):
+def table_kernel(
+    tdevices, xdevices, order, radial, u_ref, src_ref, cos_ref, sin_ref, wave_ref, pick_ref, rows_ref
+):
     place = where()
+    last = (place[1] == xdevices - 1).astype(jnp.int32)
+    for ref, first_slot, count in ((u_ref, 0, 3), (src_ref, 3, 2)):
+        for j in range(count):
+            at = pl.ds(last * 7 + j * (1 - 2 * last), 8, stride=8)
+            for i in range(u_ref.shape[0]):
+                for v in range(u_ref.shape[1]):
+                    rows_ref[first_slot + j, i, v] = ref[i, v, at, :]
     nharm, nmode = order.shape
     tcells = 8
     total = tcells * tdevices
@@ -154,9 +163,9 @@
     return jnp.concatenate(out, axis=0)
 
 
-def plane_part(last, tdevices, stagger, a_theta, a_axial, a_radial, l_rows, u_ref, src_ref, sig_ref, lo, hi, refs):
+def plane_part(last, tdevices, stagger, a_theta, a_axial, a_radial, l_rows, rows_ref, sig_ref, lo, hi, refs):
     plane, cos_ref, sin_ref, wave_ref, pick_ref, part_ref = refs
-    nhp, nvar, rows, nr = u_ref.shape
+    _, nhp, nvar, _, nr = rows_ref.shape
     nharm, nmode = plane.shape
     nset = a_theta.shape[0]
     scale = 1.0 / math.sqrt(8 * tdevices * nr)
@@ -166,9 +175,6 @@
     row1, row2 = row[0], lax.broadcasted_iota(jnp.int32, (8, nr), 0)
     side = (1 - 2 * last).astype(jnp.float32)
     at = [last * 7 + j * (1 - 2 * last) for j in range(3)]
-
-    def own_rows(ref, v, j):
-        return jnp.stack([ref[i, v, pl.ds(at[j], 8, stride=8), :] for i in range(nhp)])
 
     def shift_r(u):
         return (
@@ -203,8 +209,8 @@
         step_in.append(courant / (1.0 + sig[j]))
         step_out.append(courant / (1.0 + sig_out[j]))
 
-    state = [[own_rows(u_ref, v, j) for v in range(nvar)] for j in range(3)]
-    source = [[own_rows(src_ref, v, j) for v in range(nvar)] for j in range(2)]
+    state = [[rows_ref[j, :, v] for v in range(nvar)] for j in range(3)]
+    source = [[rows_ref[3 + j, :, v] for v in range(nvar)] for j in range(2)]
     first, first_out = [], []
     for j in range(2):
         acc, acc_out = [None] * nvar, [None] * nvar
@@ -288,8 +294,7 @@
     a_axial,
     a_radial,
     l_rows,
-    u_ref,
-    src_ref,
+    rows_ref,
     sig_ref,
     te,
     to,
@@ -304,7 +309,7 @@
     part_ref,
 ):
     place = where()
-    nhp = u_ref.shape[0]
+    nhp = rows_ref.shape[1]
     last = (place[1] == xdevices - 1).astype(jnp.int32)
     holds = jnp.logical_or(place[1] == 0, place[1] == xdevices - 1)
     todd = lax.rem(place[0], 2) == 1
@@ -319,7 +324,7 @@
     def _():
         refs = (plane, cos_ref, sin_ref, wave_ref, pick_ref, part_ref)
         plane_part(
-            last, tdevices, stagger, a_theta, a_axial, a_radial, l_rows, u_ref, src_ref, sig_ref, lo, hi, refs
+            last, tdevices, stagger, a_theta, a_axial, a_radial, l_rows, rows_ref, sig_ref, lo, hi, refs
         )
 
     @pl.when(jnp.logical_not(holds))
@@ -443,12 +448,13 @@
     coefs = (stagger, a_theta, a_axial, a_radial)
     faces = call(pack_kernel, "pack_faces", (stagger,), (u, sig), [packed] * 2 + [face] * 2)
     faces = swap(*faces)
-    tabs = call(
-        functools.partial(table_kernel, tdev),
+    *tabs, near = call(
+        functools.partial(table_kernel, tdev, xdev),
         "mode_tables",
         (),
-        (mode_order, mode_radial),
-        [array(nharm, 16, nmode)] * 2 + [array(nrad, nradial), array(nharm, nrad, nmode)],
+        (mode_order, mode_radial, u, src),
+        [array(nharm, 16, nmode)] * 2
+        + [array(nrad, nradial), array(nharm, nrad, nmode), array(5, nhp, nvar, 8, nradial)],
     )
 
     def planes(after):
@@ -456,7 +462,7 @@
             functools.partial(plane_kernel, tdev, xdev),
             "plane_part",
             (*coefs, l_rows),
-            (u, src, sig, faces[0], faces[1], mode_plane, *tabs, after, faces[2], faces[3]),
+            (near, sig, faces[0], faces[1], mode_plane, *tabs, after, faces[2], faces[3]),
             array(tdev, 8, nmode),
             3,
         )

time: 54.7 us -> 54.3 us (level)
  waiting for transfers between devices: 2.09 us -> 0.94 us
  Pallas kernels: 16.7 us -> 17.5 us
    ppermute x2, waiting for transfers between devices: 2.07 us -> 0.92 us  [swap(): lax.ppermute(xo, 'xr', odd_x)]
    pallas_call x7, Pallas kernels: 16.7 us -> 17.5 us  [call(): pl.pallas_call(kernel, in_specs=[spec(SM)] * len(scalars) + [spec(VM)] *...]
  transfers between devices with their start and end apart: 10 -> 10, of which waited for: 1 -> 1; matrix products, arithmetic and copies ran while one was open for 1% -> 1% of each run, Pallas kernels for 22% -> 24%
where the time goes in v4:
time: 54.3 us; the launch traced here: 53.8 us
  starting transfers between devices  32.5 us (60%)
  Pallas kernels  17.5 us (32%)
  local copies, waits for them, and re-layouts  2.06 us (4%)
  waiting for transfers between devices  0.94 us (2%)
  between operations  0.79 us (1%)
    pallas_call x7, Pallas kernels, call(): pl.pallas_call(kernel, in_specs=[spec(SM)] * len(scalars) + [spec(VM)] *...  17.5 us
    ppermute x2, starting transfers between devices, swap(): lax.ppermute(to, 'theta', odd_t)  12.9 us
    ppermute x2, starting transfers between devices, swap(): lax.ppermute(xo, 'xr', odd_x)  9.89 us
    all_to_all x1, starting transfers between devices, local(): got = lax.all_to_all(part, 'theta', 0, 0, tiled=True)  4.1 us
    all_to_all x1, starting transfers between devices, local(): amp = lax.all_to_all(amp, 'xr', 0, 0, tiled=True)  3.78 us
    unnamed x23, local copies, waits for them, and re-layouts  2.06 us
    ppermute x2, starting transfers between devices, swap(): lax.ppermute(xe, 'xr', even_x)  1.58 us
  transfers between devices with their start and end apart: 10, of which 1 were waited for; matrix products, arithmetic and copies ran while one was open for 1% of the time, Pallas kernels for 24%

profile of v4, /device:TPU:2, one launch (start us, length us, event | category | flops | bytes accessed | tf_op | source)
XLA Modules:
  0.0 53.8 jit_solution(1171699217170718453)
XLA Ops:
  0.6 0.0 copy-start.10
  0.6 2.1 %pack_faces.1 = (f32[7,5,8,128]{3,2,1,0:T(8,128)}, f32[7,5,8,128]{3,2,1,0:T(8,128)}, f32[6,5,8,128]{3,2,1,0:T(8,128)}, f32[6,5,8,128]{3,2,1,0:T(8,128)}) custom-call(s32[2]{0:T(128)} %stagger.7, f32[6,5,64,128]{3,2,1,0:T(8,128)} %bitcast.4, f32[64,128]{1,0:T(8,128)} %bitcast.12), custom_call_target="tpu_custom_call" | custom-call | tf_op jit(solution)/shard_map/pack_faces/pallas_call | solution.py:403
  2.8 0.0 collective-permute-start
  2.8 7.5 %collective-permute-start.1 = (f32[7,5,8,128]{3,2,1,0:T(8,128)}, f32[7,5,8,128]{3,2,1,0:T(8,128)S(1)}, u32[]{:S(2)}, u32[]{:S(2)}) collective-permute-start(f32[7,5,8,128]{3,2,1,0:T(8,128)} %get-tuple-element.17), channel_id=1, source_target_pairs={{0,248},{8,16},{16,8},{24,32},{32,24},{40,48},{48,40},{56,64},{64,... | collective-permute-start | bytes 430088 | tf_op jit(solution)/shard_map/ppermute | solution.py:443
  10.3 1.6 %collective-permute-start.2 = (f32[6,5,8,128]{3,2,1,0:T(8,128)}, f32[6,5,8,128]{3,2,1,0:T(8,128)S(1)}, u32[]{:S(2)}, u32[]{:S(2)}) collective-permute-start(f32[6,5,8,128]{3,2,1,0:T(8,128)} %get-tuple-element.18), channel_id=1, source_target_pairs={{0,1},{1,0},{2,3},{3,2},{4,5},{5,4},{6,7},{7,6},{8,9},{9,8},{10,11... | collective-permute-start | bytes 368648 | tf_op jit(solution)/shard_map/ppermute | solution.py:444
  11.9 4.9 %collective-permute-start.3 = (f32[6,5,8,128]{3,2,1,0:T(8,128)}, f32[6,5,8,128]{3,2,1,0:T(8,128)S(1)}, u32[]{:S(2)}, u32[]{:S(2)}) collective-permute-start(f32[6,5,8,128]{3,2,1,0:T(8,128)} %get-tuple-element.19), channel_id=1, source_target_pairs={{1,2},{2,1},{3,4},{4,3},{5,6},{6,5},{9,10},{10,9},{11,12},{12,11},... | collective-permute-start | bytes 368648 | tf_op jit(solution)/shard_map/ppermute | solution.py:445
  16.8 0.0 copy-done.10
  16.8 0.6 %copy.17.a_theta = f32[4,5,5]{2,1,0:T(8,128)} copy(f32[4,5,5]{2,0,1:T(4,128)S(1)} %copy-done.10) | data formatting | bytes 800 | tf_op args[4]
  17.4 2.6 %mode_tables.1 = (f32[3,16,128]{2,1,0:T(8,128)}, f32[3,16,128]{2,1,0:T(8,128)}, f32[8,128]{1,0:T(8,128)}, f32[3,8,128]{2,1,0:T(8,128)}, f32[5,6,5,8,128]{4,3,2,1,0:T(8,128)}) custom-call(s32[3,128]{1,0:T(4,128)} %order.1, s32[3,128]{1,0:T(4,128)} %radial.1, f32[6,5,64,128]{3,2,1,0:T(8,128)} %bitcast.5, f32[6,5,64,128]{3,2,1,0:T(8,128)} %bitcast.8), custom_call_target="tpu_custom_call" | custom-call | tf_op jit(solution)/shard_map/mode_tables/pallas_call | solution.py:403
  20.0 0.0 collective-permute-done.2.after2.xe
  20.0 0.0 copy-start.4
  20.0 0.9 %collective-permute-done.3.after3.xo = f32[6,5,8,128]{3,2,1,0:T(8,128)S(1)} collective-permute-done((f32[6,5,8,128]{3,2,1,0:T(8,128)}, f32[6,5,8,128]{3,2,1,0:T(8,128)S(1)}, u32[]{:S(2)}, u32[]{:S(2)}) %collective-permute-start.3) | collective-permute-done | bytes 122912 | tf_op jit(solution)/shard_map/ppermute | solution.py:445
  21.0 0.0 copy-start.5
  21.0 0.0 collective-permute-done.te
  21.0 0.0 copy-start.2
  21.0 0.0 collective-permute-done.1.to
  21.0 0.0 copy-start.3
  21.0 0.0 copy-done.4
  21.0 0.6 %copy-done.5 = f32[6,5,8,128]{3,2,1,0:T(8,128)} copy-done((f32[6,5,8,128]{3,2,1,0:T(8,128)}, f32[6,5,8,128]{3,2,1,0:T(8,128)S(1)}, u32[]{:S(2)}) %copy-start.5) | copy-done | bytes 122904
  21.6 0.1 copy-done.2
  21.7 0.0 copy-done.3
  21.7 1.9 %plane_part.1.after = f32[32,8,128]{2,1,0:T(8,128)} custom-call(s32[2]{0:T(128)} %stagger.7, f32[4,5,5]{2,1,0:T(8,128)} %copy.17.a_theta, f32[5,5]{1,0:T(8,128)} %a_axial.5, f32[5,5]{1,0:T(8,128)} %a_radial.5, f32[2,5]{1,0:T(2,128)} %l_rows.1, f32[5,6,5,8,128]{4,3,2,1,0:T(8,128)} %get-tuple-element.20.rows_ref, f32[64,128]{1,0:T(8,128)} %bitcast.13, ...), custom_call_target="tpu_custom_call" | custom-call | tf_op jit(solution)/shard_map/plane_part/pallas_call | solution.py:403
  23.6 4.1 %all-to-all-start = ((f32[32,8,128]{2,1,0:T(8,128)}), f32[32,8,128]{2,1,0:T(8,128)S(1)}, u32[]{:S(2)}, u32[]{:S(2)}) async-start(f32[32,8,128]{2,1,0:T(8,128)} %plane_part.1.after), calls=%async_computation | async-start | bytes 262144 | tf_op jit(solution)/shard_map/all_to_all | solution.py:479
  27.7 4.7 %first_step.1 = (f32[6,5,64,128]{3,2,1,0:T(8,128)}, f32[6,5,8,128]{3,2,1,0:T(8,128)}, f32[6,5,8,128]{3,2,1,0:T(8,128)}, f32[6,5,8,128]{3,2,1,0:T(8,128)}, f32[6,5,8,128]{3,2,1,0:T(8,128)}) custom-call(s32[2]{0:T(128)} %stagger.7, f32[4,5,5]{2,1,0:T(8,128)} %copy.17.a_theta, f32[5,5]{1,0:T(8,128)} %a_axial.5, f32[5,5]{1,0:T(8,128)} %a_radial.5, ...), custom_call_target="tpu_custom_call" | custom-call | tf_op jit(solution)/shard_map/first_step/pallas_call | solution.py:403
  32.5 0.3 collective-permute-start.4
  32.7 5.3 %collective-permute-start.5 = (f32[6,5,8,128]{3,2,1,0:T(8,128)}, f32[6,5,8,128]{3,2,1,0:T(8,128)S(1)}, u32[]{:S(2)}, u32[]{:S(2)}) collective-permute-start(f32[6,5,8,128]{3,2,1,0:T(8,128)} %get-tuple-element.27), channel_id=1, source_target_pairs={{0,248},{8,16},{16,8},{24,32},{32,24},{40,48},{48,40},{56,64},{64,... | collective-permute-start | bytes 368648 | tf_op jit(solution)/shard_map/ppermute | solution.py:443
  38.1 0.0 collective-permute-start.6
  38.1 4.9 %collective-permute-start.7 = (f32[6,5,8,128]{3,2,1,0:T(8,128)}, f32[6,5,8,128]{3,2,1,0:T(8,128)S(1)}, u32[]{:S(2)}, u32[]{:S(2)}) collective-permute-start(f32[6,5,8,128]{3,2,1,0:T(8,128)} %get-tuple-element.29), channel_id=1, source_target_pairs={{1,2},{2,1},{3,4},{4,3},{5,6},{6,5},{9,10},{10,9},{11,12},{12,11},... | collective-permute-start | bytes 368648 | tf_op jit(solution)/shard_map/ppermute | solution.py:445
  43.0 0.0 all-to-all-done.got_ref
  43.0 0.0 copy-start
  43.0 0.6 %share_amplitudes.1 = f32[8,8,128]{2,1,0:T(8,128)} custom-call(f32[32,8,128]{2,1,0:T(8,128)S(1)} %all-to-all-done.got_ref), custom_call_target="tpu_custom_call" | custom-call | tf_op jit(solution)/shard_map/share_amplitudes/pallas_call | solution.py:403
  43.7 3.8 %all-to-all-start.1 = ((f32[8,8,128]{2,1,0:T(8,128)}), f32[8,8,128]{2,1,0:T(8,128)S(1)}, u32[]{:S(2)}, u32[]{:S(2)}) async-start(f32[8,8,128]{2,1,0:T(8,128)} %share_amplitudes.1), calls=%async_computation.1 | async-start | bytes 65536 | tf_op jit(solution)/shard_map/all_to_all | solution.py:482
  47.5 0.0 collective-permute-done.4.te
  47.5 0.0 copy-start.6
  47.5 0.0 collective-permute-done.5.to
  47.5 0.0 copy-start.7
  47.5 0.0 collective-permute-done.6.xe
  47.5 0.0 copy-start.8
  47.5 0.0 collective-permute-done.7.xo
  47.5 0.0 copy-start.9
  47.5 0.0 copy-done
  47.5 0.6 %copy-done.6 = f32[6,5,8,128]{3,2,1,0:T(8,128)} copy-done((f32[6,5,8,128]{3,2,1,0:T(8,128)}, f32[6,5,8,128]{3,2,1,0:T(8,128)S(1)}, u32[]{:S(2)}) %copy-start.6) | copy-done | bytes 122904
  48.1 0.1 copy-done.7
  48.2 0.1 copy-done.8
  48.2 0.0 copy-done.9
  48.3 0.0 copy-start.1
  48.3 4.9 %second_step.1 = f32[6,5,64,128]{3,2,1,0:T(8,128)} custom-call(s32[2]{0:T(128)} %stagger.7, f32[4,5,5]{2,1,0:T(8,128)} %copy.17.a_theta, f32[5,5]{1,0:T(8,128)} %a_axial.5, f32[5,5]{1,0:T(8,128)} %a_radial.5, f32[2,5]{1,0:T(2,128)} %r_cols.1, f32[6,5,64,128]{3,2,1,0:T(8,128)} %get-tuple-element.25.u_ref, f32[6,5,64,128]{3,2,1,0:T(8,128)} %bitcast.7, ...), custom_call_target="tpu_custom_call" | custom-call | tf_op jit(solution)/shard_map/second_step/pallas_call | solution.py:403
  53.1 0.0 all-to-all-done.1.got_ref
  53.1 0.0 copy-done.1
  53.2 0.6 %finish_amplitudes.1 = f32[3,2,2,128]{3,2,1,0:T(2,128)} custom-call(f32[8,8,128]{2,1,0:T(8,128)S(1)} %all-to-all-done.1.got_ref, s32[3,128]{1,0:T(4,128)S(1)} %copy-done.1), custom_call_target="tpu_custom_call" | custom-call | tf_op jit(solution)/shard_map/finish_amplitudes/pallas_call | solution.py:403
Async XLA Ops:
  0.6 16.2 %copy-start.10 = (f32[4,5,5]{2,0,1:T(4,128)S(1)}, f32[4,5,5]{2,0,1:T(4,128)}, u32[]{:S(2)}) copy-start(f32[4,5,5]{2,0,1:T(4,128)} %param.17) | copy-start | bytes 1204
  2.8 18.2 %collective-permute-start = (f32[7,5,8,128]{3,2,1,0:T(8,128)}, f32[7,5,8,128]{3,2,1,0:T(8,128)S(1)}, u32[]{:S(2)}, u32[]{:S(2)}) collective-permute-start(f32[7,5,8,128]{3,2,1,0:T(8,128)} %get-tuple-element.16), channel_id=1, source_target_pairs={{0,8},{8,0},{16,24},{24,16},{32,40},{40,32},{48,56},{56,48},{64,72... | collective-permute-start | bytes 430088 | tf_op jit(solution)/shard_map/ppermute | solution.py:442
  2.8 18.2 %collective-permute-start.1 = (f32[7,5,8,128]{3,2,1,0:T(8,128)}, f32[7,5,8,128]{3,2,1,0:T(8,128)S(1)}, u32[]{:S(2)}, u32[]{:S(2)}) collective-permute-start(f32[7,5,8,128]{3,2,1,0:T(8,128)} %get-tuple-element.17), channel_id=1, source_target_pairs={{0,248},{8,16},{16,8},{24,32},{32,24},{40,48},{48,40},{56,64},{64,... | collective-permute-start | bytes 430088 | tf_op jit(solution)/shard_map/ppermute | solution.py:443
  10.3 9.7 %collective-permute-start.2 = (f32[6,5,8,128]{3,2,1,0:T(8,128)}, f32[6,5,8,128]{3,2,1,0:T(8,128)S(1)}, u32[]{:S(2)}, u32[]{:S(2)}) collective-permute-start(f32[6,5,8,128]{3,2,1,0:T(8,128)} %get-tuple-element.18), channel_id=1, source_target_pairs={{0,1},{1,0},{2,3},{3,2},{4,5},{5,4},{6,7},{7,6},{8,9},{9,8},{10,11... | collective-permute-start | bytes 368648 | tf_op jit(solution)/shard_map/ppermute | solution.py:444
  11.9 9.1 %collective-permute-start.3 = (f32[6,5,8,128]{3,2,1,0:T(8,128)}, f32[6,5,8,128]{3,2,1,0:T(8,128)S(1)}, u32[]{:S(2)}, u32[]{:S(2)}) collective-permute-start(f32[6,5,8,128]{3,2,1,0:T(8,128)} %get-tuple-element.19), channel_id=1, source_target_pairs={{1,2},{2,1},{3,4},{4,3},{5,6},{6,5},{9,10},{10,9},{11,12},{12,11},... | collective-permute-start | bytes 368648 | tf_op jit(solution)/shard_map/ppermute | solution.py:445
  20.0 0.9 %copy-start.4 = (f32[6,5,8,128]{3,2,1,0:T(8,128)}, f32[6,5,8,128]{3,2,1,0:T(8,128)S(1)}, u32[]{:S(2)}) copy-start(f32[6,5,8,128]{3,2,1,0:T(8,128)S(1)} %collective-permute-done.2.after2.xe) | copy-start | bytes 368644
  21.0 0.6 %copy-start.5 = (f32[6,5,8,128]{3,2,1,0:T(8,128)}, f32[6,5,8,128]{3,2,1,0:T(8,128)S(1)}, u32[]{:S(2)}) copy-start(f32[6,5,8,128]{3,2,1,0:T(8,128)S(1)} %collective-permute-done.3.after3.xo) | copy-start | bytes 368644
  21.0 0.7 %copy-start.2 = (f32[7,5,8,128]{3,2,1,0:T(8,128)}, f32[7,5,8,128]{3,2,1,0:T(8,128)S(1)}, u32[]{:S(2)}) copy-start(f32[7,5,8,128]{3,2,1,0:T(8,128)S(1)} %collective-permute-done.te) | copy-start | bytes 430084
  21.0 0.7 %copy-start.3 = (f32[7,5,8,128]{3,2,1,0:T(8,128)}, f32[7,5,8,128]{3,2,1,0:T(8,128)S(1)}, u32[]{:S(2)}) copy-start(f32[7,5,8,128]{3,2,1,0:T(8,128)S(1)} %collective-permute-done.1.to) | copy-start | bytes 430084
  23.6 19.4 %all-to-all-start = ((f32[32,8,128]{2,1,0:T(8,128)}), f32[32,8,128]{2,1,0:T(8,128)S(1)}, u32[]{:S(2)}, u32[]{:S(2)}) async-start(f32[32,8,128]{2,1,0:T(8,128)} %plane_part.1.after), calls=%async_computation | async-start | bytes 262144 | tf_op jit(solution)/shard_map/all_to_all | solution.py:479
  32.5 15.0 %collective-permute-start.4 = (f32[6,5,8,128]{3,2,1,0:T(8,128)}, f32[6,5,8,128]{3,2,1,0:T(8,128)S(1)}, u32[]{:S(2)}, u32[]{:S(2)}) collective-permute-start(f32[6,5,8,128]{3,2,1,0:T(8,128)} %get-tuple-element.26), channel_id=1, source_target_pairs={{0,8},{8,0},{16,24},{24,16},{32,40},{40,32},{48,56},{56,48},{64,72... | collective-permute-start | bytes 368648 | tf_op jit(solution)/shard_map/ppermute | solution.py:442
  32.7 14.7 %collective-permute-start.5 = (f32[6,5,8,128]{3,2,1,0:T(8,128)}, f32[6,5,8,128]{3,2,1,0:T(8,128)S(1)}, u32[]{:S(2)}, u32[]{:S(2)}) collective-permute-start(f32[6,5,8,128]{3,2,1,0:T(8,128)} %get-tuple-element.27), channel_id=1, source_target_pairs={{0,248},{8,16},{16,8},{24,32},{32,24},{40,48},{48,40},{56,64},{64,... | collective-permute-start | bytes 368648 | tf_op jit(solution)/shard_map/ppermute | solution.py:443
  38.1 9.4 %collective-permute-start.6 = (f32[6,5,8,128]{3,2,1,0:T(8,128)}, f32[6,5,8,128]{3,2,1,0:T(8,128)S(1)}, u32[]{:S(2)}, u32[]{:S(2)}) collective-permute-start(f32[6,5,8,128]{3,2,1,0:T(8,128)} %get-tuple-element.28), channel_id=1, source_target_pairs={{0,1},{1,0},{2,3},{3,2},{4,5},{5,4},{6,7},{7,6},{8,9},{9,8},{10,11... | collective-permute-start | bytes 368648 | tf_op jit(solution)/shard_map/ppermute | solution.py:444
  38.1 9.4 %collective-permute-start.7 = (f32[6,5,8,128]{3,2,1,0:T(8,128)}, f32[6,5,8,128]{3,2,1,0:T(8,128)S(1)}, u32[]{:S(2)}, u32[]{:S(2)}) collective-permute-start(f32[6,5,8,128]{3,2,1,0:T(8,128)} %get-tuple-element.29), channel_id=1, source_target_pairs={{1,2},{2,1},{3,4},{4,3},{5,6},{6,5},{9,10},{10,9},{11,12},{12,11},... | collective-permute-start | bytes 368648 | tf_op jit(solution)/shard_map/ppermute | solution.py:445
  43.0 4.5 %copy-start = (f32[32,8,128]{2,1,0:T(8,128)}, f32[32,8,128]{2,1,0:T(8,128)S(1)}, u32[]{:S(2)}) copy-start(f32[32,8,128]{2,1,0:T(8,128)S(1)} %all-to-all-done.got_ref) | copy-start | bytes 393220
  43.7 9.5 %all-to-all-start.1 = ((f32[8,8,128]{2,1,0:T(8,128)}), f32[8,8,128]{2,1,0:T(8,128)S(1)}, u32[]{:S(2)}, u32[]{:S(2)}) async-start(f32[8,8,128]{2,1,0:T(8,128)} %share_amplitudes.1), calls=%async_computation.1 | async-start | bytes 65536 | tf_op jit(solution)/shard_map/all_to_all | solution.py:482
  47.5 0.6 %copy-start.6 = (f32[6,5,8,128]{3,2,1,0:T(8,128)}, f32[6,5,8,128]{3,2,1,0:T(8,128)S(1)}, u32[]{:S(2)}) copy-start(f32[6,5,8,128]{3,2,1,0:T(8,128)S(1)} %collective-permute-done.4.te) | copy-start | bytes 368644
  47.5 0.7 %copy-start.7 = (f32[6,5,8,128]{3,2,1,0:T(8,128)}, f32[6,5,8,128]{3,2,1,0:T(8,128)S(1)}, u32[]{:S(2)}) copy-start(f32[6,5,8,128]{3,2,1,0:T(8,128)S(1)} %collective-permute-done.5.to) | copy-start | bytes 368644
  47.5 0.7 %copy-start.8 = (f32[6,5,8,128]{3,2,1,0:T(8,128)}, f32[6,5,8,128]{3,2,1,0:T(8,128)S(1)}, u32[]{:S(2)}) copy-start(f32[6,5,8,128]{3,2,1,0:T(8,128)S(1)} %collective-permute-done.6.xe) | copy-start | bytes 368644
  47.5 0.7 %copy-start.9 = (f32[6,5,8,128]{3,2,1,0:T(8,128)}, f32[6,5,8,128]{3,2,1,0:T(8,128)S(1)}, u32[]{:S(2)}) copy-start(f32[6,5,8,128]{3,2,1,0:T(8,128)S(1)} %collective-permute-done.7.xo) | copy-start | bytes 368644
  48.3 4.9 %copy-start.1 = (s32[3,128]{1,0:T(4,128)S(1)}, s32[3,128]{1,0:T(4,128)}, u32[]{:S(2)}) copy-start(s32[3,128]{1,0:T(4,128)} %plane.5) | copy-start | bytes 4612

commit v5 on v4

--- a/solution.py
+++ b/solution.py
@@ -380,7 +380,7 @@
 
     @pl.when(holds)
     def _():
-        amp = jnp.sum(got_ref[...], axis=0)
+        amp = got_ref[0]
         for h in range(nharm):
             cos, sin = cos_ref[h, 0:8], sin_ref[h, 0:8]
             mine = plane[h : h + 1, :] == last
@@ -479,12 +479,13 @@
     got = lax.all_to_all(part, "theta", 0, 0, tiled=True)
     faces2 = swap(*faces2)
     amp = call(functools.partial(share_kernel, xdev), "share_amplitudes", (), (got,), array(xdev, 8, nmode))
+    mine = amp
     amp = lax.all_to_all(amp, "xr", 0, 0, tiled=True)
     fields = call(
         functools.partial(second_kernel, tdev, xdev),
         "second_step",
         (*coefs, r_cols),
-        (first, u, src, sig, *faces2, got, gust, mode_plane, *tabs),
+        (first, u, src, sig, *faces2, mine, gust, mode_plane, *tabs),
         whole,
     )
     amplitudes = call(finish_kernel, "finish_amplitudes", (), (amp, mode_plane), array(nharm, 2, two, nmode))

time: 54.3 us -> 54.3 us (level)
    unnamed x23 -> x21, local copies, waits for them, and re-layouts: 2.06 us -> 2.08 us
where the time goes in v5:
time: 54.3 us; the launch traced here: 53.7 us
  starting transfers between devices  32.5 us (60%)
  Pallas kernels  17.5 us (32%)
  local copies, waits for them, and re-layouts  2.08 us (4%)
  waiting for transfers between devices  0.94 us (2%)
  between operations  0.77 us (1%)
    pallas_call x7, Pallas kernels, call(): pl.pallas_call(kernel, in_specs=[spec(SM)] * len(scalars) + [spec(VM)] *...  17.5 us
    ppermute x2, starting transfers between devices, swap(): lax.ppermute(to, 'theta', odd_t)  12.9 us
    ppermute x2, starting transfers between devices, swap(): lax.ppermute(xo, 'xr', odd_x)  9.89 us
    all_to_all x1, starting transfers between devices, local(): got = lax.all_to_all(part, 'theta', 0, 0, tiled=True)  4.1 us
    all_to_all x1, starting transfers between devices, local(): amp = lax.all_to_all(amp, 'xr', 0, 0, tiled=True)  3.78 us
    unnamed x21, local copies, waits for them, and re-layouts  2.08 us
    ppermute x2, starting transfers between devices, swap(): lax.ppermute(xe, 'xr', even_x)  1.58 us
  transfers between devices with their start and end apart: 10, of which 1 were waited for; matrix products, arithmetic and copies ran while one was open for 1% of the time, Pallas kernels for 24%

profile of v5, /device:TPU:2, one launch (start us, length us, event | category | flops | bytes accessed | tf_op | source)
XLA Modules:
  0.0 53.7 jit_solution(15200899239402950497)
XLA Ops:
  0.6 0.0 copy-start.9
  0.6 2.1 %pack_faces.1 = (f32[7,5,8,128]{3,2,1,0:T(8,128)}, f32[7,5,8,128]{3,2,1,0:T(8,128)}, f32[6,5,8,128]{3,2,1,0:T(8,128)}, f32[6,5,8,128]{3,2,1,0:T(8,128)}) custom-call(s32[2]{0:T(128)} %stagger.7, f32[6,5,64,128]{3,2,1,0:T(8,128)} %bitcast.4, f32[64,128]{1,0:T(8,128)} %bitcast.12), custom_call_target="tpu_custom_call" | custom-call | tf_op jit(solution)/shard_map/pack_faces/pallas_call | solution.py:403
  2.8 0.0 collective-permute-start
  2.8 7.5 %collective-permute-start.1 = (f32[7,5,8,128]{3,2,1,0:T(8,128)}, f32[7,5,8,128]{3,2,1,0:T(8,128)S(1)}, u32[]{:S(2)}, u32[]{:S(2)}) collective-permute-start(f32[7,5,8,128]{3,2,1,0:T(8,128)} %get-tuple-element.17), channel_id=1, source_target_pairs={{0,248},{8,16},{16,8},{24,32},{32,24},{40,48},{48,40},{56,64},{64,... | collective-permute-start | bytes 430088 | tf_op jit(solution)/shard_map/ppermute | solution.py:443
  10.3 1.6 %collective-permute-start.2 = (f32[6,5,8,128]{3,2,1,0:T(8,128)}, f32[6,5,8,128]{3,2,1,0:T(8,128)S(1)}, u32[]{:S(2)}, u32[]{:S(2)}) collective-permute-start(f32[6,5,8,128]{3,2,1,0:T(8,128)} %get-tuple-element.18), channel_id=1, source_target_pairs={{0,1},{1,0},{2,3},{3,2},{4,5},{5,4},{6,7},{7,6},{8,9},{9,8},{10,11... | collective-permute-start | bytes 368648 | tf_op jit(solution)/shard_map/ppermute | solution.py:444
  11.9 4.9 %collective-permute-start.3 = (f32[6,5,8,128]{3,2,1,0:T(8,128)}, f32[6,5,8,128]{3,2,1,0:T(8,128)S(1)}, u32[]{:S(2)}, u32[]{:S(2)}) collective-permute-start(f32[6,5,8,128]{3,2,1,0:T(8,128)} %get-tuple-element.19), channel_id=1, source_target_pairs={{1,2},{2,1},{3,4},{4,3},{5,6},{6,5},{9,10},{10,9},{11,12},{12,11},... | collective-permute-start | bytes 368648 | tf_op jit(solution)/shard_map/ppermute | solution.py:445
  16.8 0.0 copy-done.9
  16.9 0.6 %copy.17.a_theta = f32[4,5,5]{2,1,0:T(8,128)} copy(f32[4,5,5]{2,0,1:T(4,128)S(1)} %copy-done.9) | data formatting | bytes 800 | tf_op args[4]
  17.5 2.6 %mode_tables.1 = (f32[3,16,128]{2,1,0:T(8,128)}, f32[3,16,128]{2,1,0:T(8,128)}, f32[8,128]{1,0:T(8,128)}, f32[3,8,128]{2,1,0:T(8,128)}, f32[5,6,5,8,128]{4,3,2,1,0:T(8,128)}) custom-call(s32[3,128]{1,0:T(4,128)} %order.1, s32[3,128]{1,0:T(4,128)} %radial.1, f32[6,5,64,128]{3,2,1,0:T(8,128)} %bitcast.5, f32[6,5,64,128]{3,2,1,0:T(8,128)} %bitcast.8), custom_call_target="tpu_custom_call" | custom-call | tf_op jit(solution)/shard_map/mode_tables/pallas_call | solution.py:403
  20.0 0.0 collective-permute-done.2.after2.xe
  20.0 0.0 copy-start.3
  20.0 0.9 %collective-permute-done.3.after3.xo = f32[6,5,8,128]{3,2,1,0:T(8,128)S(1)} collective-permute-done((f32[6,5,8,128]{3,2,1,0:T(8,128)}, f32[6,5,8,128]{3,2,1,0:T(8,128)S(1)}, u32[]{:S(2)}, u32[]{:S(2)}) %collective-permute-start.3) | collective-permute-done | bytes 122912 | tf_op jit(solution)/shard_map/ppermute | solution.py:445
  21.0 0.0 copy-start.4
  21.0 0.0 collective-permute-done.te
  21.0 0.0 copy-start.1
  21.0 0.0 collective-permute-done.1.to
  21.0 0.0 copy-start.2
  21.0 0.0 copy-done.3
  21.0 0.6 %copy-done.4 = f32[6,5,8,128]{3,2,1,0:T(8,128)} copy-done((f32[6,5,8,128]{3,2,1,0:T(8,128)}, f32[6,5,8,128]{3,2,1,0:T(8,128)S(1)}, u32[]{:S(2)}) %copy-start.4) | copy-done | bytes 122904
  21.6 0.1 copy-done.1
  21.7 0.1 copy-done.2
  21.7 1.9 %plane_part.1.after = f32[32,8,128]{2,1,0:T(8,128)} custom-call(s32[2]{0:T(128)} %stagger.7, f32[4,5,5]{2,1,0:T(8,128)} %copy.17.a_theta, f32[5,5]{1,0:T(8,128)} %a_axial.5, f32[5,5]{1,0:T(8,128)} %a_radial.5, f32[2,5]{1,0:T(2,128)} %l_rows.1, f32[5,6,5,8,128]{4,3,2,1,0:T(8,128)} %get-tuple-element.20.rows_ref, f32[64,128]{1,0:T(8,128)} %bitcast.13, ...), custom_call_target="tpu_custom_call" | custom-call | tf_op jit(solution)/shard_map/plane_part/pallas_call | solution.py:403
  23.7 4.1 %all-to-all-start = ((f32[32,8,128]{2,1,0:T(8,128)}), f32[32,8,128]{2,1,0:T(8,128)S(1)}, u32[]{:S(2)}, u32[]{:S(2)}) async-start(f32[32,8,128]{2,1,0:T(8,128)} %plane_part.1.after), calls=%async_computation | async-start | bytes 262144 | tf_op jit(solution)/shard_map/all_to_all | solution.py:479
  27.8 4.7 %first_step.1 = (f32[6,5,64,128]{3,2,1,0:T(8,128)}, f32[6,5,8,128]{3,2,1,0:T(8,128)}, f32[6,5,8,128]{3,2,1,0:T(8,128)}, f32[6,5,8,128]{3,2,1,0:T(8,128)}, f32[6,5,8,128]{3,2,1,0:T(8,128)}) custom-call(s32[2]{0:T(128)} %stagger.7, f32[4,5,5]{2,1,0:T(8,128)} %copy.17.a_theta, f32[5,5]{1,0:T(8,128)} %a_axial.5, f32[5,5]{1,0:T(8,128)} %a_radial.5, ...), custom_call_target="tpu_custom_call" | custom-call | tf_op jit(solution)/shard_map/first_step/pallas_call | solution.py:403
  32.5 0.3 collective-permute-start.4
  32.7 5.3 %collective-permute-start.5 = (f32[6,5,8,128]{3,2,1,0:T(8,128)}, f32[6,5,8,128]{3,2,1,0:T(8,128)S(1)}, u32[]{:S(2)}, u32[]{:S(2)}) collective-permute-start(f32[6,5,8,128]{3,2,1,0:T(8,128)} %get-tuple-element.27), channel_id=1, source_target_pairs={{0,248},{8,16},{16,8},{24,32},{32,24},{40,48},{48,40},{56,64},{64,... | collective-permute-start | bytes 368648 | tf_op jit(solution)/shard_map/ppermute | solution.py:443
  38.1 0.0 collective-permute-start.6
  38.1 4.9 %collective-permute-start.7 = (f32[6,5,8,128]{3,2,1,0:T(8,128)}, f32[6,5,8,128]{3,2,1,0:T(8,128)S(1)}, u32[]{:S(2)}, u32[]{:S(2)}) collective-permute-start(f32[6,5,8,128]{3,2,1,0:T(8,128)} %get-tuple-element.29), channel_id=1, source_target_pairs={{1,2},{2,1},{3,4},{4,3},{5,6},{6,5},{9,10},{10,9},{11,12},{12,11},... | collective-permute-start | bytes 368648 | tf_op jit(solution)/shard_map/ppermute | solution.py:445
  43.0 0.0 all-to-all-done.got_ref
  43.0 0.7 %share_amplitudes.1.got_ref = f32[8,8,128]{2,1,0:T(8,128)} custom-call(f32[32,8,128]{2,1,0:T(8,128)S(1)} %all-to-all-done.got_ref), custom_call_target="tpu_custom_call" | custom-call | tf_op jit(solution)/shard_map/share_amplitudes/pallas_call | solution.py:403
  43.7 3.8 %all-to-all-start.1 = ((f32[8,8,128]{2,1,0:T(8,128)}), f32[8,8,128]{2,1,0:T(8,128)S(1)}, u32[]{:S(2)}, u32[]{:S(2)}) async-start(f32[8,8,128]{2,1,0:T(8,128)} %share_amplitudes.1.got_ref), calls=%async_computation.1 | async-start | bytes 65536 | tf_op jit(solution)/shard_map/all_to_all | solution.py:483
  47.5 0.0 collective-permute-done.4.te
  47.5 0.0 copy-start.5
  47.5 0.0 collective-permute-done.5.to
  47.5 0.0 copy-start.6
  47.5 0.0 collective-permute-done.6.xe
  47.5 0.0 copy-start.7
  47.5 0.0 collective-permute-done.7.xo
  47.5 0.0 copy-start.8
  47.5 0.6 %copy-done.5 = f32[6,5,8,128]{3,2,1,0:T(8,128)} copy-done((f32[6,5,8,128]{3,2,1,0:T(8,128)}, f32[6,5,8,128]{3,2,1,0:T(8,128)S(1)}, u32[]{:S(2)}) %copy-start.5) | copy-done | bytes 122904
  48.1 0.1 copy-done.6
  48.2 0.0 copy-done.7
  48.2 0.0 copy-done.8
  48.3 0.0 copy-start
  48.3 4.8 %second_step.1 = f32[6,5,64,128]{3,2,1,0:T(8,128)} custom-call(s32[2]{0:T(128)} %stagger.7, f32[4,5,5]{2,1,0:T(8,128)} %copy.17.a_theta, f32[5,5]{1,0:T(8,128)} %a_axial.5, f32[5,5]{1,0:T(8,128)} %a_radial.5, f32[2,5]{1,0:T(2,128)} %r_cols.1, f32[6,5,64,128]{3,2,1,0:T(8,128)} %get-tuple-element.25.u_ref, f32[6,5,64,128]{3,2,1,0:T(8,128)} %bitcast.7, ...), custom_call_target="tpu_custom_call" | custom-call | tf_op jit(solution)/shard_map/second_step/pallas_call | solution.py:403
  53.1 0.0 all-to-all-done.1.got_ref
  53.1 0.0 copy-done
  53.1 0.6 %finish_amplitudes.1 = f32[3,2,2,128]{3,2,1,0:T(2,128)} custom-call(f32[8,8,128]{2,1,0:T(8,128)S(1)} %all-to-all-done.1.got_ref, s32[3,128]{1,0:T(4,128)S(1)} %copy-done), custom_call_target="tpu_custom_call" | custom-call | tf_op jit(solution)/shard_map/finish_amplitudes/pallas_call | solution.py:403
Async XLA Ops:
  0.6 16.2 %copy-start.9 = (f32[4,5,5]{2,0,1:T(4,128)S(1)}, f32[4,5,5]{2,0,1:T(4,128)}, u32[]{:S(2)}) copy-start(f32[4,5,5]{2,0,1:T(4,128)} %param.17) | copy-start | bytes 1204
  2.8 18.2 %collective-permute-start = (f32[7,5,8,128]{3,2,1,0:T(8,128)}, f32[7,5,8,128]{3,2,1,0:T(8,128)S(1)}, u32[]{:S(2)}, u32[]{:S(2)}) collective-permute-start(f32[7,5,8,128]{3,2,1,0:T(8,128)} %get-tuple-element.16), channel_id=1, source_target_pairs={{0,8},{8,0},{16,24},{24,16},{32,40},{40,32},{48,56},{56,48},{64,72... | collective-permute-start | bytes 430088 | tf_op jit(solution)/shard_map/ppermute | solution.py:442
  2.8 18.2 %collective-permute-start.1 = (f32[7,5,8,128]{3,2,1,0:T(8,128)}, f32[7,5,8,128]{3,2,1,0:T(8,128)S(1)}, u32[]{:S(2)}, u32[]{:S(2)}) collective-permute-start(f32[7,5,8,128]{3,2,1,0:T(8,128)} %get-tuple-element.17), channel_id=1, source_target_pairs={{0,248},{8,16},{16,8},{24,32},{32,24},{40,48},{48,40},{56,64},{64,... | collective-permute-start | bytes 430088 | tf_op jit(solution)/shard_map/ppermute | solution.py:443
  10.3 9.7 %collective-permute-start.2 = (f32[6,5,8,128]{3,2,1,0:T(8,128)}, f32[6,5,8,128]{3,2,1,0:T(8,128)S(1)}, u32[]{:S(2)}, u32[]{:S(2)}) collective-permute-start(f32[6,5,8,128]{3,2,1,0:T(8,128)} %get-tuple-element.18), channel_id=1, source_target_pairs={{0,1},{1,0},{2,3},{3,2},{4,5},{5,4},{6,7},{7,6},{8,9},{9,8},{10,11... | collective-permute-start | bytes 368648 | tf_op jit(solution)/shard_map/ppermute | solution.py:444
  11.9 9.1 %collective-permute-start.3 = (f32[6,5,8,128]{3,2,1,0:T(8,128)}, f32[6,5,8,128]{3,2,1,0:T(8,128)S(1)}, u32[]{:S(2)}, u32[]{:S(2)}) collective-permute-start(f32[6,5,8,128]{3,2,1,0:T(8,128)} %get-tuple-element.19), channel_id=1, source_target_pairs={{1,2},{2,1},{3,4},{4,3},{5,6},{6,5},{9,10},{10,9},{11,12},{12,11},... | collective-permute-start | bytes 368648 | tf_op jit(solution)/shard_map/ppermute | solution.py:445
  20.0 0.9 %copy-start.3 = (f32[6,5,8,128]{3,2,1,0:T(8,128)}, f32[6,5,8,128]{3,2,1,0:T(8,128)S(1)}, u32[]{:S(2)}) copy-start(f32[6,5,8,128]{3,2,1,0:T(8,128)S(1)} %collective-permute-done.2.after2.xe) | copy-start | bytes 368644
  21.0 0.6 %copy-start.4 = (f32[6,5,8,128]{3,2,1,0:T(8,128)}, f32[6,5,8,128]{3,2,1,0:T(8,128)S(1)}, u32[]{:S(2)}) copy-start(f32[6,5,8,128]{3,2,1,0:T(8,128)S(1)} %collective-permute-done.3.after3.xo) | copy-start | bytes 368644
  21.0 0.7 %copy-start.1 = (f32[7,5,8,128]{3,2,1,0:T(8,128)}, f32[7,5,8,128]{3,2,1,0:T(8,128)S(1)}, u32[]{:S(2)}) copy-start(f32[7,5,8,128]{3,2,1,0:T(8,128)S(1)} %collective-permute-done.te) | copy-start | bytes 430084
  21.0 0.7 %copy-start.2 = (f32[7,5,8,128]{3,2,1,0:T(8,128)}, f32[7,5,8,128]{3,2,1,0:T(8,128)S(1)}, u32[]{:S(2)}) copy-start(f32[7,5,8,128]{3,2,1,0:T(8,128)S(1)} %collective-permute-done.1.to) | copy-start | bytes 430084
  23.7 19.4 %all-to-all-start = ((f32[32,8,128]{2,1,0:T(8,128)}), f32[32,8,128]{2,1,0:T(8,128)S(1)}, u32[]{:S(2)}, u32[]{:S(2)}) async-start(f32[32,8,128]{2,1,0:T(8,128)} %plane_part.1.after), calls=%async_computation | async-start | bytes 262144 | tf_op jit(solution)/shard_map/all_to_all | solution.py:479
  32.5 15.0 %collective-permute-start.4 = (f32[6,5,8,128]{3,2,1,0:T(8,128)}, f32[6,5,8,128]{3,2,1,0:T(8,128)S(1)}, u32[]{:S(2)}, u32[]{:S(2)}) collective-permute-start(f32[6,5,8,128]{3,2,1,0:T(8,128)} %get-tuple-element.26), channel_id=1, source_target_pairs={{0,8},{8,0},{16,24},{24,16},{32,40},{40,32},{48,56},{56,48},{64,72... | collective-permute-start | bytes 368648 | tf_op jit(solution)/shard_map/ppermute | solution.py:442
  32.7 14.7 %collective-permute-start.5 = (f32[6,5,8,128]{3,2,1,0:T(8,128)}, f32[6,5,8,128]{3,2,1,0:T(8,128)S(1)}, u32[]{:S(2)}, u32[]{:S(2)}) collective-permute-start(f32[6,5,8,128]{3,2,1,0:T(8,128)} %get-tuple-element.27), channel_id=1, source_target_pairs={{0,248},{8,16},{16,8},{24,32},{32,24},{40,48},{48,40},{56,64},{64,... | collective-permute-start | bytes 368648 | tf_op jit(solution)/shard_map/ppermute | solution.py:443
  38.1 9.4 %collective-permute-start.6 = (f32[6,5,8,128]{3,2,1,0:T(8,128)}, f32[6,5,8,128]{3,2,1,0:T(8,128)S(1)}, u32[]{:S(2)}, u32[]{:S(2)}) collective-permute-start(f32[6,5,8,128]{3,2,1,0:T(8,128)} %get-tuple-element.28), channel_id=1, source_target_pairs={{0,1},{1,0},{2,3},{3,2},{4,5},{5,4},{6,7},{7,6},{8,9},{9,8},{10,11... | collective-permute-start | bytes 368648 | tf_op jit(solution)/shard_map/ppermute | solution.py:444
  38.1 9.4 %collective-permute-start.7 = (f32[6,5,8,128]{3,2,1,0:T(8,128)}, f32[6,5,8,128]{3,2,1,0:T(8,128)S(1)}, u32[]{:S(2)}, u32[]{:S(2)}) collective-permute-start(f32[6,5,8,128]{3,2,1,0:T(8,128)} %get-tuple-element.29), channel_id=1, source_target_pairs={{1,2},{2,1},{3,4},{4,3},{5,6},{6,5},{9,10},{10,9},{11,12},{12,11},... | collective-permute-start | bytes 368648 | tf_op jit(solution)/shard_map/ppermute | solution.py:445
  43.7 9.4 %all-to-all-start.1 = ((f32[8,8,128]{2,1,0:T(8,128)}), f32[8,8,128]{2,1,0:T(8,128)S(1)}, u32[]{:S(2)}, u32[]{:S(2)}) async-start(f32[8,8,128]{2,1,0:T(8,128)} %share_amplitudes.1.got_ref), calls=%async_computation.1 | async-start | bytes 65536 | tf_op jit(solution)/shard_map/all_to_all | solution.py:483
  47.5 0.7 %copy-start.5 = (f32[6,5,8,128]{3,2,1,0:T(8,128)}, f32[6,5,8,128]{3,2,1,0:T(8,128)S(1)}, u32[]{:S(2)}) copy-start(f32[6,5,8,128]{3,2,1,0:T(8,128)S(1)} %collective-permute-done.4.te) | copy-start | bytes 368644
  47.5 0.7 %copy-start.6 = (f32[6,5,8,128]{3,2,1,0:T(8,128)}, f32[6,5,8,128]{3,2,1,0:T(8,128)S(1)}, u32[]{:S(2)}) copy-start(f32[6,5,8,128]{3,2,1,0:T(8,128)S(1)} %collective-permute-done.5.to) | copy-start | bytes 368644
  47.5 0.7 %copy-start.7 = (f32[6,5,8,128]{3,2,1,0:T(8,128)}, f32[6,5,8,128]{3,2,1,0:T(8,128)S(1)}, u32[]{:S(2)}) copy-start(f32[6,5,8,128]{3,2,1,0:T(8,128)S(1)} %collective-permute-done.6.xe) | copy-start | bytes 368644
  47.5 0.7 %copy-start.8 = (f32[6,5,8,128]{3,2,1,0:T(8,128)}, f32[6,5,8,128]{3,2,1,0:T(8,128)S(1)}, u32[]{:S(2)}) copy-start(f32[6,5,8,128]{3,2,1,0:T(8,128)S(1)} %collective-permute-done.7.xo) | copy-start | bytes 368644
  48.3 4.9 %copy-start = (s32[3,128]{1,0:T(4,128)S(1)}, s32[3,128]{1,0:T(4,128)}, u32[]{:S(2)}) copy-start(s32[3,128]{1,0:T(4,128)} %plane.5) | copy-start | bytes 4612
